TPU v7x, 32 devices: a whole 2x2x4 slice. The times are simulated.
32 devices in a mesh: grp: 2 (over y), pts: 4 (over z), spec: 2 (over x), cpl: 2 (over core).
Axes of the slice: x: 2, y: 2, z: 4, core: 2. Of those that a mesh axis runs over, the one named last changes fastest.
Arguments:
- spec_deck: float32 [32, 36, 16384], P('spec', 'cpl', ('grp', 'pts')), parts along dimension 2, may hold values from 0 to 1, as said below
- wind_deck: float32 [2, 16384], P(None, ('grp', 'pts')), parts along dimension 1, may hold values from -24 to 24
- cell_sea: int32 [256, 128], P('grp'), parts along dimension 0, may hold values from -1 to 8191, as said below
- atm_order: int32 [16384], P(('grp', 'pts', 'spec')), parts along dimension 0, may hold values from 0 to 8191, as said below
- ocean_order: int32 [16384], P(('grp', 'pts', 'spec')), parts along dimension 0, may hold values from 0 to 8191, as said below
Outputs:
- spec_out: float32 [32, 36, 16384], P('spec', 'cpl', ('grp', 'pts')), parts along dimension 2
- stress_atm: float32 [2, 16384], P('cpl', ('grp', 'pts', 'spec')), parts along dimension 1
- stokes_ocn: float32 [2, 16384], P('cpl', ('grp', 'pts', 'spec')), parts along dimension 1
There are 2 independent parts, one for each index of `grp`. A program takes and returns all parts, laid end to end along the dimension named above; each array names one. Nothing has to cross between parts.
Inputs may be any that keep to these rules, and one draw needn't show every extreme that they name: `cell_sea`: -1 marks land. Sea cells carry the numbers 0 to 8191 in row-major order, each once. Every grid row holds 32 or more sea cells, and some row exactly 32. In every draw some block of 32 rows starting at a multiple of 32 is all sea. `spec_deck`: spectral densities. `atm_order`: each sea point once. In every aligned block of 1024 rows, exactly 256 rows name sea points s of each value of s mod 4. `ocean_order`: each sea point once. In every aligned block of 1024 rows, exactly 256 rows name sea points s of each value of s mod 4.
All inputs are finite; a program needn't handle non-finite values.
Results may differ from a plain program's by a relative error of at most 0.00002.
Values sent between devices are 32-bit elements; how exact they have to be, the bound alone decides.
No kernel may reach another device: no remote copies, remote signals or barrier semaphores. Data moves between devices by JAX's collectives and lax.ppermute only.
A program may use at most 192 MiB of HBM per device.

v0:
```python
import math

import jax
import jax.numpy as jnp
from jax import lax
from jax.sharding import PartitionSpec as P

COURANT_MAX = 0.68
BASE_FREQ = 0.035
GRAVITY = 9.81
GROWTH_RATE = 0.02
SLOPE_REF = 0.09
STRESS_GAIN = 64.0
STOKES_GAIN = 64.0


def passed_along(shard, axis, by):
    devices = lax.axis_size(axis)
    pairs = [(i, i + by) for i in range(devices) if 0 <= i + by < devices]
    return lax.ppermute(shard, axis, pairs)


def upwind(extended, mask_rows, courant_east, courant_north):
    middle = extended[:, :, 1:-1]
    prior_row = extended[:, :, :-2]
    next_row = extended[:, :, 2:]
    side_pad = jnp.pad(middle, ((0, 0), (0, 0), (0, 0), (1, 1)))
    prior_col = side_pad[..., :-2]
    next_col = side_pad[..., 2:]
    advanced = (
        middle
        - jnp.maximum(courant_east, 0.0) * (middle - prior_row)
        - jnp.maximum(-courant_east, 0.0) * (middle - next_row)
        - jnp.maximum(courant_north, 0.0) * (middle - prior_col)
        - jnp.maximum(-courant_north, 0.0) * (middle - next_col)
    )
    return advanced * mask_rows


def local(spec_deck, wind_deck, cell_sea, atm_order, ocean_order):
    owners = lax.axis_size("pts")
    spec_groups = lax.axis_size("spec")
    cpl_groups = lax.axis_size("cpl")
    my_pts = lax.axis_index("pts")
    my_spec = lax.axis_index("spec")
    my_cpl = lax.axis_index("cpl")
    freq_local, dirs_local, slots_local = spec_deck.shape
    grid_rows, grid_cols = cell_sea.shape
    freq_count = freq_local * spec_groups
    dir_count = dirs_local * cpl_groups
    sea_mask = cell_sea >= 0
    row_counts = jnp.sum(sea_mask.astype(jnp.int32), axis=1)
    before_row = jnp.concatenate([jnp.zeros((1,), jnp.int32), jnp.cumsum(row_counts)])
    tile_freq = my_spec * freq_local + jnp.arange(freq_local)
    height = 2 * (grid_rows // owners)
    capacity = (slots_local + grid_cols) // owners + 1
    targets = jnp.arange(owners + 1, dtype=jnp.int32) * slots_local
    row_starts = jnp.sum((before_row[None, :] < targets[:, None]).astype(jnp.int32), axis=1)
    width_cells = height * grid_cols
    bounds = jnp.take(before_row, row_starts)
    starts = bounds[:-1]
    my_row = jnp.take(row_starts, my_pts)
    my_height = jnp.take(row_starts, my_pts + 1) - my_row
    first_slot = -((jnp.arange(owners, dtype=jnp.int32)[None, :] - starts[:, None]) // owners)
    slot_range = jnp.arange(capacity, dtype=jnp.int32)
    own_first = jnp.take(first_slot, my_pts, axis=1)
    picked = jnp.clip(own_first[:, None] + slot_range[None, :], 0, slots_local - 1).reshape(-1)
    outgoing = jnp.take(spec_deck, picked, axis=2)
    arrived = lax.all_to_all(outgoing, "pts", split_axis=2, concat_axis=2, tiled=True)
    freq_here = arrived.shape[0]
    padded_map = jnp.concatenate([cell_sea, jnp.full((height, grid_cols), -1, jnp.int32)], axis=0)
    strip_map = lax.dynamic_slice_in_dim(padded_map, my_row, height, 0)
    row_valid = jnp.arange(height) < my_height
    strip_sea = ((strip_map >= 0) & row_valid[:, None]).reshape(-1)
    strip_map = strip_map.reshape(-1)
    safe_index = jnp.maximum(strip_map, 0)
    source = safe_index % owners
    strip_first = jnp.take(first_slot, my_pts, axis=0)
    where_from = jnp.where(
        strip_sea, source * capacity + safe_index // owners - jnp.take(strip_first, source), 0
    )
    wave_field = jnp.take(arrived, where_from, axis=2) * strip_sea.astype(jnp.float32)
    wave_field = wave_field.reshape(freq_here, dirs_local, height, grid_cols)
    freq_index = tile_freq.astype(jnp.float32)
    dir_index = (my_cpl * dirs_local + jnp.arange(dirs_local)).astype(jnp.float32)
    angles = 2.0 * math.pi * (dir_index + 0.5) / dir_count
    dir_cosine = jnp.cos(angles)
    dir_sine = jnp.sin(angles)
    speeds = COURANT_MAX * jnp.power(1.1, -freq_index)
    courant_east = (speeds[:, None] * dir_cosine[None, :])[:, :, None, None]
    courant_north = (speeds[:, None] * dir_sine[None, :])[:, :, None, None]
    strip_mask = strip_sea.astype(jnp.float32).reshape(height, grid_cols)
    last_row = lax.dynamic_slice_in_dim(wave_field, my_height - 1, 1, 2)
    from_above = passed_along(last_row, "pts", 1)
    from_below = passed_along(wave_field[:, :, :1], "pts", -1)
    extended = jnp.concatenate([from_above, wave_field, jnp.zeros_like(from_below)], axis=2)
    extended = lax.dynamic_update_slice_in_dim(extended, from_below, my_height + 1, 2)
    wave_field = upwind(extended, strip_mask, courant_east, courant_north)
    flat_field = wave_field.reshape(freq_here, dirs_local, width_cells)
    strip_start = jnp.take(starts, my_pts)
    inverse = (
        jnp.zeros((width_cells,), jnp.int32)
        .at[jnp.where(strip_sea, strip_map - strip_start, width_cells)]
        .set(jnp.arange(width_cells, dtype=jnp.int32), mode="drop")
    )
    wanted = (strip_first[:, None] + slot_range[None, :]) * owners + jnp.arange(
        owners, dtype=jnp.int32
    )[:, None]
    cells_out = jnp.take(inverse, jnp.clip(wanted - strip_start, 0, width_cells - 1).reshape(-1))
    leaving = jnp.take(flat_field, cells_out, axis=2)
    returned = lax.all_to_all(leaving, "pts", split_axis=2, concat_axis=2, tiled=True)
    slot_index = jnp.arange(slots_local, dtype=jnp.int32)
    points = slot_index * owners + my_pts
    strip_of = jnp.sum((starts[None, 1:] <= points[:, None]).astype(jnp.int32), axis=1)
    offset = slot_index - jnp.take(own_first, strip_of)
    position = strip_of * capacity + offset
    propagated = jnp.take(returned, position, axis=2)
    band_freq = (my_spec * freq_local + jnp.arange(freq_local)).astype(jnp.float32)
    sigma_freq = 2.0 * math.pi * BASE_FREQ * jnp.power(1.1, band_freq)
    phase_speed = GRAVITY / sigma_freq
    slope_weight = jnp.power(1.1, 0.4 * band_freq)
    slope_part = jnp.sum(propagated * slope_weight[:, None, None], axis=(0, 1))
    slope_total = lax.psum(slope_part, ("spec", "cpl")) / (SLOPE_REF * freq_count * dir_count)
    wind_along = (
        wind_deck[0][None, None, :] * dir_cosine[None, :, None]
        + wind_deck[1][None, None, :] * dir_sine[None, :, None]
    )
    growth = (
        GROWTH_RATE
        * sigma_freq[:, None, None]
        * jnp.maximum(wind_along / phase_speed[:, None, None] - 1.0, 0.0)
    )
    sigma_top = 2.0 * math.pi * BASE_FREQ * 1.1 ** (freq_count - 1)
    damping = (sigma_freq / sigma_top)[:, None, None] * (slope_total * slope_total)[None, None, :]
    updated = propagated * jnp.exp(growth - damping)
    lifted = growth * propagated
    drift_part = updated * jnp.power(1.1, 2.0 * (band_freq - (freq_count - 1)))[:, None, None]
    stress_scale = STRESS_GAIN / freq_count
    stokes_scale = STOKES_GAIN / math.sqrt(freq_count * dir_count)
    coupled_part = jnp.stack(
        [
            stress_scale * jnp.sum(lifted * dir_cosine[None, :, None], axis=(0, 1)),
            stress_scale * jnp.sum(lifted * dir_sine[None, :, None], axis=(0, 1)),
            stokes_scale * jnp.sum(drift_part * dir_cosine[None, :, None], axis=(0, 1)),
            stokes_scale * jnp.sum(drift_part * dir_sine[None, :, None], axis=(0, 1)),
        ]
    )
    coupled_total = lax.psum(coupled_part, ("spec", "cpl"))
    coupled_all = lax.all_gather(coupled_total, "pts", axis=1, tiled=True)
    atm_col = atm_order % owners * slots_local + atm_order // owners
    ocean_col = ocean_order % owners * slots_local + ocean_order // owners
    stress_atm = jnp.take(lax.dynamic_slice_in_dim(coupled_all, my_cpl, 1, 0), atm_col, axis=1)
    stokes_ocn = jnp.take(
        lax.dynamic_slice_in_dim(coupled_all, 2 + my_cpl, 1, 0), ocean_col, axis=1
    )
    return (updated, stress_atm, stokes_ocn)


def solution(mesh):
    return jax.shard_map(
        local,
        mesh=mesh,
        in_specs=(
            P("spec", "cpl", ("grp", "pts")),
            P(None, ("grp", "pts")),
            P("grp", None),
            P(("grp", "pts", "spec")),
            P(("grp", "pts", "spec")),
        ),
        out_specs=(
            P("spec", "cpl", ("grp", "pts")),
            P("cpl", ("grp", "pts", "spec")),
            P("cpl", ("grp", "pts", "spec")),
        ),
        check_vma=False,
    )
```

profile of v0, /device:TPU:0, one launch (start us, length us, event | category | flops | bytes accessed | tf_op | source)
XLA Modules:
  0.0 731.9 jit_solution(6396375507489536334)
XLA Ops:
  0.6 0.9 convert_reduce_fusion
  2.3 0.6 gather_fusion
  3.3 12.4 %copy.23 = f32[16,18,2048]{1,0,2:T(8,128)} copy(f32[16,18,2048]{2,0,1:T(8,128)} %param.7) | data formatting | bytes 4718592 | tf_op args[0]
  15.7 16.0 %gather_fusion.2 = f32[2180,16,18]{2,1,0:T(8,128)} fusion(f32[16,18,2048]{1,0,2:T(8,128)} %copy.23, s32[3072]{0:T(1024)S(1)} %pad_clamp_fusion.1), kind=kCustom, calls=%fused_computation.4 | custom fusion | bytes 5031440 | tf_op jit(solution)/shard_map/jit(_take)/gather | solution.py:68
  31.7 13.9 %fusion.52 = f32[2180,16,18]{2,1,0:T(8,128)} fusion(f32[2180,16,18]{2,1,0:T(8,128)} %gather_fusion.2, pred[2180]{0:T(1024)(128)(4,1)S(1)} %compare_and_fusion.2), kind=kLoop, calls=%fused_computation.187 | loop fusion | flops 627840 | bytes 5024900
  45.6 30.2 %reshape.1116 = f32[4,1,156960]{2,1,0:T(1,128)} reshape(f32[2180,16,18]{2,1,0:T(8,128)} %fusion.52) | data formatting | bytes 5022720
  75.8 6.3 all-to-all-start
  82.9 0.6 fusion.51
  84.0 0.6 fusion.49
  85.3 2.6 compare_select_fusion.3
  89.0 2.8 compare_select_fusion.2
  91.8 30.7 %scatter_custom_fusion = s32[8192]{0:T(1024)S(1)} fusion(s32[8192]{0:T(1024)S(1)} %bitcast.102, s32[8192]{0:T(1024)S(1)} %iota.63, s32[]{:T(128)} %constant.297.clone.1), kind=kCustom, calls=%fused_computation.91 | custom fusion | bytes 32772 | tf_op jit(solution)/shard_map/scatter | solution.py:104
  122.6 12.0 %gather_fusion.1 = s32[2180]{0:T(1024)S(1)} fusion(s32[8192]{0:T(1024)S(1)} %scatter_custom_fusion, s32[3072]{0:T(1024)S(1)} %pad_clamp_fusion.2), kind=kCustom, calls=%fused_computation.3 | custom fusion | bytes 26160 | tf_op jit(solution)/shard_map/jit(_take)/gather | solution.py:109
  134.8 4.4 all-to-all-done
  139.2 1.5 copy-done.1
  141.2 20.7 %reduce.9 = f32[4,156960]{1,0:T(4,128)S(1)} reduce(f32[4,1,156960]{2,1,0:T(1,128)} %copy-done.1, f32[]{:T(128)} %broadcast.1460), dimensions={1}, to_apply=%all_to_all.6.reduce_sub_computation | reduce | bytes 5022724 | tf_op jit(solution)/shard_map/all_to_all | solution.py:69
  161.8 17.9 %reshape.1117 = f32[2180,16,18]{2,1,0:T(8,128)} reshape(f32[4,156960]{1,0:T(4,128)S(1)} %reduce.9) | data formatting | bytes 5022720
  179.7 79.6 %gather_fusion.3 = f32[8192,16,18]{2,1,0:T(8,128)} fusion(f32[16,18,2180]{1,0,2:T(8,128)} %bitcast.89, s32[8192]{0:T(1024)S(1)} %broadcast_clamp_fusion), kind=kCustom, calls=%fused_computation.5 | custom fusion | bytes 18907136 | tf_op jit(solution)/shard_map/jit(_take)/gather | solution.py:82
  259.4 37.8 %copy.24 = f32[16,18,64,128]{3,0,2,1:T(8,128)} copy(f32[16,18,64,128]{1,0,3,2:T(8,128)} %bitcast.27) | data formatting | bytes 18874368 | tf_op jit(solution)/shard_map/jit(_take)/gather | solution.py:82
  297.2 4.7 select_multiply_fusion
  302.0 3.6 copy-done
  305.6 1.3 collective-permute-start
  307.1 12.0 %collective-permute-start.1 = (f32[16,18,1,128]{3,0,2,1:T(8,128)S(1)}, f32[16,18,1,128]{3,0,2,1:T(8,128)S(1)}, u32[]{:S(2)}, u32[]{:S(2)}) collective-permute-start(f32[16,18,1,128]{3,0,2,1:T(8,128)S(1)} %get-tuple-element.88), channel_id=1, source_target_pairs={{4,0},{8,4},{12,8},{5,1},{9,5},{13,9},{6,2},{10,6},{14,10},{7,3},{... | collective-permute-start | bytes 442376 | tf_op jit(solution)/shard_map/ppermute | solution.py:20
  319.1 4.8 maximum_maximum_fusion
  323.9 4.2 slice.113
  328.2 18.6 %fusion.7 = f32[16,18,64,128]{3,0,2,1:T(8,128)} fusion(f32[16,18,64,128]{3,0,2,1:T(8,128)} %slice.113, f32[16,18,66,128]{3,0,2,1:T(8,128)S(1)} %constant_dynamic-update-slice_fusion, f32[16,18]{0,1:T(8,128)S(1)} %get-tuple-element.110, f32[16,18]{0,1:T(8,128)S(1)} %get-tuple-element.111, f32[16,18]{0,1:T(8,128)S(1)} %get-tuple-element.103, ...), kind=kLoop, calls=%fused_computation.29 | loop fusion | flops 30670848 | bytes 37786112 | tf_op jit(solution)/shard_map/mul | solution.py:37
  346.8 33.1 %copy.25 = f32[16,18,64,128]{1,0,3,2:T(8,128)} copy(f32[16,18,64,128]{3,0,2,1:T(8,128)} %fusion.7) | data formatting | bytes 18874368 | tf_op jit(solution)/shard_map/mul | solution.py:37
  379.9 22.1 %gather_fusion.4 = f32[2180,16,18]{2,1,0:T(8,128)} fusion(f32[16,18,8192]{1,0,2:T(8,128)} %bitcast.28, s32[3072]{0:T(1024)S(1)} %pad_clamp_fusion), kind=kCustom, calls=%fused_computation.6 | custom fusion | bytes 5031440 | tf_op jit(solution)/shard_map/jit(_take)/gather | solution.py:110
  402.0 13.8 %fusion.53 = f32[2180,16,18]{2,1,0:T(8,128)} fusion(f32[2180,16,18]{2,1,0:T(8,128)} %gather_fusion.4, pred[2180]{0:T(1024)(128)(4,1)S(1)} %compare_and_fusion.3), kind=kLoop, calls=%fused_computation.188 | loop fusion | flops 627840 | bytes 5024900
  415.8 30.2 %reshape.1118 = f32[4,1,156960]{2,1,0:T(1,128)} reshape(f32[2180,16,18]{2,1,0:T(8,128)} %fusion.53) | data formatting | bytes 5022720
  446.0 6.0 all-to-all-start.1
  452.2 1.3 copy.26
  453.6 0.6 fusion.50
  454.4 2.6 compare_select_fusion.11
  457.0 50.5 %all-to-all-done.1 = f32[4,1,156960]{2,1,0:T(1,128)} async-done(((f32[4,1,156960]{2,1,0:T(1,128)}), f32[4,1,156960]{2,1,0:T(1,128)}, u32[]{:S(2)}, u32[]{:S(2)}) %all-to-all-start.1) | async-done | bytes 2511392 | tf_op jit(solution)/shard_map/all_to_all | solution.py:111
  507.5 20.9 %reduce.10 = f32[4,156960]{1,0:T(4,128)S(1)} reduce(f32[4,1,156960]{2,1,0:T(1,128)} %all-to-all-done.1, f32[]{:T(128)} %broadcast.1460), dimensions={1}, to_apply=%all_to_all.7.reduce_sub_computation | reduce | bytes 5022724 | tf_op jit(solution)/shard_map/all_to_all | solution.py:111
  528.4 17.8 %reshape.1119 = f32[2180,16,18]{2,1,0:T(8,128)} reshape(f32[4,156960]{1,0:T(4,128)S(1)} %reduce.10) | data formatting | bytes 5022720
  546.2 24.9 %gather_fusion.5 = f32[2048,16,18]{2,1,0:T(8,128)} fusion(f32[16,18,2180]{1,0,2:T(8,128)} %bitcast.90, s32[2048]{0:T(1024)S(1)} %broadcast_clamp_fusion.1), kind=kCustom, calls=%fused_computation.7 | custom fusion | bytes 4726784 | tf_op jit(solution)/shard_map/jit(_take)/gather | solution.py:117
  571.0 44.5 %fusion.2 = (f32[2048]{0:T(1024)S(1)}, f32[16,18,2048]{1,0,2:T(8,128)}) fusion(f32[2048,16,18]{2,1,0:T(8,128)} %gather_fusion.5, f32[16]{0:T(128)S(1)} %get-tuple-element.116, pred[2048]{0:T(1024)(128)(4,1)S(1)} %compare_and_fusion.4, f32[16]{0:T(128)S(1)} %get-tuple-element.117, f32[18,2048]{0,1:T(8,128)} %copy.26, f32[16]{0:T(128)S(1)} %get-tuple-element.119), kind=kLoop, calls=%fused_computation.19 | loop fusion | flops 4716544 | bytes 4876480 | tf_op jit(solution)/shard_map/reduce_sum | solution.py:122
  615.5 6.1 psum.14
  622.1 59.8 %multiply_reduce_fusion.3 = (f32[2048]{0:T(1024)S(1)}, f32[2048]{0:T(1024)S(1)}, f32[2048]{0:T(1024)S(1)}, f32[2048]{0:T(1024)S(1)}, f32[16,18,2048]{1,0,2:T(8,128)}) fusion(f32[16,18,2048]{1,0,2:T(8,128)} %get-tuple-element.87, f32[18]{0:T(128)S(1)} %get-tuple-element.115, f32[18]{0:T(128)S(1)} %get-tuple-element.114, f32[16]{0:T(128)S(1)} %multiply_power_fusion, ...), kind=kLoop, calls=%fused_computation.23 | loop fusion | flops 9428992 | bytes 7391568 | tf_op jit(solution)/shard_map/reduce_sum | solution.py:142
  681.9 10.9 %psum.15 = f32[4,2048]{1,0:T(4,128)S(1)} all-reduce(f32[4,2048]{1,0:T(4,128)S(1)} %pad_maximum_fusion), channel_id=1, replica_groups=mesh['grp'=2,'pts'=4,'spec'=2,'cpl'=2] {'spec','cpl'}, use_global_device_ids=true, to_apply=%region_11.12 | all-reduce | flops 8192 | bytes 65536 | tf_op jit(solution)/shard_map/psum | solution.py:148
  692.9 13.6 %all_gather.3 = f32[4,8192]{1,0:T(4,128)S(1)} all-gather(f32[4,2048]{1,0:T(4,128)S(1)} %psum.15), channel_id=1, replica_groups=mesh['grp'=2,'pts'=4,'spec'=2,'cpl'=2] {'pts'}, dimensions={1}, use_global_device_ids=true | all-gather | bytes 163840 | tf_op jit(solution)/shard_map/all_gather | solution.py:149
  706.5 6.2 gather_fusion.6
  712.7 0.6 and_select_fusion.5
  713.3 6.1 gather_fusion.7
  719.4 0.6 and_select_fusion.4
  720.0 11.4 %copy.27 = f32[16,18,2048]{2,0,1:T(8,128)} copy(f32[16,18,2048]{1,0,2:T(8,128)} %get-tuple-element.77) | data formatting | bytes 4718592
  (75 shorter events, 3.9 us)
Async XLA Ops:
  45.6 39.6 %copy-start.3 = (s32[128,128]{1,0:T(8,128)S(1)}, s32[128,128]{1,0:T(8,128)}, u32[]{:S(2)}) copy-start(s32[128,128]{1,0:T(8,128)} %param.9) | copy-start | bytes 196612
  75.8 63.4 %all-to-all-start = ((f32[4,1,156960]{2,1,0:T(1,128)}), f32[4,1,156960]{2,1,0:T(1,128)S(1)}, u32[]{:S(2)}, u32[]{:S(2)}) async-start(f32[4,1,156960]{2,1,0:T(1,128)} %reshape.1116), calls=%async_computation | async-start | bytes 5025792 | tf_op jit(solution)/shard_map/all_to_all | solution.py:69
  139.2 1.5 copy-start.1
  301.9 3.6 copy-start
  305.6 13.5 %collective-permute-start = (f32[16,18,1,128]{3,0,2,1:T(8,128)S(1)}, f32[16,18,1,128]{3,0,2,1:T(8,128)S(1)}, u32[]{:S(2)}, u32[]{:S(2)}) collective-permute-start(f32[16,18,1,128]{3,0,2,1:T(8,128)S(1)} %get-tuple-element.89), channel_id=1, source_target_pairs={{0,4},{4,8},{8,12},{1,5},{5,9},{9,13},{2,6},{6,10},{10,14},{3,7},{... | collective-permute-start | bytes 442376 | tf_op jit(solution)/shard_map/ppermute | solution.py:20
  307.1 16.9 %collective-permute-start.1 = (f32[16,18,1,128]{3,0,2,1:T(8,128)S(1)}, f32[16,18,1,128]{3,0,2,1:T(8,128)S(1)}, u32[]{:S(2)}, u32[]{:S(2)}) collective-permute-start(f32[16,18,1,128]{3,0,2,1:T(8,128)S(1)} %get-tuple-element.88), channel_id=1, source_target_pairs={{4,0},{8,4},{12,8},{5,1},{9,5},{13,9},{6,2},{10,6},{14,10},{7,3},{... | collective-permute-start | bytes 442376 | tf_op jit(solution)/shard_map/ppermute | solution.py:20
  415.8 36.3 %copy-start.6 = (f32[2,2048]{1,0:T(2,128)S(1)}, f32[2,2048]{1,0:T(2,128)}, u32[]{:S(2)}) copy-start(f32[2,2048]{1,0:T(2,128)} %param.8) | copy-start | bytes 49156
  415.8 38.5 %copy-start.4 = (s32[1024]{0:T(1024)S(1)}, s32[1024]{0:T(1024)}, u32[]{:S(2)}) copy-start(s32[1024]{0:T(1024)} %param.10) | copy-start | bytes 12292
  415.8 38.6 %copy-start.5 = (s32[1024]{0:T(1024)S(1)}, s32[1024]{0:T(1024)}, u32[]{:S(2)}) copy-start(s32[1024]{0:T(1024)} %param.11) | copy-start | bytes 12292
  446.0 61.5 %all-to-all-start.1 = ((f32[4,1,156960]{2,1,0:T(1,128)}), f32[4,1,156960]{2,1,0:T(1,128)}, u32[]{:S(2)}, u32[]{:S(2)}) async-start(f32[4,1,156960]{2,1,0:T(1,128)} %reshape.1118), calls=%async_computation.1 | async-start | bytes 5025792 | tf_op jit(solution)/shard_map/all_to_all | solution.py:111
  571.0 51.0 %copy-start.2 = (f32[18,2048]{0,1:T(8,128)S(1)}, f32[18,2048]{0,1:T(8,128)}, u32[]{:S(2)}) copy-start(f32[18,2048]{0,1:T(8,128)} %copy.26) | copy-start | bytes 442372
where the time goes:
time: 743 us; the launch traced here: 732 us
  local copies, waits for them, and re-layouts  403 us (54%)
  other arithmetic  214 us (29%)
  waiting for transfers between devices  54.9 us (7%)
  blocking collectives  30.7 us (4%)
  starting transfers between devices  25.7 us (3%)
    unnamed x20, local copies, waits for them, and re-layouts  125 us
    gather x2, local copies, waits for them, and re-layouts, local(): jnp.take(arrived, where_from, axis=2) * strip_sea.astype(jnp.float32)  117 us
    reduce_sum x1, other arithmetic, local(): jnp.sum(lifted * dir_cosine[None, :, None], axis=(0, 1))  59.8 us
    all_to_all x1, waiting for transfers between devices, local(): lax.all_to_all(leaving, 'pts', split_axis=2, concat_axis=2, tiled=True)  50.5 us
    reduce_sum x1, other arithmetic, local(): slope_part = jnp.sum(propagated * slope_weight[:, None, None], axis=(0, 1))  44.5 us
    mul x1, local copies, waits for them, and re-layouts, upwind(): return advanced * mask_rows  33.1 us
    scatter x1, local copies, waits for them, and re-layouts, local(): inverse = jnp.zeros((width_cells,), jnp.int32).at[jnp.where(strip_sea, st...  30.7 us
    unnamed x2, other arithmetic  27.7 us
  transfers between devices with their start and end apart: 4, of which 2 were waited for; matrix products, arithmetic and copies ran while one was open for 8% of the time, Pallas kernels for 0%

commit v1 on v0

--- a/solution.py
+++ b/solution.py
@@ -1,8 +1,11 @@
+import functools
 import math
 
 import jax
 import jax.numpy as jnp
 from jax import lax
+from jax.experimental import pallas as pl
+from jax.experimental.pallas import tpu as pltpu
 from jax.sharding import PartitionSpec as P
 
 COURANT_MAX = 0.68
@@ -12,6 +15,12 @@
 SLOPE_REF = 0.09
 STRESS_GAIN = 64.0
 STOKES_GAIN = 64.0
+LANES = 128
+F32 = jnp.float32
+BF16 = jnp.bfloat16
+I32 = jnp.int32
+WHOLE = pl.BlockSpec(memory_space=pltpu.VMEM)
+SCALARS = pl.BlockSpec(memory_space=pltpu.SMEM)
 
 
 def passed_along(shard, axis, by):
@@ -37,7 +46,7 @@
     return advanced * mask_rows
 
 
-def local(spec_deck, wind_deck, cell_sea, atm_order, ocean_order):
+def general(spec_deck, wind_deck, cell_sea, atm_order, ocean_order):
     owners = lax.axis_size("pts")
     spec_groups = lax.axis_size("spec")
     cpl_groups = lax.axis_size("cpl")
@@ -156,6 +165,413 @@
     return (updated, stress_atm, stokes_ocn)
 
 
+C_KEEP, C_ROW, C_COL, C_SLOPE, C_EAST, C_NORTH, C_ONE, C_DAMP = range(8)
+C_S_EAST, C_S_NORTH, C_T_EAST, C_T_NORTH = range(8, 12)
+
+
+def split3(value):
+    high = value.astype(BF16)
+    rest = value - high.astype(F32)
+    middle = rest.astype(BF16)
+    low = (rest - middle.astype(F32)).astype(BF16)
+    return high, middle, low
+
+
+def times_exact(value, one_hot, dims):
+    parts = [
+        lax.dot_general(part, one_hot, (dims, ((), ())), preferred_element_type=F32)
+        for part in split3(value)
+    ]
+    return parts[0] + parts[1] + parts[2]
+
+
+def index_kernel(owners, par_ref, cell_ref, g_ref, idx_ref, *list_refs):
+    slots = idx_ref.shape[1]
+    blocks = slots // LANES
+    half_rows = g_ref.shape[0] // 2
+    shift = owners.bit_length() - 1
+    pts = par_ref[0]
+    number = cell_ref[...].astype(F32)
+    sea = number >= 0.0
+    first = jnp.min(jnp.where(sea, number, 1e9), axis=1, keepdims=True)
+    last = jnp.max(jnp.where(sea, number, -1.0), axis=1, keepdims=True)
+    rank = jnp.where(sea, number - first + 1.0, 0.0)
+    edge = jnp.full((1, number.shape[1]), -1.0, F32)
+    above = jnp.concatenate([edge, number[:-1]], axis=0)
+    below = jnp.concatenate([number[1:], edge], axis=0)
+    to_above = jnp.where(sea & (above >= 0.0), number - above, 0.0)
+    to_below = jnp.where(sea & (below >= 0.0), below - number, 0.0)
+    cols = number.shape[1]
+    column = lax.broadcasted_iota(I32, number.shape, 1)
+    left = jnp.where(column == 0, -1.0, pltpu.roll(number, 1, 1))
+    right = jnp.where(column == cols - 1, -1.0, pltpu.roll(number, cols - 1, 1))
+    beside = jnp.where(par_ref[4] == 0, left, right)
+    beside = jnp.where(sea & (beside >= 0.0), 1.0, 0.0)
+
+    slot = lax.broadcasted_iota(I32, (1, slots), 1)
+    point = slot * owners + pts
+    pointf = point.astype(F32)
+    in_row = (first <= pointf) & (pointf <= last)
+    row_hot = jnp.where(in_row, 1.0, 0.0).astype(BF16)
+    row_first = jnp.sum(jnp.where(in_row, first, 0.0), axis=0, keepdims=True)
+
+    def of_row(values):
+        return jnp.dot(
+            jnp.transpose(values).astype(BF16), row_hot, preferred_element_type=F32
+        )
+
+    here = of_row(rank) == (pointf - row_first + 1.0)
+
+    def of_point(values):
+        return jnp.sum(jnp.where(here, of_row(values), 0.0), axis=0, keepdims=True)
+
+    step_above = of_point(to_above).astype(I32)
+    step_below = of_point(to_below).astype(I32)
+    has_beside = of_point(beside).astype(I32)
+
+    groups = max(8, owners)
+    group = lax.broadcasted_iota(I32, (groups, slots), 0)
+    codes, masks = [], []
+    for half in range(2):
+        up = par_ref[1 + half] < 0
+        for sends in range(2):
+            minus = up if sends == 0 else jnp.logical_not(up)
+            step = jnp.where(minus, step_above, step_below)
+            other = jnp.where(minus, point - step_above, point + step_below)
+            owner = other & (owners - 1)
+            away = (pts - owner) if sends == 0 else (owner - pts)
+            away = jnp.where(step > 0, away & (owners - 1), -1)
+            codes.append((away, other >> shift))
+            masks.append(jnp.where(group == away, 1.0, 0.0))
+    mask = jnp.concatenate(masks, axis=0)
+    before = jnp.where(
+        lax.broadcasted_iota(I32, (LANES, LANES), 0) < lax.broadcasted_iota(I32, (LANES, LANES), 1),
+        1.0,
+        0.0,
+    ).astype(BF16)
+    carry = jnp.zeros((mask.shape[0], 1), F32)
+    counts = []
+    for block in range(blocks):
+        part = mask[:, block * LANES : (block + 1) * LANES]
+        inside = jnp.dot(part.astype(BF16), before, preferred_element_type=F32)
+        counts.append((inside + carry) * part)
+        carry = carry + jnp.sum(part, axis=1, keepdims=True)
+    counts = jnp.concatenate(counts, axis=1)
+    excess = jnp.zeros((1, slots), I32)
+    entry = lax.broadcasted_iota(I32, ((owners - 1) * LANES, slots), 0)
+    for half in range(2):
+        places = [
+            jnp.sum(
+                counts[(2 * half + sends) * groups : (2 * half + sends + 1) * groups],
+                axis=0,
+                keepdims=True,
+            ).astype(I32)
+            for sends in range(2)
+        ]
+        away, other_slot = codes[2 * half]
+        place = places[0]
+        excess = jnp.maximum(excess, jnp.where((away > 0) & (place >= LANES), 1, 0))
+        same_block = (other_slot >> 7) == (slot >> 7)
+        code = jnp.where(away == 0, jnp.where(same_block, 1, 2), away + 2)
+        code = jnp.where(away < 0, 0, code)
+        lane = jnp.where(away == 0, other_slot & (LANES - 1), jnp.minimum(place, LANES - 1))
+        idx_ref[2 * half : 2 * half + 1, :] = jnp.where(away < 0, 0, lane)
+        idx_ref[2 * half + 1 : 2 * half + 2, :] = code
+        away, _ = codes[2 * half + 1]
+        place = places[1]
+        key = jnp.where((away > 0) & (place < LANES), (away - 1) * LANES + place, -1)
+        one_hot = jnp.where(entry == key, 1.0, 0.0).astype(BF16)
+        rows = slice(half * half_rows, (half + 1) * half_rows)
+        packed = times_exact(g_ref[rows, :], one_hot, ((1,), (1,)))
+        for at, list_ref in enumerate(list_refs):
+            list_ref[rows, :] = packed[:, at * LANES : (at + 1) * LANES]
+    idx_ref[4:5, :] = has_beside
+    idx_ref[5:6, :] = excess
+    idx_ref[6:8, :] = jnp.zeros((2, slots), I32)
+
+
+def lane_take(values, lanes):
+    return jnp.take_along_axis(values, lanes, axis=1)
+
+
+def advance_kernel(owners, par_ref, coef_ref, idx_ref, g_ref, beside_ref, *refs):
+    list_refs = refs[: owners - 1]
+    out_ref, slope_ref, total_ref = refs[owners - 1 :]
+    slots = idx_ref.shape[1]
+    blocks = slots // LANES
+    tiles = g_ref.shape[0] // 16
+    shape = (8, LANES)
+    total_ref[...] = jnp.zeros_like(total_ref)
+    turn = par_ref[3]
+    lane = lax.broadcasted_iota(I32, shape, 1)
+    beside_lane = (lane + turn) & (LANES - 1)
+    beyond = (lane + turn) != beside_lane
+
+    for half in range(2):
+        way = par_ref[1 + half]
+
+        @pl.loop(0, tiles)
+        def _(tile):
+            rows = pl.ds(pl.multiple_of((half * tiles + tile) * 8, 8), 8)
+            coef = coef_ref[rows, :]
+
+            def factor(at):
+                return jnp.broadcast_to(coef[:, at : at + 1], shape)
+
+            keep, by_row, by_col = factor(C_KEEP), factor(C_ROW), factor(C_COL)
+            by_slope = factor(C_SLOPE)
+            lists = [ref[rows, :] for ref in list_refs]
+            for block in range(blocks):
+                at = slice(block * LANES, (block + 1) * LANES)
+
+                def near(ref, step):
+                    which = jnp.clip(block + step, 0, blocks - 1)
+                    return ref[rows, pl.ds(pl.multiple_of(which * LANES, LANES), LANES)]
+
+                lanes = jnp.broadcast_to(idx_ref[2 * half : 2 * half + 1, at], shape)
+                code = jnp.broadcast_to(idx_ref[2 * half + 1 : 2 * half + 2, at], shape)
+                has_beside = jnp.broadcast_to(idx_ref[4:5, at], shape)
+                own = g_ref[rows, at]
+                row_value = jnp.where(code == 1, lane_take(own, lanes), 0.0)
+                row_value = jnp.where(code == 2, lane_take(near(g_ref, way), lanes), row_value)
+                for number, values in enumerate(lists):
+                    row_value = jnp.where(code == 3 + number, lane_take(values, lanes), row_value)
+                col_value = jnp.where(
+                    beyond,
+                    lane_take(near(beside_ref, turn), beside_lane),
+                    lane_take(beside_ref[rows, at], beside_lane),
+                )
+                col_value = jnp.where(has_beside > 0, col_value, 0.0)
+                moved = keep * own + by_row * row_value + by_col * col_value
+                out_ref[rows, at] = moved
+                total_ref[:, at] += by_slope * moved
+
+    slope_ref[...] = jnp.sum(total_ref[...], axis=0, keepdims=True)
+
+
+def source_kernel(coef_ref, wind_ref, slope_ref, prop_ref, out_ref, sums_ref, total_ref):
+    slots = prop_ref.shape[1]
+    blocks = slots // LANES
+    shape = (8, LANES)
+    total_ref[...] = jnp.zeros_like(total_ref)
+
+    @pl.loop(0, prop_ref.shape[0] // 8)
+    def _(tile):
+        rows = pl.ds(pl.multiple_of(tile * 8, 8), 8)
+        coef = coef_ref[rows, :]
+
+        def factor(at):
+            return jnp.broadcast_to(coef[:, at : at + 1], shape)
+
+        east, north, one, damp = factor(C_EAST), factor(C_NORTH), factor(C_ONE), factor(C_DAMP)
+        s_east, s_north = factor(C_S_EAST), factor(C_S_NORTH)
+        t_east, t_north = factor(C_T_EAST), factor(C_T_NORTH)
+        for block in range(blocks):
+            at = slice(block * LANES, (block + 1) * LANES)
+            wind_east = jnp.broadcast_to(wind_ref[0:1, at], shape)
+            wind_north = jnp.broadcast_to(wind_ref[1:2, at], shape)
+            slope = jnp.broadcast_to(slope_ref[0:1, at], shape)
+            value = prop_ref[rows, at]
+            growth = jnp.maximum(east * wind_east + north * wind_north - one, 0.0)
+            updated = value * jnp.exp(growth - damp * (slope * slope))
+            out_ref[rows, at] = updated
+            lifted = growth * value
+            total_ref[0, :, at] += s_east * lifted
+            total_ref[1, :, at] += s_north * lifted
+            total_ref[2, :, at] += t_east * updated
+            total_ref[3, :, at] += t_north * updated
+
+    for item in range(4):
+        for block in range(blocks):
+            at = slice(block * LANES, (block + 1) * LANES)
+            sums_ref[item, block : block + 1, :] = jnp.sum(
+                total_ref[item, :, at], axis=0, keepdims=True
+            )
+
+
+def pick_kernel(owners, table_ref, atm_ref, ocean_ref, stress_ref, stokes_ref):
+    shift = owners.bit_length() - 1
+    blocks = table_ref.shape[1] // owners
+    for item, (order_ref, out_ref) in enumerate(((atm_ref, stress_ref), (ocean_ref, stokes_ref))):
+        point = order_ref[...]
+        count = point.shape[1]
+        slot = point >> shift
+        row = (point & (owners - 1)) * blocks + (slot >> 7)
+        lane = slot & (LANES - 1)
+        rows = table_ref.shape[1]
+        hot = jnp.where(lax.broadcasted_iota(I32, (rows, count), 0) == row, 1.0, 0.0).astype(BF16)
+        table = jnp.transpose(table_ref[item])
+        found = times_exact(table, hot, ((1,), (0,)))
+        pick = lax.broadcasted_iota(I32, (LANES, count), 0) == lane
+        out_ref[...] = jnp.sum(jnp.where(pick, found, 0.0), axis=0, keepdims=True)
+
+
+def coefficients(freq_local, dirs_local, pad_half, my_spec, my_cpl, freq_count, dir_count):
+    freq = (my_spec * freq_local + jnp.arange(freq_local)).astype(F32)
+    direction = (my_cpl * dirs_local + jnp.arange(dirs_local)).astype(F32)
+    angles = 2.0 * math.pi * (direction + 0.5) / dir_count
+    cosine, sine = jnp.cos(angles)[:, None], jnp.sin(angles)[:, None]
+    speed = COURANT_MAX * jnp.power(1.1, -freq)[None, :]
+    by_row, by_col = jnp.abs(speed * cosine), jnp.abs(speed * sine)
+    sigma = (2.0 * math.pi * BASE_FREQ * jnp.power(1.1, freq))[None, :]
+    sigma_top = 2.0 * math.pi * BASE_FREQ * 1.1 ** (freq_count - 1)
+    inverse_speed = sigma / GRAVITY
+    rate = GROWTH_RATE * sigma
+    drift = jnp.power(1.1, 2.0 * (freq - (freq_count - 1)))[None, :]
+    stress_scale = STRESS_GAIN / freq_count
+    stokes_scale = STOKES_GAIN / math.sqrt(freq_count * dir_count)
+    shape = (dirs_local, freq_local)
+    columns = [
+        1.0 - by_row - by_col,
+        by_row,
+        by_col,
+        jnp.power(1.1, 0.4 * freq)[None, :] / (SLOPE_REF * freq_count * dir_count),
+        rate * inverse_speed * cosine,
+        rate * inverse_speed * sine,
+        rate,
+        sigma / sigma_top,
+        stress_scale * cosine,
+        stress_scale * sine,
+        stokes_scale * drift * cosine,
+        stokes_scale * drift * sine,
+    ]
+    table = jnp.stack([jnp.broadcast_to(column, shape) for column in columns], axis=-1)
+    table = table.reshape(2, -1, len(columns))
+    table = jnp.pad(table, ((0, 0), (0, pad_half), (0, 16 - len(columns))))
+    return table.reshape(-1, 16)
+
+
+def shape_of(*dims, kind=F32):
+    return jax.ShapeDtypeStruct(dims, kind)
+
+
+def call(kernel, inputs, outputs, scratch=(), flops=0, moved=0):
+    return pl.pallas_call(
+        kernel,
+        in_specs=inputs,
+        out_specs=[WHOLE] * len(outputs),
+        out_shape=outputs,
+        scratch_shapes=list(scratch),
+        compiler_params=pltpu.CompilerParams(vmem_limit_bytes=48 * 1024 * 1024),
+        cost_estimate=pl.CostEstimate(flops=flops, bytes_accessed=moved, transcendentals=0),
+    )
+
+
+def local(spec_deck, wind_deck, cell_sea, atm_order, ocean_order):
+    owners = lax.axis_size("pts")
+    spec_groups = lax.axis_size("spec")
+    cpl_groups = lax.axis_size("cpl")
+    my_pts = lax.axis_index("pts")
+    my_spec = lax.axis_index("spec")
+    my_cpl = lax.axis_index("cpl")
+    freq_local, dirs_local, slots = spec_deck.shape
+    freq_count = freq_local * spec_groups
+    dir_count = dirs_local * cpl_groups
+    blocks = slots // LANES
+    half_rows = freq_local * dirs_local // 2
+    pad_half = -half_rows % 8
+    rows = 2 * (half_rows + pad_half)
+
+    field = jnp.transpose(spec_deck, (1, 0, 2)).reshape(2, half_rows, slots)
+    if pad_half:
+        field = jnp.pad(field, ((0, 0), (0, pad_half), (0, 0)))
+    field = field.reshape(rows, slots)
+
+    flat = owners * cpl_groups
+    ring = []
+    for owner in range(owners):
+        ring.append((owner * 2, (owner + 1) % owners * 2))
+        ring.append((owner * 2 + 1, (owner - 1) % owners * 2 + 1))
+    assert flat == len(ring)
+    beside = lax.ppermute(field, ("pts", "cpl"), ring)
+
+    first_way = 2 * my_cpl - 1
+    turn = jnp.where(
+        (my_cpl == 0) & (my_pts == 0), -1, jnp.where((my_cpl == 1) & (my_pts == owners - 1), 1, 0)
+    )
+    par = jnp.stack([my_pts, first_way, -first_way, turn, my_cpl]).astype(I32)
+    coef = coefficients(
+        freq_local, dirs_local, pad_half, my_spec, my_cpl, freq_count, dir_count
+    )
+
+    found = call(
+        functools.partial(index_kernel, owners),
+        [SCALARS, WHOLE, WHOLE],
+        [shape_of(8, slots, kind=I32)] + [shape_of(rows, LANES)] * (owners - 1),
+        flops=6 * rows * slots * LANES * owners,
+        moved=rows * slots * 4,
+    )(par, cell_sea, field)
+    idx, lists = found[0], found[1:]
+    arrived = [
+        lax.ppermute(values, "pts", [(i, (i + 1 + away) % owners) for i in range(owners)])
+        for away, values in enumerate(lists)
+    ]
+    excess = lax.pmax(jnp.max(idx[5]), ("grp", "pts"))
+
+    propagated, slope_part = call(
+        functools.partial(advance_kernel, owners),
+        [SCALARS] + [WHOLE] * (owners + 3),
+        [shape_of(rows, slots), shape_of(1, slots)],
+        [pltpu.VMEM((8, slots), F32)],
+        flops=rows * slots * 20,
+        moved=rows * slots * 12,
+    )(par, coef, idx, field, beside, *arrived)
+
+    peers = spec_groups * cpl_groups
+    slope = slope_part
+    if spec_groups == 2:
+        for turned in range(1, peers):
+            slope = slope + lax.ppermute(
+                slope_part, ("spec", "cpl"), [(i, i ^ turned) for i in range(peers)]
+            )
+    else:
+        slope = lax.psum(slope_part, ("spec", "cpl"))
+
+    updated, sums = call(
+        source_kernel,
+        [WHOLE] * 4,
+        [shape_of(rows, slots), shape_of(4, blocks, LANES)],
+        [pltpu.VMEM((4, 8, slots), F32)],
+        flops=rows * slots * 40,
+        moved=rows * slots * 8,
+    )(coef, wind_deck, slope, propagated)
+
+    mine = jnp.take(sums.reshape(2, 2, blocks, LANES), my_cpl, axis=1)
+    others = jnp.take(sums.reshape(2, 2, blocks, LANES), 1 - my_cpl, axis=1)
+    mine = mine + lax.ppermute(others, "cpl", [(0, 1), (1, 0)])
+    if spec_groups == 2:
+        mine = mine + lax.ppermute(mine, "spec", [(0, 1), (1, 0)])
+    else:
+        mine = lax.psum(mine, "spec")
+    if owners == 4:
+        around = [mine] + [
+            lax.ppermute(mine, "pts", [(i, i ^ turned) for i in range(owners)])
+            for turned in range(1, owners)
+        ]
+        table = jnp.stack(around, axis=1)
+        looked = lambda order: order ^ my_pts
+    else:
+        table = lax.all_gather(mine, "pts", axis=1)
+        looked = lambda order: order
+    table = table.reshape(2, owners * blocks, LANES)
+    count = atm_order.shape[0]
+    stress_atm, stokes_ocn = call(
+        functools.partial(pick_kernel, owners),
+        [WHOLE] * 3,
+        [shape_of(1, count)] * 2,
+        flops=owners * blocks * LANES * count * 12,
+        moved=owners * blocks * LANES * 8,
+    )(table, looked(atm_order)[None, :], looked(ocean_order)[None, :])
+
+    updated = updated.reshape(2, half_rows + pad_half, slots)[:, :half_rows]
+    updated = jnp.transpose(updated.reshape(dirs_local, freq_local, slots), (1, 0, 2))
+    return lax.cond(
+        excess > 0,
+        lambda: general(spec_deck, wind_deck, cell_sea, atm_order, ocean_order),
+        lambda: (updated, stress_atm, stokes_ocn),
+    )
+
+
 def solution(mesh):
     return jax.shard_map(
         local,

time: 743 us -> 142 us (0.19); the launches traced: 732 us -> 141 us
  local copies, waits for them, and re-layouts: 403 us -> 29.1 us
  other arithmetic: 214 us -> 1.61 us
  Pallas kernels: 0 us -> 24.9 us
  blocking collectives: 30.7 us -> 12 us
    gather x11 -> x0, local copies, waits for them, and re-layouts: 207 us -> none  [the longest x2 117 us: local(): jnp.take(arrived, where_from, axis=2) * strip_sea.astype(jnp.float32)]
    unnamed x20 -> x18, local copies, waits for them, and re-layouts: 125 us -> 3.91 us
    reduce_sum x5 -> x0, other arithmetic: 106 us -> none  [the longest x1 59.8 us: local(): jnp.sum(lifted * dir_cosine[None, :, None], axis=(0, 1))]
    all_to_all x2 -> x0, waiting for transfers between devices: 54.9 us -> none  [the longest x1 50.5 us: local(): lax.all_to_all(leaving, 'pts', split_axis=2, concat_axis=2, tiled=True)]
    ppermute x2 -> x12, waiting for transfers between devices: 0.01 us -> 52.4 us  [the longest x3 45.7 us: local(): lax.ppermute(values, 'pts', [(i, (i + 1 + away) % owners) for i in range(...]
    all_to_all x2 -> x0, other arithmetic: 41.5 us -> none  [the longest x1 20.9 us: local(): lax.all_to_all(leaving, 'pts', split_axis=2, concat_axis=2, tiled=True)]
    mul x1 -> x10, local copies, waits for them, and re-layouts: 33.1 us -> 0.57 us  [the longest x6 0.4 us: coefficients(): by_row, by_col = (jnp.abs(speed * cosine), jnp.abs(speed * sine))]
    scatter x1 -> x0, local copies, waits for them, and re-layouts: 30.7 us -> none  [local(): inverse = jnp.zeros((width_cells,), jnp.int32).at[jnp.where(strip_sea, st...]
  transfers between devices with their start and end apart: 4 -> 12, of which waited for: 2 -> 6; matrix products, arithmetic and copies ran while one was open for 8% -> 11% of each run, Pallas kernels for 0% -> 4%
where the time goes in v1:
time: 142 us; the launch traced here: 141 us
  waiting for transfers between devices  52.4 us (37%)
  local copies, waits for them, and re-layouts  29.1 us (20%)
  Pallas kernels  24.9 us (18%)
  starting transfers between devices  19.8 us (14%)
  blocking collectives  12 us (8%)
  other arithmetic  1.61 us (1%)
  between operations  1.47 us (1%)
    ppermute x3, waiting for transfers between devices, local(): lax.ppermute(values, 'pts', [(i, (i + 1 + away) % owners) for i in range(...  45.7 us
    pallas_call x1, Pallas kernels, local(): call(functools.partial(advance_kernel, owners), [SCALARS] + [WHOLE] * (ow...  12.8 us
    pmax x1, blocking collectives, local(): excess = lax.pmax(jnp.max(idx[5]), ('grp', 'pts'))  12 us
    another operation x1, local copies, waits for them, and re-layouts, local(): updated.reshape(dirs_local, freq_local, slots)  11.6 us
    cond x1, local copies, waits for them, and re-layouts, local(): lax.cond(excess > 0, lambda: general(spec_deck, wind_deck, cell_sea, atm_...  11.4 us
    pallas_call x1, Pallas kernels, local(): call(functools.partial(index_kernel, owners), [SCALARS, WHOLE, WHOLE], [s...  5.99 us
    ppermute x3, starting transfers between devices, local(): lax.ppermute(mine, 'pts', [(i, i ^ turned) for i in range(owners)])  5.95 us
    ppermute x3, starting transfers between devices, local(): lax.ppermute(values, 'pts', [(i, (i + 1 + away) % owners) for i in range(...  5.57 us
  transfers between devices with their start and end apart: 12, of which 6 were waited for; matrix products, arithmetic and copies ran while one was open for 11% of the time, Pallas kernels for 4%

profile of v1, /device:TPU:0, one launch (start us, length us, event | category | flops | bytes accessed | tf_op | source)
XLA Modules:
  0.0 141.3 jit_solution(3651448126641463586)
XLA Ops:
  0.6 3.1 %collective-permute-start.2 = (f32[288,2048]{1,0:T(8,128)}, f32[288,2048]{1,0:T(8,128)S(1)}, u32[]{:S(2)}, u32[]{:S(2)}) collective-permute-start(f32[288,2048]{1,0:T(8,128)} %bitcast.147), channel_id=1, source_target_pairs={{0,4},{1,13},{4,8},{5,1},{8,12},{9,5},{12,0},{13,9},{2,6},{3,15},{... | collective-permute-start | bytes 7077896 | tf_op jit(solution)/shard_map/ppermute | solution.py:486
  3.7 0.1 stack.55.par_ref
  3.8 6.0 %shard_map.82 = (s32[8,2048]{1,0:T(8,128)S(1)}, f32[288,128]{1,0:T(8,128)S(1)}, f32[288,128]{1,0:T(8,128)S(1)}, f32[288,128]{1,0:T(8,128)S(1)}) custom-call(s32[5]{0:T(128)S(1)} %stack.55.par_ref, s32[128,128]{1,0:T(8,128)} %cell_ref.1, f32[288,2048]{1,0:T(8,128)} %bitcast.148), custom_call_target="tpu_custom_call" | custom-call | flops 1811939328 | bytes 2359296 | tf_op jit(solution)/shard_map/pallas_call | solution.py:497
  9.8 1.6 %collective-permute-start.3 = (f32[288,128]{1,0:T(8,128)S(1)}, f32[288,128]{1,0:T(8,128)S(1)}, u32[]{:S(2)}, u32[]{:S(2)}) collective-permute-start(f32[288,128]{1,0:T(8,128)S(1)} %get-tuple-element.37), channel_id=1, source_target_pairs={{0,4},{4,8},{8,12},{12,0},{1,5},{5,9},{9,13},{13,1},{2,6},{6,10},{... | collective-permute-start | bytes 442376 | tf_op jit(solution)/shard_map/ppermute | solution.py:506
  11.4 1.1 collective-permute-start.4
  12.5 2.8 %collective-permute-start.5 = (f32[288,128]{1,0:T(8,128)S(1)}, f32[288,128]{1,0:T(8,128)S(1)}, u32[]{:S(2)}, u32[]{:S(2)}) collective-permute-start(f32[288,128]{1,0:T(8,128)S(1)} %get-tuple-element.39), channel_id=1, source_target_pairs={{0,12},{4,0},{8,4},{12,8},{1,13},{5,1},{9,5},{13,9},{2,14},{6,2},{... | collective-permute-start | bytes 442376 | tf_op jit(solution)/shard_map/ppermute | solution.py:506
  15.5 0.1 broadcast_multiply_fusion.7
  15.5 0.1 mul.596
  15.6 0.1 mul.597
  15.7 0.1 mul.599
  15.7 0.1 mul.600
  15.8 0.1 mul.594
  15.9 0.1 stack_broadcast_in_dim.42
  16.0 0.1 mul.607
  16.1 0.1 stack_broadcast_in_dim.45
  16.2 0.1 stack_broadcast_in_dim.48
  16.3 0.1 stack_broadcast_in_dim.50
  16.3 0.1 stack_broadcast_in_dim.51
  16.4 0.1 stack_broadcast_in_dim.52
  16.5 0.1 stack_broadcast_in_dim.53
  16.6 0.1 mul.615
  16.8 0.8 copy.66
  17.6 0.9 pad.9.clone
  18.5 42.7 %collective-permute-done.3.refs_0_ = f32[288,128]{1,0:T(8,128)S(1)} collective-permute-done((f32[288,128]{1,0:T(8,128)S(1)}, f32[288,128]{1,0:T(8,128)S(1)}, u32[]{:S(2)}, u32[]{:S(2)}) %collective-permute-start.3) | collective-permute-done | bytes 147488 | tf_op jit(solution)/shard_map/ppermute | solution.py:506
  61.2 3.0 %collective-permute-done.5.refs_2_ = f32[288,128]{1,0:T(8,128)S(1)} collective-permute-done((f32[288,128]{1,0:T(8,128)S(1)}, f32[288,128]{1,0:T(8,128)S(1)}, u32[]{:S(2)}, u32[]{:S(2)}) %collective-permute-start.5) | collective-permute-done | bytes 147488 | tf_op jit(solution)/shard_map/ppermute | solution.py:506
  64.2 12.8 %shard_map.83 = (f32[288,2048]{1,0:T(8,128)S(1)}, f32[1,2048]{1,0:T(1,128)S(1)}) custom-call(s32[5]{0:T(128)S(1)} %stack.55.par_ref, f32[288,16]{1,0:T(8,128)S(1)} %bitcast.135, s32[8,2048]{1,0:T(8,128)S(1)} %get-tuple-element.36.idx_ref, f32[288,2048]{1,0:T(8,128)} %bitcast.149, f32[288,2048]{1,0:T(8,128)S(1)} %collective-permute-done.2.beside_ref, ...), custom_call_target="tpu_custom_call" | custom-call | flops 11796480 | bytes 7077888 | tf_op jit(solution)/shard_map/pallas_call | solution.py:511
  77.0 0.0 copy-start
  77.0 1.4 copy-done
  78.4 3.0 %collective-permute-start.6 = (f32[1,2048]{1,0:T(1,128)S(1)}, f32[1,2048]{1,0:T(1,128)S(1)}, u32[]{:S(2)}, u32[]{:S(2)}) collective-permute-start(f32[1,2048]{1,0:T(1,128)S(1)} %get-tuple-element.40), channel_id=1, source_target_pairs={{0,1},{1,0},{2,3},{3,2},{4,5},{5,4},{6,7},{7,6},{8,9},{9,8},{10,11... | collective-permute-start | bytes 24584 | tf_op jit(solution)/shard_map/ppermute | solution.py:524
  81.4 1.5 %collective-permute-start.7 = (f32[1,2048]{1,0:T(1,128)S(1)}, f32[1,2048]{1,0:T(1,128)S(1)}, u32[]{:S(2)}, u32[]{:S(2)}) collective-permute-start(f32[1,2048]{1,0:T(1,128)S(1)} %get-tuple-element.40), channel_id=1, source_target_pairs={{0,2},{1,3},{2,0},{3,1},{4,6},{5,7},{6,4},{7,5},{8,10},{9,11},{10,... | collective-permute-start | bytes 24584 | tf_op jit(solution)/shard_map/ppermute | solution.py:524
  82.9 2.2 %collective-permute-done.7 = f32[1,2048]{1,0:T(1,128)S(1)} collective-permute-done((f32[1,2048]{1,0:T(1,128)S(1)}, f32[1,2048]{1,0:T(1,128)S(1)}, u32[]{:S(2)}, u32[]{:S(2)}) %collective-permute-start.7) | collective-permute-done | bytes 8224 | tf_op jit(solution)/shard_map/ppermute | solution.py:524
  85.0 0.9 collective-permute-done.8
  86.0 0.0 copy-start.1
  86.0 1.7 %copy-done.1 = f32[288,2048]{1,0:T(8,128)S(1)} copy-done((f32[288,2048]{1,0:T(8,128)S(1)}, f32[288,2048]{1,0:T(8,128)}, u32[]{:S(2)}) %copy-start.1) | copy-done | bytes 2359320
  87.7 4.9 %shard_map.84 = (f32[288,2048]{1,0:T(8,128)S(1)}, f32[4,16,128]{2,1,0:T(8,128)S(1)}) custom-call(f32[288,16]{1,0:T(8,128)S(1)} %bitcast.136, f32[2,2048]{1,0:T(2,128)} %wind_ref.1, f32[1,2048]{1,0:T(1,128)S(1)} %add_add_fusion.slope_ref, f32[288,2048]{1,0:T(8,128)S(1)} %copy-done.1), custom_call_target="tpu_custom_call" | custom-call | flops 23592960 | bytes 4718592 | tf_op jit(solution)/shard_map/pallas_call | solution.py:530
  92.6 0.1 collective-permute-start.9
  92.7 1.2 collective-permute-done.9
  93.8 0.6 collective-permute-start.10
  94.5 0.6 slice_reduce_fusion
  95.1 2.5 %collective-permute-done.10 = f32[2,16,128]{2,1,0:T(8,128)S(1)} collective-permute-done((f32[2,16,128]{2,1,0:T(8,128)S(1)}, f32[2,16,128]{2,1,0:T(8,128)S(1)}, u32[]{:S(2)}, u32[]{:S(2)}) %collective-permute-start.10) | collective-permute-done | bytes 16416 | tf_op jit(solution)/shard_map/ppermute | solution.py:543
  97.6 2.6 %collective-permute-start.11 = (f32[2,16,128]{2,1,0:T(8,128)S(1)}, f32[2,16,128]{2,1,0:T(8,128)S(1)}, u32[]{:S(2)}, u32[]{:S(2)}) collective-permute-start(f32[2,16,128]{2,1,0:T(8,128)S(1)} %add.600), channel_id=1, source_target_pairs={{0,4},{4,0},{8,12},{12,8},{1,5},{5,1},{9,13},{13,9},{2,6},{6,2},{1... | collective-permute-start | bytes 49160 | tf_op jit(solution)/shard_map/ppermute | solution.py:548
  100.1 3.4 %collective-permute-start.12 = (f32[2,16,128]{2,1,0:T(8,128)S(1)}, f32[2,16,128]{2,1,0:T(8,128)S(1)}, u32[]{:S(2)}, u32[]{:S(2)}) collective-permute-start(f32[2,16,128]{2,1,0:T(8,128)S(1)} %add.600), channel_id=1, source_target_pairs={{0,8},{4,12},{8,0},{12,4},{1,9},{5,13},{9,1},{13,5},{2,10},{6,14},... | collective-permute-start | bytes 49160 | tf_op jit(solution)/shard_map/ppermute | solution.py:548
  103.5 0.7 broadcast_xor_fusion
  104.2 12.0 %pmax.7 = s32[]{:T(128)} all-reduce(s32[]{:T(128)} %slice_reduce_fusion), channel_id=1, replica_groups=mesh['grp'=2,'pts'=4,'spec'=2,'cpl'=2] {'grp','pts'}, use_global_device_ids=true, to_apply=%region_1.2 | all-reduce | flops 1 | bytes 8 | tf_op jit(solution)/shard_map/pmax | solution.py:509
  116.9 11.6 %copy.52 = f32[18,16,2048]{0,1,2:T(8,128)} copy(f32[18,16,2048]{2,1,0:T(8,128)S(1)} %bitcast.134) | data formatting | bytes 4718592 | tf_op jit(solution)/shard_map/reshape;reshape | solution.py:567
  128.6 1.2 shard_map.85
  129.8 11.5 %conditional.1 = (f32[1,1024]{1,0:T(1,128)}, f32[1,1024]{1,0:T(1,128)}, f32[16,18,2048]{2,0,1:T(8,128)}) conditional(s32[]{:T(128)} %convert_element_type.106, (f32[16,18,2048]{1,0,2:T(8,128)}, f32[1,1024]{1,0:T(1,128)}, f32[1,1024]{1,0:T(1,128)}) %tuple.100, (s32[128,128]{1,0:T(8,128)S(1)}, f32[16,18,2048]{2,0,1:T(8,128)}, f32[2,2048]{1,0:T(2,128)S(1)}, ...), branch_computations={%region_2.4_spmd, %region_3.18_spmd} | conditional | flops 56902224 | bytes 335072736 | solution.py:568
  129.8 11.4 %copy.60 = f32[16,18,2048]{2,0,1:T(8,128)} copy(f32[16,18,2048]{1,0,2:T(8,128)} %get-tuple-element.150) | data formatting | bytes 4718592 | tf_op jit(solution)/shard_map/cond | solution.py:568
  (43 shorter events, 0.3 us)
Async XLA Ops:
  0.6 63.6 %collective-permute-start.2 = (f32[288,2048]{1,0:T(8,128)}, f32[288,2048]{1,0:T(8,128)S(1)}, u32[]{:S(2)}, u32[]{:S(2)}) collective-permute-start(f32[288,2048]{1,0:T(8,128)} %bitcast.147), channel_id=1, source_target_pairs={{0,4},{1,13},{4,8},{5,1},{8,12},{9,5},{12,0},{13,9},{2,6},{3,15},{... | collective-permute-start | bytes 7077896 | tf_op jit(solution)/shard_map/ppermute | solution.py:486
  3.8 126.0 %copy-start.6 = (s32[128,128]{1,0:T(8,128)S(1)}, s32[128,128]{1,0:T(8,128)}, u32[]{:S(2)}) copy-start(s32[128,128]{1,0:T(8,128)} %cell_ref.1) | copy-start | bytes 196612
  3.8 126.0 %copy-start.7 = (f32[2,2048]{1,0:T(2,128)S(1)}, f32[2,2048]{1,0:T(2,128)}, u32[]{:S(2)}) copy-start(f32[2,2048]{1,0:T(2,128)} %wind_ref.1) | copy-start | bytes 49156
  3.8 126.0 %copy-start.8 = (s32[1024]{0:T(1024)S(1)}, s32[1024]{0:T(1024)}, u32[]{:S(2)}) copy-start(s32[1024]{0:T(1024)} %param.15) | copy-start | bytes 12292
  3.8 126.0 %copy-start.9 = (s32[1024]{0:T(1024)S(1)}, s32[1024]{0:T(1024)}, u32[]{:S(2)}) copy-start(s32[1024]{0:T(1024)} %param.14) | copy-start | bytes 12292
  9.8 51.4 %collective-permute-start.3 = (f32[288,128]{1,0:T(8,128)S(1)}, f32[288,128]{1,0:T(8,128)S(1)}, u32[]{:S(2)}, u32[]{:S(2)}) collective-permute-start(f32[288,128]{1,0:T(8,128)S(1)} %get-tuple-element.37), channel_id=1, source_target_pairs={{0,4},{4,8},{8,12},{12,0},{1,5},{5,9},{9,13},{13,1},{2,6},{6,10},{... | collective-permute-start | bytes 442376 | tf_op jit(solution)/shard_map/ppermute | solution.py:506
  11.4 49.8 %collective-permute-start.4 = (f32[288,128]{1,0:T(8,128)S(1)}, f32[288,128]{1,0:T(8,128)S(1)}, u32[]{:S(2)}, u32[]{:S(2)}) collective-permute-start(f32[288,128]{1,0:T(8,128)S(1)} %get-tuple-element.38), channel_id=1, source_target_pairs={{0,8},{4,12},{8,0},{12,4},{1,9},{5,13},{9,1},{13,5},{2,10},{6,14},... | collective-permute-start | bytes 442376 | tf_op jit(solution)/shard_map/ppermute | solution.py:506
  12.5 51.7 %collective-permute-start.5 = (f32[288,128]{1,0:T(8,128)S(1)}, f32[288,128]{1,0:T(8,128)S(1)}, u32[]{:S(2)}, u32[]{:S(2)}) collective-permute-start(f32[288,128]{1,0:T(8,128)S(1)} %get-tuple-element.39), channel_id=1, source_target_pairs={{0,12},{4,0},{8,4},{12,8},{1,13},{5,1},{9,5},{13,9},{2,14},{6,2},{... | collective-permute-start | bytes 442376 | tf_op jit(solution)/shard_map/ppermute | solution.py:506
  77.0 1.4 copy-start
  78.4 4.5 %collective-permute-start.6 = (f32[1,2048]{1,0:T(1,128)S(1)}, f32[1,2048]{1,0:T(1,128)S(1)}, u32[]{:S(2)}, u32[]{:S(2)}) collective-permute-start(f32[1,2048]{1,0:T(1,128)S(1)} %get-tuple-element.40), channel_id=1, source_target_pairs={{0,1},{1,0},{2,3},{3,2},{4,5},{5,4},{6,7},{7,6},{8,9},{9,8},{10,11... | collective-permute-start | bytes 24584 | tf_op jit(solution)/shard_map/ppermute | solution.py:524
  81.4 3.7 %collective-permute-start.7 = (f32[1,2048]{1,0:T(1,128)S(1)}, f32[1,2048]{1,0:T(1,128)S(1)}, u32[]{:S(2)}, u32[]{:S(2)}) collective-permute-start(f32[1,2048]{1,0:T(1,128)S(1)} %get-tuple-element.40), channel_id=1, source_target_pairs={{0,2},{1,3},{2,0},{3,1},{4,6},{5,7},{6,4},{7,5},{8,10},{9,11},{10,... | collective-permute-start | bytes 24584 | tf_op jit(solution)/shard_map/ppermute | solution.py:524
  82.9 3.1 %collective-permute-start.8 = (f32[1,2048]{1,0:T(1,128)S(1)}, f32[1,2048]{1,0:T(1,128)S(1)}, u32[]{:S(2)}, u32[]{:S(2)}) collective-permute-start(f32[1,2048]{1,0:T(1,128)S(1)} %get-tuple-element.40), channel_id=1, source_target_pairs={{0,3},{1,2},{2,1},{3,0},{4,7},{5,6},{6,5},{7,4},{8,11},{9,10},{10,... | collective-permute-start | bytes 24584 | tf_op jit(solution)/shard_map/ppermute | solution.py:524
  86.0 1.7 %copy-start.1 = (f32[288,2048]{1,0:T(8,128)S(1)}, f32[288,2048]{1,0:T(8,128)}, u32[]{:S(2)}) copy-start(f32[288,2048]{1,0:T(8,128)} %copy-done) | copy-start | bytes 7077892
  92.6 1.2 collective-permute-start.9
  93.8 3.7 %collective-permute-start.10 = (f32[2,16,128]{2,1,0:T(8,128)S(1)}, f32[2,16,128]{2,1,0:T(8,128)S(1)}, u32[]{:S(2)}, u32[]{:S(2)}) collective-permute-start(f32[2,16,128]{2,1,0:T(8,128)S(1)} %fusion.48), channel_id=1, source_target_pairs={{0,2},{2,0},{1,3},{3,1},{4,6},{6,4},{5,7},{7,5},{8,10},{10,8},{9,1... | collective-permute-start | bytes 49160 | tf_op jit(solution)/shard_map/ppermute | solution.py:543
  97.6 31.0 %collective-permute-start.11 = (f32[2,16,128]{2,1,0:T(8,128)S(1)}, f32[2,16,128]{2,1,0:T(8,128)S(1)}, u32[]{:S(2)}, u32[]{:S(2)}) collective-permute-start(f32[2,16,128]{2,1,0:T(8,128)S(1)} %add.600), channel_id=1, source_target_pairs={{0,4},{4,0},{8,12},{12,8},{1,5},{5,1},{9,13},{13,9},{2,6},{6,2},{1... | collective-permute-start | bytes 49160 | tf_op jit(solution)/shard_map/ppermute | solution.py:548
  100.1 28.4 %collective-permute-start.12 = (f32[2,16,128]{2,1,0:T(8,128)S(1)}, f32[2,16,128]{2,1,0:T(8,128)S(1)}, u32[]{:S(2)}, u32[]{:S(2)}) collective-permute-start(f32[2,16,128]{2,1,0:T(8,128)S(1)} %add.600), channel_id=1, source_target_pairs={{0,8},{4,12},{8,0},{12,4},{1,9},{5,13},{9,1},{13,5},{2,10},{6,14},... | collective-permute-start | bytes 49160 | tf_op jit(solution)/shard_map/ppermute | solution.py:548
  103.5 25.0 %collective-permute-start.13 = (f32[2,16,128]{2,1,0:T(8,128)S(1)}, f32[2,16,128]{2,1,0:T(8,128)S(1)}, u32[]{:S(2)}, u32[]{:S(2)}) collective-permute-start(f32[2,16,128]{2,1,0:T(8,128)S(1)} %add.600), channel_id=1, source_target_pairs={{0,12},{4,8},{8,4},{12,0},{1,13},{5,9},{9,5},{13,1},{2,14},{6,10},... | collective-permute-start | bytes 49160 | tf_op jit(solution)/shard_map/ppermute | solution.py:548

commit v2 on v1

--- a/solution.py
+++ b/solution.py
@@ -167,6 +167,7 @@
 
 C_KEEP, C_ROW, C_COL, C_SLOPE, C_EAST, C_NORTH, C_ONE, C_DAMP = range(8)
 C_S_EAST, C_S_NORTH, C_T_EAST, C_T_NORTH = range(8, 12)
+CHUNK_ENDS = (5, 10, 15)
 
 
 def split3(value):
@@ -185,8 +186,8 @@
     return parts[0] + parts[1] + parts[2]
 
 
-def index_kernel(owners, par_ref, cell_ref, g_ref, idx_ref, *list_refs):
-    slots = idx_ref.shape[1]
+def index_kernel(owners, par_ref, cell_ref, coef_ref, g_ref, idx_ref, count_ref, sum_ref, *list_refs):
+    slots = g_ref.shape[1]
     blocks = slots // LANES
     half_rows = g_ref.shape[0] // 2
     shift = owners.bit_length() - 1
@@ -201,6 +202,17 @@
     below = jnp.concatenate([number[1:], edge], axis=0)
     to_above = jnp.where(sea & (above >= 0.0), number - above, 0.0)
     to_below = jnp.where(sea & (below >= 0.0), below - number, 0.0)
+    ids = cell_ref[...] & (owners - 1)
+    above_ids = above.astype(I32) & (owners - 1)
+    crossing = (to_above > 0.0) & (ids != above_ids)
+    pair = jnp.where(crossing, above_ids * owners + ids, -1)
+
+    @pl.loop(0, owners * owners)
+    def _(which):
+        count_ref[pl.ds(which, 1), :] = jnp.sum(
+            jnp.where(pair == which, 1.0, 0.0), axis=0, keepdims=True
+        )
+
     cols = number.shape[1]
     column = lax.broadcasted_iota(I32, number.shape, 1)
     left = jnp.where(column == 0, -1.0, pltpu.roll(number, 1, 1))
@@ -257,7 +269,15 @@
         counts.append((inside + carry) * part)
         carry = carry + jnp.sum(part, axis=1, keepdims=True)
     counts = jnp.concatenate(counts, axis=1)
-    excess = jnp.zeros((1, slots), I32)
+    sum_ref[...] = jnp.zeros_like(sum_ref)
+    for half in range(2):
+        rows = slice(half * half_rows, (half + 1) * half_rows)
+        weight = coef_ref[rows, C_SLOPE : C_SLOPE + 1]
+        weighted = g_ref[rows, :] * weight
+        for at, column_of in ((0, C_KEEP), (1 + half, C_ROW), (3, C_COL)):
+            sum_ref[at : at + 1, :] += jnp.sum(
+                weighted * coef_ref[rows, column_of : column_of + 1], axis=0, keepdims=True
+            )
     entry = lax.broadcasted_iota(I32, ((owners - 1) * LANES, slots), 0)
     for half in range(2):
         places = [
@@ -270,110 +290,129 @@
         ]
         away, other_slot = codes[2 * half]
         place = places[0]
-        excess = jnp.maximum(excess, jnp.where((away > 0) & (place >= LANES), 1, 0))
         same_block = (other_slot >> 7) == (slot >> 7)
         code = jnp.where(away == 0, jnp.where(same_block, 1, 2), away + 2)
         code = jnp.where(away < 0, 0, code)
         lane = jnp.where(away == 0, other_slot & (LANES - 1), jnp.minimum(place, LANES - 1))
-        idx_ref[2 * half : 2 * half + 1, :] = jnp.where(away < 0, 0, lane)
-        idx_ref[2 * half + 1 : 2 * half + 2, :] = code
+        lane = jnp.where(away < 0, 0, lane)
+        idx_ref[2 * half] = jnp.broadcast_to(lane, (8, slots))
+        idx_ref[2 * half + 1] = jnp.broadcast_to(code, (8, slots))
         away, _ = codes[2 * half + 1]
         place = places[1]
         key = jnp.where((away > 0) & (place < LANES), (away - 1) * LANES + place, -1)
         one_hot = jnp.where(entry == key, 1.0, 0.0).astype(BF16)
         rows = slice(half * half_rows, (half + 1) * half_rows)
         packed = times_exact(g_ref[rows, :], one_hot, ((1,), (1,)))
+        sums = times_exact(sum_ref[...], one_hot, ((1,), (1,)))
         for at, list_ref in enumerate(list_refs):
-            list_ref[rows, :] = packed[:, at * LANES : (at + 1) * LANES]
-    idx_ref[4:5, :] = has_beside
-    idx_ref[5:6, :] = excess
-    idx_ref[6:8, :] = jnp.zeros((2, slots), I32)
+            lanes = slice(at * LANES, (at + 1) * LANES)
+            list_ref[rows, :] = packed[:, lanes]
+            row = 2 * half_rows + half
+            list_ref[row : row + 1, :] = sums[1 + half : 2 + half, lanes]
+    for list_ref in list_refs:
+        list_ref[2 * half_rows + 2 :, :] = jnp.zeros((6, LANES), F32)
+    idx_ref[4] = jnp.broadcast_to(has_beside, (8, slots))
 
 
 def lane_take(values, lanes):
     return jnp.take_along_axis(values, lanes, axis=1)
 
 
-def advance_kernel(owners, par_ref, coef_ref, idx_ref, g_ref, beside_ref, *refs):
-    list_refs = refs[: owners - 1]
-    out_ref, slope_ref, total_ref = refs[owners - 1 :]
-    slots = idx_ref.shape[1]
-    blocks = slots // LANES
-    tiles = g_ref.shape[0] // 16
+def row_neighbour(shape, code, lanes, own, near, lists):
+    value = jnp.where(code == 1, lane_take(own, lanes), 0.0)
+    value = jnp.where(code == 2, lane_take(near, lanes), value)
+    for number, values in enumerate(lists):
+        value = jnp.where(code == 3 + number, lane_take(values, lanes), value)
+    return value
+
+
+def near_block(ref, rows, block, step):
+    which = jnp.clip(block + step, 0, ref.shape[1] // LANES - 1)
+    return ref[rows, pl.ds(pl.multiple_of(which * LANES, LANES), LANES)]
+
+
+def turned_lanes(turn):
+    lane = lax.broadcasted_iota(I32, (8, LANES), 1)
+    lanes = (lane + turn) & (LANES - 1)
+    return lanes, (lane + turn) != lanes
+
+
+def slope_kernel(par_ref, idx_ref, sum_ref, beside_ref, *refs):
+    list_refs, slope_ref = refs[:-1], refs[-1]
     shape = (8, LANES)
-    total_ref[...] = jnp.zeros_like(total_ref)
     turn = par_ref[3]
-    lane = lax.broadcasted_iota(I32, shape, 1)
-    beside_lane = (lane + turn) & (LANES - 1)
-    beyond = (lane + turn) != beside_lane
-
-    for half in range(2):
-        way = par_ref[1 + half]
-
-        @pl.loop(0, tiles)
-        def _(tile):
-            rows = pl.ds(pl.multiple_of((half * tiles + tile) * 8, 8), 8)
-            coef = coef_ref[rows, :]
-
-            def factor(at):
-                return jnp.broadcast_to(coef[:, at : at + 1], shape)
-
-            keep, by_row, by_col = factor(C_KEEP), factor(C_ROW), factor(C_COL)
-            by_slope = factor(C_SLOPE)
-            lists = [ref[rows, :] for ref in list_refs]
-            for block in range(blocks):
-                at = slice(block * LANES, (block + 1) * LANES)
-
-                def near(ref, step):
-                    which = jnp.clip(block + step, 0, blocks - 1)
-                    return ref[rows, pl.ds(pl.multiple_of(which * LANES, LANES), LANES)]
-
-                lanes = jnp.broadcast_to(idx_ref[2 * half : 2 * half + 1, at], shape)
-                code = jnp.broadcast_to(idx_ref[2 * half + 1 : 2 * half + 2, at], shape)
-                has_beside = jnp.broadcast_to(idx_ref[4:5, at], shape)
-                own = g_ref[rows, at]
-                row_value = jnp.where(code == 1, lane_take(own, lanes), 0.0)
-                row_value = jnp.where(code == 2, lane_take(near(g_ref, way), lanes), row_value)
-                for number, values in enumerate(lists):
-                    row_value = jnp.where(code == 3 + number, lane_take(values, lanes), row_value)
-                col_value = jnp.where(
-                    beyond,
-                    lane_take(near(beside_ref, turn), beside_lane),
-                    lane_take(beside_ref[rows, at], beside_lane),
-                )
-                col_value = jnp.where(has_beside > 0, col_value, 0.0)
-                moved = keep * own + by_row * row_value + by_col * col_value
-                out_ref[rows, at] = moved
-                total_ref[:, at] += by_slope * moved
-
-    slope_ref[...] = jnp.sum(total_ref[...], axis=0, keepdims=True)
-
-
-def source_kernel(coef_ref, wind_ref, slope_ref, prop_ref, out_ref, sums_ref, total_ref):
-    slots = prop_ref.shape[1]
-    blocks = slots // LANES
+    beside_lanes, beyond = turned_lanes(turn)
+    every = slice(0, 8)
+    lists = [ref[...] for ref in list_refs]
+    for block in range(sum_ref.shape[1] // LANES):
+        at = slice(block * LANES, (block + 1) * LANES)
+        own = sum_ref[:, at]
+        slope = own[0:1]
+        for half in range(2):
+            lanes, code = idx_ref[2 * half, :, at], idx_ref[2 * half + 1, :, at]
+            near = near_block(sum_ref, every, block, par_ref[1 + half])
+            here = jnp.where(code == 1, lane_take(own, lanes), 0.0)
+            here = jnp.where(code == 2, lane_take(near, lanes), here)
+            slope = slope + here[1 + half : 2 + half]
+            there = jnp.zeros(shape, F32)
+            for number, values in enumerate(lists):
+                there = jnp.where(code == 3 + number, lane_take(values, lanes), there)
+            slope = slope + there[half : half + 1]
+        column = jnp.where(
+            beyond,
+            lane_take(jnp.broadcast_to(near_block(beside_ref, slice(0, 1), block, turn), shape), beside_lanes),
+            lane_take(jnp.broadcast_to(beside_ref[:, at], shape), beside_lanes),
+        )
+        slope_ref[:, at] = slope + jnp.where(idx_ref[4, 0:1, at] > 0, column[0:1], 0.0)
+
+
+def step_kernel(owners, first_step, half_steps, chained, final, par_ref, idx_ref, wind_ref, slope_ref, coef_ref, g_ref, beside_ref, *refs):
+    list_refs, refs = refs[: owners - 1], refs[owners - 1 :]
+    if chained:
+        _, before_ref, refs = refs[0], refs[1], refs[2:]
+    out_ref, sums_refs, total_ref, damp_ref = refs[0], refs[1:-2], refs[-2], refs[-1]
+    blocks = g_ref.shape[1] // LANES
     shape = (8, LANES)
-    total_ref[...] = jnp.zeros_like(total_ref)
-
-    @pl.loop(0, prop_ref.shape[0] // 8)
-    def _(tile):
-        rows = pl.ds(pl.multiple_of(tile * 8, 8), 8)
+    half = jnp.where(pl.program_id(0) + first_step >= half_steps, 1, 0)
+    way, turn = par_ref[1 + half], par_ref[3]
+    beside_lanes, beyond = turned_lanes(turn)
+
+    @pl.when(pl.program_id(0) == 0)
+    def _():
+        total_ref[...] = jnp.zeros_like(total_ref)
+        slope = slope_ref[...]
+        damp_ref[...] = jnp.broadcast_to(slope * slope, damp_ref.shape)
+
+    for tile in range(g_ref.shape[0] // 8):
+        rows = slice(tile * 8, tile * 8 + 8)
         coef = coef_ref[rows, :]
 
         def factor(at):
             return jnp.broadcast_to(coef[:, at : at + 1], shape)
 
+        keep, by_row, by_col = factor(C_KEEP), factor(C_ROW), factor(C_COL)
         east, north, one, damp = factor(C_EAST), factor(C_NORTH), factor(C_ONE), factor(C_DAMP)
         s_east, s_north = factor(C_S_EAST), factor(C_S_NORTH)
         t_east, t_north = factor(C_T_EAST), factor(C_T_NORTH)
+        lists = [ref[rows, :] for ref in list_refs]
         for block in range(blocks):
             at = slice(block * LANES, (block + 1) * LANES)
+            lanes, code = idx_ref[2 * half, :, at], idx_ref[2 * half + 1, :, at]
+            has_beside = idx_ref[4, :, at]
+            own = g_ref[rows, at]
+            near = near_block(g_ref, rows, block, way)
+            row_value = row_neighbour(shape, code, lanes, own, near, lists)
+            col_value = jnp.where(
+                beyond,
+                lane_take(near_block(beside_ref, rows, block, turn), beside_lanes),
+                lane_take(beside_ref[rows, at], beside_lanes),
+            )
+            col_value = jnp.where(has_beside > 0, col_value, 0.0)
+            value = keep * own + by_row * row_value + by_col * col_value
             wind_east = jnp.broadcast_to(wind_ref[0:1, at], shape)
             wind_north = jnp.broadcast_to(wind_ref[1:2, at], shape)
-            slope = jnp.broadcast_to(slope_ref[0:1, at], shape)
-            value = prop_ref[rows, at]
             growth = jnp.maximum(east * wind_east + north * wind_north - one, 0.0)
-            updated = value * jnp.exp(growth - damp * (slope * slope))
+            updated = value * jnp.exp(growth - damp * damp_ref[:, at])
             out_ref[rows, at] = updated
             lifted = growth * value
             total_ref[0, :, at] += s_east * lifted
@@ -381,26 +420,41 @@
             total_ref[2, :, at] += t_east * updated
             total_ref[3, :, at] += t_north * updated
 
-    for item in range(4):
-        for block in range(blocks):
-            at = slice(block * LANES, (block + 1) * LANES)
-            sums_ref[item, block : block + 1, :] = jnp.sum(
-                total_ref[item, :, at], axis=0, keepdims=True
-            )
-
-
-def pick_kernel(owners, table_ref, atm_ref, ocean_ref, stress_ref, stokes_ref):
+    @pl.when(pl.program_id(0) == pl.num_programs(0) - 1)
+    def _():
+        cpl = par_ref[4]
+        for item in range(2):
+            for block in range(blocks):
+                at = slice(block * LANES, (block + 1) * LANES)
+                pair = []
+                for part in range(2):
+                    value = jnp.sum(total_ref[2 * item + part, :, at], axis=0, keepdims=True)
+                    if chained:
+                        value = value + before_ref[2 * item + part, block : block + 1, :]
+                    pair.append(value)
+                where = slice(block, block + 1)
+                if final:
+                    sums_refs[0][item, where, :] = jnp.where(cpl == 0, pair[0], pair[1])
+                    sums_refs[1][item, where, :] = jnp.where(cpl == 0, pair[1], pair[0])
+                else:
+                    sums_refs[0][2 * item, where, :] = pair[0]
+                    sums_refs[0][2 * item + 1, where, :] = pair[1]
+
+
+def pick_kernel(owners, atm_ref, ocean_ref, *refs):
+    table_refs, (stress_ref, stokes_ref) = refs[:owners], refs[owners:]
     shift = owners.bit_length() - 1
-    blocks = table_ref.shape[1] // owners
+    blocks = table_refs[0].shape[1]
     for item, (order_ref, out_ref) in enumerate(((atm_ref, stress_ref), (ocean_ref, stokes_ref))):
         point = order_ref[...]
         count = point.shape[1]
         slot = point >> shift
         row = (point & (owners - 1)) * blocks + (slot >> 7)
         lane = slot & (LANES - 1)
-        rows = table_ref.shape[1]
+        rows = owners * blocks
         hot = jnp.where(lax.broadcasted_iota(I32, (rows, count), 0) == row, 1.0, 0.0).astype(BF16)
-        table = jnp.transpose(table_ref[item])
+        table = jnp.concatenate([ref[item] for ref in table_refs], axis=0)
+        table = jnp.transpose(table)
         found = times_exact(table, hot, ((1,), (0,)))
         pick = lax.broadcasted_iota(I32, (LANES, count), 0) == lane
         out_ref[...] = jnp.sum(jnp.where(pick, found, 0.0), axis=0, keepdims=True)
@@ -457,13 +511,20 @@
     )
 
 
+def chunks_of(steps):
+    ends = sorted({max(1, steps * part // 18) for part in CHUNK_ENDS} | {steps})
+    return list(zip([0] + ends[:-1], ends))
+
+
 def local(spec_deck, wind_deck, cell_sea, atm_order, ocean_order):
     owners = lax.axis_size("pts")
     spec_groups = lax.axis_size("spec")
     cpl_groups = lax.axis_size("cpl")
+    groups = lax.axis_size("grp")
     my_pts = lax.axis_index("pts")
     my_spec = lax.axis_index("spec")
     my_cpl = lax.axis_index("cpl")
+    assert cpl_groups == 2 and owners & (owners - 1) == 0
     freq_local, dirs_local, slots = spec_deck.shape
     freq_count = freq_local * spec_groups
     dir_count = dirs_local * cpl_groups
@@ -471,19 +532,27 @@
     half_rows = freq_local * dirs_local // 2
     pad_half = -half_rows % 8
     rows = 2 * (half_rows + pad_half)
+    step_rows = 16 if (half_rows + pad_half) % 16 == 0 else 8
+    steps = rows // step_rows
 
     field = jnp.transpose(spec_deck, (1, 0, 2)).reshape(2, half_rows, slots)
     if pad_half:
         field = jnp.pad(field, ((0, 0), (0, pad_half), (0, 0)))
     field = field.reshape(rows, slots)
 
-    flat = owners * cpl_groups
     ring = []
     for owner in range(owners):
         ring.append((owner * 2, (owner + 1) % owners * 2))
         ring.append((owner * 2 + 1, (owner - 1) % owners * 2 + 1))
-    assert flat == len(ring)
-    beside = lax.ppermute(field, ("pts", "cpl"), ring)
+
+    def around(values):
+        return lax.ppermute(values, ("pts", "cpl"), ring)
+
+    def chunk(values, at):
+        return values[at[0] * step_rows : at[1] * step_rows]
+
+    chunks = chunks_of(steps)
+    beside = [around(chunk(field, chunks[0]))]
 
     first_way = 2 * my_cpl - 1
     turn = jnp.where(
@@ -496,26 +565,41 @@
 
     found = call(
         functools.partial(index_kernel, owners),
-        [SCALARS, WHOLE, WHOLE],
-        [shape_of(8, slots, kind=I32)] + [shape_of(rows, LANES)] * (owners - 1),
+        [SCALARS, WHOLE, WHOLE, WHOLE],
+        [
+            shape_of(5, 8, slots, kind=I32),
+            shape_of(owners * owners, cell_sea.shape[1]),
+            shape_of(8, slots),
+        ]
+        + [shape_of(rows + 8, LANES)] * (owners - 1),
         flops=6 * rows * slots * LANES * owners,
         moved=rows * slots * 4,
-    )(par, cell_sea, field)
-    idx, lists = found[0], found[1:]
+    )(par, cell_sea, coef, field)
+    (idx, counts, row_sums), lists = found[:3], found[3:]
     arrived = [
         lax.ppermute(values, "pts", [(i, (i + 1 + away) % owners) for i in range(owners)])
         for away, values in enumerate(lists)
     ]
-    excess = lax.pmax(jnp.max(idx[5]), ("grp", "pts"))
-
-    propagated, slope_part = call(
-        functools.partial(advance_kernel, owners),
-        [SCALARS] + [WHOLE] * (owners + 3),
-        [shape_of(rows, slots), shape_of(1, slots)],
-        [pltpu.VMEM((8, slots), F32)],
-        flops=rows * slots * 20,
-        moved=rows * slots * 12,
-    )(par, coef, idx, field, beside, *arrived)
+    beside_sums = around(row_sums[3:4])
+    later, *_ = lax.optimization_barrier((field, *lists))
+    beside += [around(chunk(later, at)) for at in chunks[1:]]
+
+    longest = jnp.max(jnp.sum(counts, axis=1)).reshape(1, 1)
+    if groups == 2:
+        longest = jnp.maximum(longest, lax.ppermute(longest, "grp", [(0, 1), (1, 0)]))
+    else:
+        longest = lax.pmax(longest, "grp")
+
+    tail_block = pl.BlockSpec((8, LANES), lambda i: (rows // 8, 0))
+    whole = lambda *dims: pl.BlockSpec(dims, lambda i: (0,) * len(dims))
+    slope_part = pl.pallas_call(
+        slope_kernel,
+        grid=(1,),
+        in_specs=[SCALARS, whole(5, 8, slots), whole(8, slots), whole(1, slots)]
+        + [tail_block] * (owners - 1),
+        out_specs=whole(1, slots),
+        out_shape=shape_of(1, slots),
+    )(par, idx, row_sums, beside_sums, *arrived)
 
     peers = spec_groups * cpl_groups
     slope = slope_part
@@ -527,49 +611,81 @@
     else:
         slope = lax.psum(slope_part, ("spec", "cpl"))
 
-    updated, sums = call(
-        source_kernel,
-        [WHOLE] * 4,
-        [shape_of(rows, slots), shape_of(4, blocks, LANES)],
-        [pltpu.VMEM((4, 8, slots), F32)],
-        flops=rows * slots * 40,
-        moved=rows * slots * 8,
-    )(coef, wind_deck, slope, propagated)
-
-    mine = jnp.take(sums.reshape(2, 2, blocks, LANES), my_cpl, axis=1)
-    others = jnp.take(sums.reshape(2, 2, blocks, LANES), 1 - my_cpl, axis=1)
+    updated = sums = None
+    for at, near in zip(chunks, beside):
+        start, stop = at
+        chained, final = start > 0, stop == steps
+        in_rows = lambda width: pl.BlockSpec(
+            (step_rows, width), functools.partial(lambda first, i: (first + i, 0), start)
+        )
+        inputs = [par, idx, wind_deck, slope, coef, field, near, *arrived]
+        specs = [SCALARS, whole(5, 8, slots), whole(2, slots), whole(1, slots), in_rows(16)]
+        specs += [in_rows(slots), pl.BlockSpec((step_rows, slots), lambda i: (i, 0))]
+        specs += [in_rows(LANES)] * (owners - 1)
+        aliases = {}
+        if chained:
+            aliases = {len(inputs): 0}
+            inputs += [updated, sums]
+            specs += [pl.BlockSpec(memory_space=pl.ANY), whole(4, blocks, LANES)]
+        sum_shapes = [(2, blocks, LANES)] * 2 if final else [(4, blocks, LANES)]
+        updated, *sums = pl.pallas_call(
+            functools.partial(step_kernel, owners, start, steps // 2, chained, final),
+            grid=(stop - start,),
+            in_specs=specs,
+            out_specs=[in_rows(slots)] + [whole(*dims) for dims in sum_shapes],
+            out_shape=[shape_of(rows, slots)] + [shape_of(*dims) for dims in sum_shapes],
+            scratch_shapes=[pltpu.VMEM((4, 8, slots), F32), pltpu.VMEM((8, slots), F32)],
+            input_output_aliases=aliases,
+            compiler_params=pltpu.CompilerParams(vmem_limit_bytes=24 * 1024 * 1024),
+            cost_estimate=pl.CostEstimate(
+                flops=(stop - start) * step_rows * slots * 50,
+                bytes_accessed=(stop - start) * step_rows * slots * 12,
+                transcendentals=(stop - start) * step_rows * slots,
+            ),
+        )(*inputs)
+        if not final:
+            sums = sums[0]
+
+    mine, others = sums
     mine = mine + lax.ppermute(others, "cpl", [(0, 1), (1, 0)])
     if spec_groups == 2:
         mine = mine + lax.ppermute(mine, "spec", [(0, 1), (1, 0)])
     else:
         mine = lax.psum(mine, "spec")
     if owners == 4:
-        around = [mine] + [
+        tables = [mine] + [
             lax.ppermute(mine, "pts", [(i, i ^ turned) for i in range(owners)])
             for turned in range(1, owners)
         ]
-        table = jnp.stack(around, axis=1)
-        looked = lambda order: order ^ my_pts
+        looked = lambda order: (order ^ my_pts)[None, :]
     else:
-        table = lax.all_gather(mine, "pts", axis=1)
-        looked = lambda order: order
-    table = table.reshape(2, owners * blocks, LANES)
+        gathered = lax.all_gather(mine, "pts", axis=0)
+        tables = [gathered[owner] for owner in range(owners)]
+        looked = lambda order: order[None, :]
     count = atm_order.shape[0]
     stress_atm, stokes_ocn = call(
         functools.partial(pick_kernel, owners),
-        [WHOLE] * 3,
+        [WHOLE] * (2 + owners),
         [shape_of(1, count)] * 2,
         flops=owners * blocks * LANES * count * 12,
         moved=owners * blocks * LANES * 8,
-    )(table, looked(atm_order)[None, :], looked(ocean_order)[None, :])
-
-    updated = updated.reshape(2, half_rows + pad_half, slots)[:, :half_rows]
+    )(looked(atm_order), looked(ocean_order), *tables)
+
+    def by_direction(values):
+        return jnp.transpose(values, (1, 0, 2)).reshape(dirs_local * freq_local, slots)
+
+    def general_way():
+        spectra, stress, stokes = general(spec_deck, wind_deck, cell_sea, atm_order, ocean_order)
+        return by_direction(spectra), stress, stokes
+
+    if pad_half:
+        updated = updated.reshape(2, half_rows + pad_half, slots)[:, :half_rows]
+        updated = updated.reshape(2 * half_rows, slots)
+    updated, stress_atm, stokes_ocn = lax.cond(
+        longest[0, 0] > LANES, general_way, lambda: (updated, stress_atm, stokes_ocn)
+    )
     updated = jnp.transpose(updated.reshape(dirs_local, freq_local, slots), (1, 0, 2))
-    return lax.cond(
-        excess > 0,
-        lambda: general(spec_deck, wind_deck, cell_sea, atm_order, ocean_order),
-        lambda: (updated, stress_atm, stokes_ocn),
-    )
+    return updated, stress_atm, stokes_ocn
 
 
 def solution(mesh):

time: 142 us -> 119 us (0.84)
  local copies, waits for them, and re-layouts: 29.1 us -> 12.7 us
  blocking collectives: 12 us -> 0 us
  starting transfers between devices: 19.8 us -> 24.2 us
  Pallas kernels: 24.9 us -> 28 us
  waiting for transfers between devices: 52.4 us -> 49.6 us
    ppermute x1 -> x6, waiting for transfers between devices: 0.01 us -> 39.2 us  [the longest x5 39.2 us: around(): return lax.ppermute(values, ('pts', 'cpl'), ring)]
    ppermute x3, waiting for transfers between devices: 45.7 us -> 6.63 us  [local(): lax.ppermute(values, 'pts', [(i, (i + 1 + away) % owners) for i in range(...]
    pmax x1 -> x0, blocking collectives: 12 us -> none  [local(): excess = lax.pmax(jnp.max(idx[5]), ('grp', 'pts'))]
    another operation x1 -> x0, local copies, waits for them, and re-layouts: 11.6 us -> none  [local(): updated.reshape(dirs_local, freq_local, slots)]
    cond x1 -> x0, local copies, waits for them, and re-layouts: 11.4 us -> none  [local(): lax.cond(excess > 0, lambda: general(spec_deck, wind_deck, cell_sea, atm_...]
    ppermute x1 -> x6, starting transfers between devices: 3.08 us -> 9.02 us  [the longest x5 7.49 us: around(): return lax.ppermute(values, ('pts', 'cpl'), ring)]
    slice x0 -> x4, local copies, waits for them, and re-layouts: none -> 5.49 us  [the longest x3 5.48 us: chunk(): return values[at[0] * step_rows:at[1] * step_rows]]
    pallas_call x4 -> x7, Pallas kernels: 24.9 us -> 28 us  [the longest x4 15.6 us: local(): pl.pallas_call(functools.partial(step_kernel, owners, start, steps // 2,...]
  transfers between devices with their start and end apart: 12 -> 17, of which waited for: 6 -> 6; matrix products, arithmetic and copies ran while one was open for 11% -> 6% of each run, Pallas kernels for 4% -> 13%
where the time goes in v2:
time: 119 us; the launch traced here: 118 us
  waiting for transfers between devices  49.6 us (42%)
  Pallas kernels  28 us (24%)
  starting transfers between devices  24.2 us (20%)
  local copies, waits for them, and re-layouts  12.7 us (11%)
  between operations  2.34 us (2%)
  other arithmetic  1.65 us (1%)
    ppermute x5, waiting for transfers between devices, around(): return lax.ppermute(values, ('pts', 'cpl'), ring)  39.2 us
    pallas_call x4, Pallas kernels, local(): pl.pallas_call(functools.partial(step_kernel, owners, start, steps // 2,...  15.6 us
    pallas_call x1, Pallas kernels, local(): call(functools.partial(index_kernel, owners), [SCALARS, WHOLE, WHOLE, WHO...  9.03 us
    ppermute x5, starting transfers between devices, around(): return lax.ppermute(values, ('pts', 'cpl'), ring)  7.49 us
    ppermute x3, waiting for transfers between devices, local(): lax.ppermute(values, 'pts', [(i, (i + 1 + away) % owners) for i in range(...  6.63 us
    unnamed x44, local copies, waits for them, and re-layouts  6 us
    ppermute x3, starting transfers between devices, local(): lax.ppermute(values, 'pts', [(i, (i + 1 + away) % owners) for i in range(...  5.69 us
    slice x3, local copies, waits for them, and re-layouts, chunk(): return values[at[0] * step_rows:at[1] * step_rows]  5.48 us
  transfers between devices with their start and end apart: 17, of which 6 were waited for; matrix products, arithmetic and copies ran while one was open for 6% of the time, Pallas kernels for 13%

profile of v2, /device:TPU:0, one launch (start us, length us, event | category | flops | bytes accessed | tf_op | source)
XLA Modules:
  0.0 118.4 jit_solution(11252504877268433397)
XLA Ops:
  0.9 0.1 mul.605
  1.0 0.1 mul.608
  1.3 0.1 mul.615
  1.7 0.1 stack_broadcast_in_dim.51
  1.8 0.1 stack_broadcast_in_dim.53
  2.1 0.1 copy.39
  2.3 0.1 stack.40.par_ref
  2.4 9.0 %shard_map.76 = (s32[5,8,2048]{2,1,0:T(8,128)S(1)}, f32[16,128]{1,0:T(8,128)S(1)}, f32[8,2048]{1,0:T(8,128)S(1)}, f32[296,128]{1,0:T(8,128)S(1)}, f32[296,128]{1,0:T(8,128)S(1)}, /*index=5*/f32[296,128]{1,0:T(8,128)S(1)}) custom-call(s32[5]{0:T(128)S(1)} %stack.40.par_ref, s32[128,128]{1,0:T(8,128)} %cell_ref.1, f32[288,16]{1,0:T(8,128)S(1)} %bitcast.114, ...), custom_call_target="tpu_custom_call" | custom-call | flops 1811939328 | bytes 2359296 | tf_op jit(solution)/shard_map/pallas_call | solution.py:566
  11.4 0.7 copy-done
  12.1 3.0 %collective-permute-start.4 = (f32[296,128]{1,0:T(8,128)S(1)}, f32[296,128]{1,0:T(8,128)S(1)}, u32[]{:S(2)}, u32[]{:S(2)}) collective-permute-start(f32[296,128]{1,0:T(8,128)S(1)} %get-tuple-element.49), channel_id=1, source_target_pairs={{0,4},{4,8},{8,12},{12,0},{1,5},{5,9},{9,13},{13,1},{2,6},{6,10},{... | collective-permute-start | bytes 454664 | tf_op jit(solution)/shard_map/ppermute | solution.py:580
  15.1 2.0 %slice.128 = f32[5,16,2048]{2,1,0:T(8,128)} slice(f32[18,16,2048]{2,1,0:T(8,128)} %bitcast.124), slice={[0:5], [0:16], [0:2048]} | slice | bytes 1310720 | tf_op jit(solution)/shard_map/slice | solution.py:552
  17.1 1.6 %collective-permute-start.13 = (f32[80,2048]{1,0:T(8,128)}, f32[80,2048]{1,0:T(8,128)S(1)}, u32[]{:S(2)}, u32[]{:S(2)}) collective-permute-start(f32[80,2048]{1,0:T(8,128)} %bitcast.56), channel_id=1, source_target_pairs={{0,4},{1,13},{4,8},{5,1},{8,12},{9,5},{12,0},{13,9},{2,6},{3,15},{... | collective-permute-start | bytes 1966088 | tf_op jit(solution)/shard_map/ppermute | solution.py:549
  18.7 2.5 %fusion.60 = (f32[80,2048]{1,0:T(8,128)}, f32[80,2048]{1,0:T(8,128)}) fusion(f32[288,2048]{1,0:T(8,128)} %bitcast.125), kind=kLoop, calls=%fused_computation.223 | loop fusion | bytes 2621440 | tf_op jit(solution)/shard_map/slice | solution.py:552
  21.2 1.6 %collective-permute-start.12 = (f32[80,2048]{1,0:T(8,128)}, f32[80,2048]{1,0:T(8,128)S(1)}, u32[]{:S(2)}, u32[]{:S(2)}) collective-permute-start(f32[80,2048]{1,0:T(8,128)} %get-tuple-element.191), channel_id=1, source_target_pairs={{0,4},{1,13},{4,8},{5,1},{8,12},{9,5},{12,0},{13,9},{2,6},{3,15},{... | collective-permute-start | bytes 1966088 | tf_op jit(solution)/shard_map/ppermute | solution.py:549
  22.8 1.8 %collective-permute-start.3 = (f32[1,2048]{1,0:T(1,128)S(1)}, f32[1,2048]{1,0:T(1,128)S(1)}, u32[]{:S(2)}, u32[]{:S(2)}) collective-permute-start(f32[1,2048]{1,0:T(1,128)S(1)} %slice.53), channel_id=1, source_target_pairs={{0,4},{1,13},{4,8},{5,1},{8,12},{9,5},{12,0},{13,9},{2,6},{3,15},{... | collective-permute-start | bytes 24584 | tf_op jit(solution)/shard_map/ppermute | solution.py:549
  24.6 39.2 %collective-permute-done.3.beside_ref = f32[1,2048]{1,0:T(1,128)S(1)} collective-permute-done((f32[1,2048]{1,0:T(1,128)S(1)}, f32[1,2048]{1,0:T(1,128)S(1)}, u32[]{:S(2)}, u32[]{:S(2)}) %collective-permute-start.3) | collective-permute-done | bytes 8224 | tf_op jit(solution)/shard_map/ppermute | solution.py:549
  63.8 1.3 %collective-permute-start.5 = (f32[296,128]{1,0:T(8,128)S(1)}, f32[296,128]{1,0:T(8,128)S(1)}, u32[]{:S(2)}, u32[]{:S(2)}) collective-permute-start(f32[296,128]{1,0:T(8,128)S(1)} %get-tuple-element.50), channel_id=1, source_target_pairs={{0,8},{4,12},{8,0},{12,4},{1,9},{5,13},{9,1},{13,5},{2,10},{6,14},... | collective-permute-start | bytes 454664 | tf_op jit(solution)/shard_map/ppermute | solution.py:580
  65.1 1.4 %collective-permute-start.6 = (f32[296,128]{1,0:T(8,128)S(1)}, f32[296,128]{1,0:T(8,128)S(1)}, u32[]{:S(2)}, u32[]{:S(2)}) collective-permute-start(f32[296,128]{1,0:T(8,128)S(1)} %get-tuple-element.51), channel_id=1, source_target_pairs={{0,12},{4,0},{8,4},{12,8},{1,13},{5,1},{9,5},{13,9},{2,14},{6,2},{... | collective-permute-start | bytes 454664 | tf_op jit(solution)/shard_map/ppermute | solution.py:580
  66.5 6.6 %collective-permute-done.5.refs_1_ = f32[296,128]{1,0:T(8,128)S(1)} collective-permute-done((f32[296,128]{1,0:T(8,128)S(1)}, f32[296,128]{1,0:T(8,128)S(1)}, u32[]{:S(2)}, u32[]{:S(2)}) %collective-permute-start.5) | collective-permute-done | bytes 151584 | tf_op jit(solution)/shard_map/ppermute | solution.py:580
  73.2 0.6 copy-done.4
  73.8 0.1 copy-done.6
  73.9 2.1 %shard_map.77 = f32[1,2048]{1,0:T(1,128)} custom-call(s32[5]{0:T(128)} %copy-done.9, s32[5,8,2048]{2,1,0:T(8,128)} %copy-done, f32[8,2048]{1,0:T(8,128)} %copy-done.8, f32[1,2048]{1,0:T(1,128)} %copy-done.21, f32[296,128]{1,0:T(8,128)} %copy-done.2, f32[296,128]{1,0:T(8,128)} %copy-done.4, f32[296,128]{1,0:T(8,128)} %copy-done.6), custom_call_target="tpu_custom_call" | custom-call | tf_op jit(solution)/shard_map/pallas_call | solution.py:595
  75.9 1.5 %collective-permute-start.8 = (f32[1,2048]{1,0:T(1,128)}, f32[1,2048]{1,0:T(1,128)S(1)}, u32[]{:S(2)}, u32[]{:S(2)}) collective-permute-start(f32[1,2048]{1,0:T(1,128)} %shard_map.77), channel_id=1, source_target_pairs={{0,2},{1,3},{2,0},{3,1},{4,6},{5,7},{6,4},{7,5},{8,10},{9,11},{10,... | collective-permute-start | bytes 24584 | tf_op jit(solution)/shard_map/ppermute | solution.py:608
  77.4 1.1 collective-permute-start.9
  78.6 1.0 slice.54
  79.6 0.2 collective-permute-done.8
  79.8 2.5 %collective-permute-start.10 = (f32[48,2048]{1,0:T(8,128)S(1)}, f32[48,2048]{1,0:T(8,128)S(1)}, u32[]{:S(2)}, u32[]{:S(2)}) collective-permute-start(f32[48,2048]{1,0:T(8,128)S(1)} %slice.54), channel_id=1, source_target_pairs={{0,4},{1,13},{4,8},{5,1},{8,12},{9,5},{12,0},{13,9},{2,6},{3,15},{... | collective-permute-start | bytes 1179656 | tf_op jit(solution)/shard_map/ppermute | solution.py:549
  82.3 0.7 add_add_fusion.slope_ref
  83.0 1.0 copy-done.1
  84.0 0.9 copy-done.3
  84.9 0.9 copy-done.5
  85.8 0.9 copy-done.7
  86.7 0.7 copy-done.10
  87.4 4.8 %shard_map.78 = (f32[288,2048]{1,0:T(8,128)S(1)}, f32[4,16,128]{2,1,0:T(8,128)S(1)}) custom-call(s32[5]{0:T(128)S(1)} %copy-done.10, s32[5,8,2048]{2,1,0:T(8,128)S(1)} %copy-done.1, f32[2,2048]{1,0:T(2,128)S(1)} %copy-done.18, f32[1,2048]{1,0:T(1,128)S(1)} %add_add_fusion.slope_ref, f32[288,16]{1,0:T(8,128)S(1)} %bitcast.115, f32[288,2048]{1,0:T(8,128)} %bitcast.127, ...), custom_call_target="tpu_custom_call" | custom-call | flops 8192000 | bytes 1966080 | tf_op jit(solution)/shard_map/pallas_call | solution.py:631
  92.2 4.7 %shard_map.79 = (f32[288,2048]{1,0:T(8,128)S(1)}, f32[4,16,128]{2,1,0:T(8,128)S(1)}) custom-call(s32[5]{0:T(128)S(1)} %copy-done.10, s32[5,8,2048]{2,1,0:T(8,128)S(1)} %copy-done.1, f32[2,2048]{1,0:T(2,128)S(1)} %copy-done.18, f32[1,2048]{1,0:T(1,128)S(1)} %add_add_fusion.slope_ref, f32[288,16]{1,0:T(8,128)S(1)} %bitcast.116, ...), custom_call_target="tpu_custom_call", output_to_operand_aliasing={{0}: (10, {})} | custom-call | flops 8192000 | bytes 1966080 | tf_op jit(solution)/shard_map/pallas_call | solution.py:631
  97.0 3.7 %shard_map.80 = (f32[288,2048]{1,0:T(8,128)S(1)}, f32[4,16,128]{2,1,0:T(8,128)S(1)}) custom-call(s32[5]{0:T(128)S(1)} %copy-done.10, s32[5,8,2048]{2,1,0:T(8,128)S(1)} %copy-done.1, f32[2,2048]{1,0:T(2,128)S(1)} %copy-done.18, f32[1,2048]{1,0:T(1,128)S(1)} %add_add_fusion.slope_ref, f32[288,16]{1,0:T(8,128)S(1)} %bitcast.117, ...), custom_call_target="tpu_custom_call", output_to_operand_aliasing={{0}: (10, {})} | custom-call | flops 8192000 | bytes 1966080 | tf_op jit(solution)/shard_map/pallas_call | solution.py:631
  100.7 2.5 %shard_map.81 = (f32[288,2048]{1,0:T(8,128)S(1)}, f32[2,16,128]{2,1,0:T(8,128)S(1)}, f32[2,16,128]{2,1,0:T(8,128)S(1)}) custom-call(s32[5]{0:T(128)S(1)} %copy-done.10, s32[5,8,2048]{2,1,0:T(8,128)S(1)} %copy-done.1, f32[2,2048]{1,0:T(2,128)S(1)} %copy-done.18, f32[1,2048]{1,0:T(1,128)S(1)} %add_add_fusion.slope_ref, ...), custom_call_target="tpu_custom_call", output_to_operand_aliasing={{0}: (10, {})} | custom-call | flops 4915200 | bytes 1179648 | tf_op jit(solution)/shard_map/pallas_call | solution.py:631
  103.2 1.8 %collective-permute-start.14 = (f32[2,16,128]{2,1,0:T(8,128)S(1)}, f32[2,16,128]{2,1,0:T(8,128)S(1)}, u32[]{:S(2)}, u32[]{:S(2)}) collective-permute-start(f32[2,16,128]{2,1,0:T(8,128)S(1)} %get-tuple-element.61), channel_id=1, source_target_pairs={{0,1},{1,0},{2,3},{3,2},{4,5},{5,4},{6,7},{7,6},{8,9},{9,8},{10,11... | collective-permute-start | bytes 49160 | tf_op jit(solution)/shard_map/ppermute | solution.py:650
  104.9 0.8 collective-permute-done.14
  105.8 0.6 collective-permute-start.15
  106.4 0.1 reduce_sum.85
  106.6 0.6 reduce_max.9
  107.2 1.5 %collective-permute-start.2 = (f32[1,1]{1,0:T(1,128)}, f32[1,1]{1,0:T(1,128)}, u32[]{:S(2)}, u32[]{:S(2)}) collective-permute-start(f32[1,1]{1,0:T(1,128)} %bitcast.53), channel_id=1, source_target_pairs={{0,16},{16,0},{1,17},{17,1},{2,18},{18,2},{3,19},{19,3},{4,20},{20... | collective-permute-start | bytes 20 | tf_op jit(solution)/shard_map/ppermute | solution.py:589
  108.7 0.8 collective-permute-done.15
  109.5 2.0 %collective-permute-start.17 = (f32[2,16,128]{2,1,0:T(8,128)S(1)}, f32[2,16,128]{2,1,0:T(8,128)S(1)}, u32[]{:S(2)}, u32[]{:S(2)}) collective-permute-start(f32[2,16,128]{2,1,0:T(8,128)S(1)} %add.598.refs_0_), channel_id=1, source_target_pairs={{0,8},{4,12},{8,0},{12,4},{1,9},{5,13},{9,1},{13,5},{2,10},{6,14},... | collective-permute-start | bytes 49160 | tf_op jit(solution)/shard_map/ppermute | solution.py:657
  111.6 2.3 %collective-permute-start.18 = (f32[2,16,128]{2,1,0:T(8,128)S(1)}, f32[2,16,128]{2,1,0:T(8,128)S(1)}, u32[]{:S(2)}, u32[]{:S(2)}) collective-permute-start(f32[2,16,128]{2,1,0:T(8,128)S(1)} %add.598.refs_0_), channel_id=1, source_target_pairs={{0,12},{4,8},{8,4},{12,0},{1,13},{5,9},{9,5},{13,1},{2,14},{6,10},... | collective-permute-start | bytes 49160 | tf_op jit(solution)/shard_map/ppermute | solution.py:657
  115.2 1.9 %collective-permute-done.18.refs_3_ = f32[2,16,128]{2,1,0:T(8,128)S(1)} collective-permute-done((f32[2,16,128]{2,1,0:T(8,128)S(1)}, f32[2,16,128]{2,1,0:T(8,128)S(1)}, u32[]{:S(2)}, u32[]{:S(2)}) %collective-permute-start.18) | collective-permute-done | bytes 16416 | tf_op jit(solution)/shard_map/ppermute | solution.py:657
  117.1 1.2 %shard_map.82 = (f32[1,1024]{1,0:T(1,128)}, f32[1,1024]{1,0:T(1,128)}) custom-call(s32[1,1024]{1,0:T(1,128)S(1)} %bitcast.120, s32[1,1024]{1,0:T(1,128)S(1)} %bitcast.119, f32[2,16,128]{2,1,0:T(8,128)S(1)} %add.598.refs_0_, f32[2,16,128]{2,1,0:T(8,128)S(1)} %collective-permute-done.16.refs_1_, f32[2,16,128]{2,1,0:T(8,128)S(1)} %collective-permute-done.17.refs_2_, ...), custom_call_target="tpu_custom_call" | custom-call | flops 100663296 | bytes 65536 | tf_op jit(solution)/shard_map/pallas_call | solution.py:666
  (82 shorter events, 1.1 us)
Async XLA Ops:
  0.6 82.4 %copy-start.18 = (f32[2,2048]{1,0:T(2,128)S(1)}, f32[2,2048]{1,0:T(2,128)}, u32[]{:S(2)}) copy-start(f32[2,2048]{1,0:T(2,128)} %wind_ref.7) | copy-start | bytes 49156
  2.4 70.8 %copy-start.9 = (s32[5]{0:T(128)}, s32[5]{0:T(128)S(1)}, u32[]{:S(2)}) copy-start(s32[5]{0:T(128)S(1)} %stack.40.par_ref) | copy-start | bytes 64
  11.4 0.7 copy-start
  12.1 61.0 %copy-start.8 = (f32[8,2048]{1,0:T(8,128)}, f32[8,2048]{1,0:T(8,128)S(1)}, u32[]{:S(2)}) copy-start(f32[8,2048]{1,0:T(8,128)S(1)} %get-tuple-element.48.sum_ref) | copy-start | bytes 196612
  12.1 53.0 %collective-permute-start.4 = (f32[296,128]{1,0:T(8,128)S(1)}, f32[296,128]{1,0:T(8,128)S(1)}, u32[]{:S(2)}, u32[]{:S(2)}) collective-permute-start(f32[296,128]{1,0:T(8,128)S(1)} %get-tuple-element.49), channel_id=1, source_target_pairs={{0,4},{4,8},{8,12},{12,0},{1,5},{5,9},{9,13},{13,1},{2,6},{6,10},{... | collective-permute-start | bytes 454664 | tf_op jit(solution)/shard_map/ppermute | solution.py:580
  17.1 65.9 %collective-permute-start.13 = (f32[80,2048]{1,0:T(8,128)}, f32[80,2048]{1,0:T(8,128)S(1)}, u32[]{:S(2)}, u32[]{:S(2)}) collective-permute-start(f32[80,2048]{1,0:T(8,128)} %bitcast.56), channel_id=1, source_target_pairs={{0,4},{1,13},{4,8},{5,1},{8,12},{9,5},{12,0},{13,9},{2,6},{3,15},{... | collective-permute-start | bytes 1966088 | tf_op jit(solution)/shard_map/ppermute | solution.py:549
  21.2 71.0 %collective-permute-start.12 = (f32[80,2048]{1,0:T(8,128)}, f32[80,2048]{1,0:T(8,128)S(1)}, u32[]{:S(2)}, u32[]{:S(2)}) collective-permute-start(f32[80,2048]{1,0:T(8,128)} %get-tuple-element.191), channel_id=1, source_target_pairs={{0,4},{1,13},{4,8},{5,1},{8,12},{9,5},{12,0},{13,9},{2,6},{3,15},{... | collective-permute-start | bytes 1966088 | tf_op jit(solution)/shard_map/ppermute | solution.py:549
  22.7 74.2 %collective-permute-start.11 = (f32[80,2048]{1,0:T(8,128)}, f32[80,2048]{1,0:T(8,128)S(1)}, u32[]{:S(2)}, u32[]{:S(2)}) collective-permute-start(f32[80,2048]{1,0:T(8,128)} %get-tuple-element.192), channel_id=1, source_target_pairs={{0,4},{1,13},{4,8},{5,1},{8,12},{9,5},{12,0},{13,9},{2,6},{3,15},{... | collective-permute-start | bytes 1966088 | tf_op jit(solution)/shard_map/ppermute | solution.py:549
  22.8 41.0 %collective-permute-start.3 = (f32[1,2048]{1,0:T(1,128)S(1)}, f32[1,2048]{1,0:T(1,128)S(1)}, u32[]{:S(2)}, u32[]{:S(2)}) collective-permute-start(f32[1,2048]{1,0:T(1,128)S(1)} %slice.53), channel_id=1, source_target_pairs={{0,4},{1,13},{4,8},{5,1},{8,12},{9,5},{12,0},{13,9},{2,6},{3,15},{... | collective-permute-start | bytes 24584 | tf_op jit(solution)/shard_map/ppermute | solution.py:549
  63.8 9.3 %copy-start.21 = (f32[1,2048]{1,0:T(1,128)}, f32[1,2048]{1,0:T(1,128)S(1)}, u32[]{:S(2)}) copy-start(f32[1,2048]{1,0:T(1,128)S(1)} %collective-permute-done.3.beside_ref) | copy-start | bytes 24580
  63.8 9.3 %collective-permute-start.5 = (f32[296,128]{1,0:T(8,128)S(1)}, f32[296,128]{1,0:T(8,128)S(1)}, u32[]{:S(2)}, u32[]{:S(2)}) collective-permute-start(f32[296,128]{1,0:T(8,128)S(1)} %get-tuple-element.50), channel_id=1, source_target_pairs={{0,8},{4,12},{8,0},{12,4},{1,9},{5,13},{9,1},{13,5},{2,10},{6,14},... | collective-permute-start | bytes 454664 | tf_op jit(solution)/shard_map/ppermute | solution.py:580
  65.1 8.0 %copy-start.2 = (f32[296,128]{1,0:T(8,128)}, f32[296,128]{1,0:T(8,128)S(1)}, u32[]{:S(2)}) copy-start(f32[296,128]{1,0:T(8,128)S(1)} %collective-permute-done.4.refs_0_) | copy-start | bytes 454660
  65.1 8.0 %collective-permute-start.6 = (f32[296,128]{1,0:T(8,128)S(1)}, f32[296,128]{1,0:T(8,128)S(1)}, u32[]{:S(2)}, u32[]{:S(2)}) collective-permute-start(f32[296,128]{1,0:T(8,128)S(1)} %get-tuple-element.51), channel_id=1, source_target_pairs={{0,12},{4,0},{8,4},{12,8},{1,13},{5,1},{9,5},{13,9},{2,14},{6,2},{... | collective-permute-start | bytes 454664 | tf_op jit(solution)/shard_map/ppermute | solution.py:580
  73.1 0.7 copy-start.4
  73.1 0.7 copy-start.6
  75.9 1.5 %collective-permute-start.7 = (f32[1,2048]{1,0:T(1,128)}, f32[1,2048]{1,0:T(1,128)S(1)}, u32[]{:S(2)}, u32[]{:S(2)}) collective-permute-start(f32[1,2048]{1,0:T(1,128)} %shard_map.77), channel_id=1, source_target_pairs={{0,1},{1,0},{2,3},{3,2},{4,5},{5,4},{6,7},{7,6},{8,9},{9,8},{10,11... | collective-permute-start | bytes 24584 | tf_op jit(solution)/shard_map/ppermute | solution.py:608
  75.9 3.9 %collective-permute-start.8 = (f32[1,2048]{1,0:T(1,128)}, f32[1,2048]{1,0:T(1,128)S(1)}, u32[]{:S(2)}, u32[]{:S(2)}) collective-permute-start(f32[1,2048]{1,0:T(1,128)} %shard_map.77), channel_id=1, source_target_pairs={{0,2},{1,3},{2,0},{3,1},{4,6},{5,7},{6,4},{7,5},{8,10},{9,11},{10,... | collective-permute-start | bytes 24584 | tf_op jit(solution)/shard_map/ppermute | solution.py:608
  77.4 4.9 %collective-permute-start.9 = (f32[1,2048]{1,0:T(1,128)}, f32[1,2048]{1,0:T(1,128)S(1)}, u32[]{:S(2)}, u32[]{:S(2)}) collective-permute-start(f32[1,2048]{1,0:T(1,128)} %shard_map.77), channel_id=1, source_target_pairs={{0,3},{1,2},{2,1},{3,0},{4,7},{5,6},{6,5},{7,4},{8,11},{9,10},{10,... | collective-permute-start | bytes 24584 | tf_op jit(solution)/shard_map/ppermute | solution.py:608
  79.8 20.9 %collective-permute-start.10 = (f32[48,2048]{1,0:T(8,128)S(1)}, f32[48,2048]{1,0:T(8,128)S(1)}, u32[]{:S(2)}, u32[]{:S(2)}) collective-permute-start(f32[48,2048]{1,0:T(8,128)S(1)} %slice.54), channel_id=1, source_target_pairs={{0,4},{1,13},{4,8},{5,1},{8,12},{9,5},{12,0},{13,9},{2,6},{3,15},{... | collective-permute-start | bytes 1179656 | tf_op jit(solution)/shard_map/ppermute | solution.py:549
  83.0 1.0 copy-start.1
  84.0 0.9 copy-start.3
  84.9 0.9 copy-start.5
  85.8 0.9 copy-start.7
  86.7 0.7 copy-start.10
  87.4 9.6 %copy-start.12 = (f32[16,18,2048]{2,0,1:T(8,128)S(1)}, f32[16,18,2048]{2,0,1:T(8,128)}, u32[]{:S(2)}) copy-start(f32[16,18,2048]{2,0,1:T(8,128)} %param.9) | copy-start | bytes 7077892
  92.2 21.8 %copy-start.19 = (s32[1024]{0:T(1024)S(1)}, s32[1024]{0:T(1024)}, u32[]{:S(2)}) copy-start(s32[1024]{0:T(1024)} %param.13) | copy-start | bytes 12292
  92.2 21.7 %copy-start.20 = (s32[1024]{0:T(1024)S(1)}, s32[1024]{0:T(1024)}, u32[]{:S(2)}) copy-start(s32[1024]{0:T(1024)} %param.12) | copy-start | bytes 12292
  92.2 26.2 %copy-start.17 = (s32[128,128]{1,0:T(8,128)S(1)}, s32[128,128]{1,0:T(8,128)}, u32[]{:S(2)}) copy-start(s32[128,128]{1,0:T(8,128)} %cell_ref.1) | copy-start | bytes 196612
  96.9 21.4 %copy-start.13 = (f32[16,18,2048]{2,0,1:T(8,128)S(1)}, f32[16,18,2048]{2,0,1:T(8,128)}, u32[]{:S(2)}) copy-start(f32[16,18,2048]{2,0,1:T(8,128)} %param.9) | copy-start | bytes 7077892
  103.1 2.6 %copy-start.15 = (f32[288,2048]{1,0:T(8,128)}, f32[288,2048]{1,0:T(8,128)S(1)}, u32[]{:S(2)}) copy-start(f32[288,2048]{1,0:T(8,128)S(1)} %get-tuple-element.59) | copy-start | bytes 7077892
  103.2 2.6 %collective-permute-start.14 = (f32[2,16,128]{2,1,0:T(8,128)S(1)}, f32[2,16,128]{2,1,0:T(8,128)S(1)}, u32[]{:S(2)}, u32[]{:S(2)}) collective-permute-start(f32[2,16,128]{2,1,0:T(8,128)S(1)} %get-tuple-element.61), channel_id=1, source_target_pairs={{0,1},{1,0},{2,3},{3,2},{4,5},{5,4},{6,7},{7,6},{8,9},{9,8},{10,11... | collective-permute-start | bytes 49160 | tf_op jit(solution)/shard_map/ppermute | solution.py:650
  105.8 3.7 %collective-permute-start.15 = (f32[2,16,128]{2,1,0:T(8,128)S(1)}, f32[2,16,128]{2,1,0:T(8,128)S(1)}, u32[]{:S(2)}, u32[]{:S(2)}) collective-permute-start(f32[2,16,128]{2,1,0:T(8,128)S(1)} %add.597), channel_id=1, source_target_pairs={{0,2},{2,0},{1,3},{3,1},{4,6},{6,4},{5,7},{7,5},{8,10},{10,8},{9,1... | collective-permute-start | bytes 49160 | tf_op jit(solution)/shard_map/ppermute | solution.py:652
  107.2 6.8 %collective-permute-start.2 = (f32[1,1]{1,0:T(1,128)}, f32[1,1]{1,0:T(1,128)}, u32[]{:S(2)}, u32[]{:S(2)}) collective-permute-start(f32[1,1]{1,0:T(1,128)} %bitcast.53), channel_id=1, source_target_pairs={{0,16},{16,0},{1,17},{17,1},{2,18},{18,2},{3,19},{19,3},{4,20},{20... | collective-permute-start | bytes 20 | tf_op jit(solution)/shard_map/ppermute | solution.py:589
  109.5 5.7 %collective-permute-start.16 = (f32[2,16,128]{2,1,0:T(8,128)S(1)}, f32[2,16,128]{2,1,0:T(8,128)S(1)}, u32[]{:S(2)}, u32[]{:S(2)}) collective-permute-start(f32[2,16,128]{2,1,0:T(8,128)S(1)} %add.598.refs_0_), channel_id=1, source_target_pairs={{0,4},{4,0},{8,12},{12,8},{1,5},{5,1},{9,13},{13,9},{2,6},{6,2},{1... | collective-permute-start | bytes 49160 | tf_op jit(solution)/shard_map/ppermute | solution.py:657
  109.5 5.7 %collective-permute-start.17 = (f32[2,16,128]{2,1,0:T(8,128)S(1)}, f32[2,16,128]{2,1,0:T(8,128)S(1)}, u32[]{:S(2)}, u32[]{:S(2)}) collective-permute-start(f32[2,16,128]{2,1,0:T(8,128)S(1)} %add.598.refs_0_), channel_id=1, source_target_pairs={{0,8},{4,12},{8,0},{12,4},{1,9},{5,13},{9,1},{13,5},{2,10},{6,14},... | collective-permute-start | bytes 49160 | tf_op jit(solution)/shard_map/ppermute | solution.py:657
  111.6 5.5 %collective-permute-start.18 = (f32[2,16,128]{2,1,0:T(8,128)S(1)}, f32[2,16,128]{2,1,0:T(8,128)S(1)}, u32[]{:S(2)}, u32[]{:S(2)}) collective-permute-start(f32[2,16,128]{2,1,0:T(8,128)S(1)} %add.598.refs_0_), channel_id=1, source_target_pairs={{0,12},{4,8},{8,4},{12,0},{1,13},{5,9},{9,5},{13,1},{2,14},{6,10},... | collective-permute-start | bytes 49160 | tf_op jit(solution)/shard_map/ppermute | solution.py:657

commit v3 on v2

--- a/solution.py
+++ b/solution.py
@@ -167,7 +167,8 @@
 
 C_KEEP, C_ROW, C_COL, C_SLOPE, C_EAST, C_NORTH, C_ONE, C_DAMP = range(8)
 C_S_EAST, C_S_NORTH, C_T_EAST, C_T_NORTH = range(8, 12)
-CHUNK_ENDS = (5, 10, 15)
+CHUNK_ENDS = (4, 8, 13, 16)
+VMEM_BYTES = 40 * 1024 * 1024
 
 
 def split3(value):
@@ -343,7 +344,7 @@
     turn = par_ref[3]
     beside_lanes, beyond = turned_lanes(turn)
     every = slice(0, 8)
-    lists = [ref[...] for ref in list_refs]
+    lists = [ref[-8:, :] for ref in list_refs]
     for block in range(sum_ref.shape[1] // LANES):
         at = slice(block * LANES, (block + 1) * LANES)
         own = sum_ref[:, at]
@@ -383,8 +384,11 @@
         slope = slope_ref[...]
         damp_ref[...] = jnp.broadcast_to(slope * slope, damp_ref.shape)
 
-    for tile in range(g_ref.shape[0] // 8):
-        rows = slice(tile * 8, tile * 8 + 8)
+    for tile in range(out_ref.shape[0] // 8):
+        here = slice(tile * 8, tile * 8 + 8)
+        first = pl.program_id(0) * out_ref.shape[0] + tile * 8
+        near_rows = pl.ds(pl.multiple_of(first, 8), 8)
+        rows = pl.ds(pl.multiple_of(first + first_step * out_ref.shape[0], 8), 8)
         coef = coef_ref[rows, :]
 
         def factor(at):
@@ -404,8 +408,8 @@
             row_value = row_neighbour(shape, code, lanes, own, near, lists)
             col_value = jnp.where(
                 beyond,
-                lane_take(near_block(beside_ref, rows, block, turn), beside_lanes),
-                lane_take(beside_ref[rows, at], beside_lanes),
+                lane_take(near_block(beside_ref, near_rows, block, turn), beside_lanes),
+                lane_take(beside_ref[near_rows, at], beside_lanes),
             )
             col_value = jnp.where(has_beside > 0, col_value, 0.0)
             value = keep * own + by_row * row_value + by_col * col_value
@@ -413,7 +417,7 @@
             wind_north = jnp.broadcast_to(wind_ref[1:2, at], shape)
             growth = jnp.maximum(east * wind_east + north * wind_north - one, 0.0)
             updated = value * jnp.exp(growth - damp * damp_ref[:, at])
-            out_ref[rows, at] = updated
+            out_ref[here, at] = updated
             lifted = growth * value
             total_ref[0, :, at] += s_east * lifted
             total_ref[1, :, at] += s_north * lifted
@@ -506,7 +510,7 @@
         out_specs=[WHOLE] * len(outputs),
         out_shape=outputs,
         scratch_shapes=list(scratch),
-        compiler_params=pltpu.CompilerParams(vmem_limit_bytes=48 * 1024 * 1024),
+        compiler_params=pltpu.CompilerParams(vmem_limit_bytes=VMEM_BYTES),
         cost_estimate=pl.CostEstimate(flops=flops, bytes_accessed=moved, transcendentals=0),
     )
 
@@ -575,14 +579,19 @@
         flops=6 * rows * slots * LANES * owners,
         moved=rows * slots * 4,
     )(par, cell_sea, coef, field)
-    (idx, counts, row_sums), lists = found[:3], found[3:]
+    (idx, counts, row_sums), *lists = lax.optimization_barrier((found[:3], *found[3:], beside[0]))
+    beside = [lists.pop()]
     arrived = [
         lax.ppermute(values, "pts", [(i, (i + 1 + away) % owners) for i in range(owners)])
         for away, values in enumerate(lists)
     ]
     beside_sums = around(row_sums[3:4])
-    later, *_ = lax.optimization_barrier((field, *lists))
-    beside += [around(chunk(later, at)) for at in chunks[1:]]
+    second = chunk(field, chunks[1])
+    second, *_ = lax.optimization_barrier((second, *lists))
+    beside.append(around(second))
+    later = [chunk(field, at) for at in chunks[2:]]
+    later, arrived, beside_sums = lax.optimization_barrier((later, arrived, beside_sums))
+    beside += [around(values) for values in later]
 
     longest = jnp.max(jnp.sum(counts, axis=1)).reshape(1, 1)
     if groups == 2:
@@ -590,14 +599,10 @@
     else:
         longest = lax.pmax(longest, "grp")
 
-    tail_block = pl.BlockSpec((8, LANES), lambda i: (rows // 8, 0))
-    whole = lambda *dims: pl.BlockSpec(dims, lambda i: (0,) * len(dims))
     slope_part = pl.pallas_call(
         slope_kernel,
-        grid=(1,),
-        in_specs=[SCALARS, whole(5, 8, slots), whole(8, slots), whole(1, slots)]
-        + [tail_block] * (owners - 1),
-        out_specs=whole(1, slots),
+        in_specs=[SCALARS, WHOLE, WHOLE, WHOLE] + [WHOLE] * (owners - 1),
+        out_specs=WHOLE,
         out_shape=shape_of(1, slots),
     )(par, idx, row_sums, beside_sums, *arrived)
 
@@ -611,6 +616,7 @@
     else:
         slope = lax.psum(slope_part, ("spec", "cpl"))
 
+    slope, longest = lax.optimization_barrier((slope, longest))
     updated = sums = None
     for at, near in zip(chunks, beside):
         start, stop = at
@@ -619,24 +625,22 @@
             (step_rows, width), functools.partial(lambda first, i: (first + i, 0), start)
         )
         inputs = [par, idx, wind_deck, slope, coef, field, near, *arrived]
-        specs = [SCALARS, whole(5, 8, slots), whole(2, slots), whole(1, slots), in_rows(16)]
-        specs += [in_rows(slots), pl.BlockSpec((step_rows, slots), lambda i: (i, 0))]
-        specs += [in_rows(LANES)] * (owners - 1)
+        specs = [SCALARS] + [WHOLE] * (owners + 5)
         aliases = {}
         if chained:
             aliases = {len(inputs): 0}
             inputs += [updated, sums]
-            specs += [pl.BlockSpec(memory_space=pl.ANY), whole(4, blocks, LANES)]
+            specs += [pl.BlockSpec(memory_space=pl.ANY), WHOLE]
         sum_shapes = [(2, blocks, LANES)] * 2 if final else [(4, blocks, LANES)]
         updated, *sums = pl.pallas_call(
             functools.partial(step_kernel, owners, start, steps // 2, chained, final),
             grid=(stop - start,),
             in_specs=specs,
-            out_specs=[in_rows(slots)] + [whole(*dims) for dims in sum_shapes],
-            out_shape=[shape_of(rows, slots)] + [shape_of(*dims) for dims in sum_shapes],
+            out_specs=[in_rows(slots)] + [WHOLE] * len(sum_shapes),
+            out_shape=[pltpu.HBM((rows, slots), F32)] + [shape_of(*dims) for dims in sum_shapes],
             scratch_shapes=[pltpu.VMEM((4, 8, slots), F32), pltpu.VMEM((8, slots), F32)],
             input_output_aliases=aliases,
-            compiler_params=pltpu.CompilerParams(vmem_limit_bytes=24 * 1024 * 1024),
+            compiler_params=pltpu.CompilerParams(vmem_limit_bytes=VMEM_BYTES),
             cost_estimate=pl.CostEstimate(
                 flops=(stop - start) * step_rows * slots * 50,
                 bytes_accessed=(stop - start) * step_rows * slots * 12,

time: 119 us -> 98.8 us (0.83)
  waiting for transfers between devices: 49.6 us -> 23.4 us
  Pallas kernels: 28 us -> 35.5 us
  starting transfers between devices: 24.2 us -> 23 us
    ppermute x5 -> x6, waiting for transfers between devices: 39.2 us -> 12.5 us  [around(): return lax.ppermute(values, ('pts', 'cpl'), ring)]
    pallas_call x4 -> x5, Pallas kernels: 15.6 us -> 23 us  [local(): pl.pallas_call(functools.partial(step_kernel, owners, start, steps // 2,...]
    ppermute x3, waiting for transfers between devices: 6.63 us -> 0.01 us  [local(): lax.ppermute(values, 'pts', [(i, (i + 1 + away) % owners) for i in range(...]
    ppermute x3, waiting for transfers between devices: 1.88 us -> 5.19 us  [local(): lax.ppermute(mine, 'pts', [(i, i ^ turned) for i in range(owners)])]
    ppermute x1, waiting for transfers between devices: 0.01 us -> 2.11 us  [local(): lax.ppermute(longest, 'grp', [(0, 1), (1, 0)])]
    ppermute x5 -> x6, starting transfers between devices: 7.49 us -> 9.44 us  [around(): return lax.ppermute(values, ('pts', 'cpl'), ring)]
    ppermute x1, starting transfers between devices: 1.79 us -> 0.01 us  [local(): mine = mine + lax.ppermute(others, 'cpl', [(0, 1), (1, 0)])]
    ppermute x1, waiting for transfers between devices: 0.84 us -> 2.25 us  [local(): mine = mine + lax.ppermute(mine, 'spec', [(0, 1), (1, 0)])]
  transfers between devices with their start and end apart: 17 -> 18, of which waited for: 6 -> 9; matrix products, arithmetic and copies ran while one was open for 6% -> 7% of each run, Pallas kernels for 13% -> 31%
where the time goes in v3:
time: 98.8 us; the launch traced here: 98.1 us
  Pallas kernels  35.5 us (36%)
  waiting for transfers between devices  23.4 us (24%)
  starting transfers between devices  23 us (23%)
  local copies, waits for them, and re-layouts  12.4 us (13%)
  between operations  2.2 us (2%)
  other arithmetic  1.64 us (2%)
    pallas_call x5, Pallas kernels, local(): pl.pallas_call(functools.partial(step_kernel, owners, start, steps // 2,...  23 us
    ppermute x6, waiting for transfers between devices, around(): return lax.ppermute(values, ('pts', 'cpl'), ring)  12.5 us
    ppermute x6, starting transfers between devices, around(): return lax.ppermute(values, ('pts', 'cpl'), ring)  9.44 us
    pallas_call x1, Pallas kernels, local(): call(functools.partial(index_kernel, owners), [SCALARS, WHOLE, WHOLE, WHO...  9.02 us
    slice x4, local copies, waits for them, and re-layouts, chunk(): return values[at[0] * step_rows:at[1] * step_rows]  5.91 us
    unnamed x38, local copies, waits for them, and re-layouts  5.25 us
    ppermute x3, waiting for transfers between devices, local(): lax.ppermute(mine, 'pts', [(i, i ^ turned) for i in range(owners)])  5.19 us
    ppermute x3, starting transfers between devices, local(): lax.ppermute(values, 'pts', [(i, (i + 1 + away) % owners) for i in range(...  4.62 us
  transfers between devices with their start and end apart: 18, of which 9 were waited for; matrix products, arithmetic and copies ran while one was open for 7% of the time, Pallas kernels for 31%

profile of v3, /device:TPU:0, one launch (start us, length us, event | category | flops | bytes accessed | tf_op | source)
XLA Modules:
  0.0 98.1 jit_solution(1664384829370903987)
XLA Ops:
  0.6 2.1 %fusion.60 = (f32[4,16,2048]{2,1,0:T(8,128)}, f32[4,16,2048]{2,1,0:T(8,128)S(1)}) fusion(f32[18,16,2048]{2,1,0:T(8,128)} %bitcast.51), kind=kLoop, calls=%fused_computation.223 | loop fusion | bytes 2097152 | tf_op jit(solution)/shard_map/slice | solution.py:556
  2.7 3.0 %collective-permute-start.2 = (f32[64,2048]{1,0:T(8,128)S(1)}, f32[64,2048]{1,0:T(8,128)S(1)}, u32[]{:S(2)}, u32[]{:S(2)}) collective-permute-start(f32[64,2048]{1,0:T(8,128)S(1)} %bitcast.134), channel_id=1, source_target_pairs={{0,4},{1,13},{4,8},{5,1},{8,12},{9,5},{12,0},{13,9},{2,6},{3,15},{... | collective-permute-start | bytes 1572872 | tf_op jit(solution)/shard_map/ppermute | solution.py:553
  6.0 0.1 mul.605
  6.9 0.1 stack_broadcast_in_dim.53
  7.2 0.1 copy.40
  7.4 0.1 stack.40.par_ref
  7.4 9.0 %shard_map.76 = (s32[5,8,2048]{2,1,0:T(8,128)S(1)}, f32[16,128]{1,0:T(8,128)S(1)}, f32[8,2048]{1,0:T(8,128)S(1)}, f32[296,128]{1,0:T(8,128)S(1)}, f32[296,128]{1,0:T(8,128)S(1)}, /*index=5*/f32[296,128]{1,0:T(8,128)S(1)}) custom-call(s32[5]{0:T(128)S(1)} %stack.40.par_ref, s32[128,128]{1,0:T(8,128)} %cell_ref.1, f32[288,16]{1,0:T(8,128)S(1)} %bitcast.118, ...), custom_call_target="tpu_custom_call" | custom-call | flops 1811939328 | bytes 2359296 | tf_op jit(solution)/shard_map/pallas_call | solution.py:570
  16.5 0.7 copy-done
  17.2 2.6 %collective-permute-done.2.beside_ref = f32[64,2048]{1,0:T(8,128)S(1)} collective-permute-done((f32[64,2048]{1,0:T(8,128)S(1)}, f32[64,2048]{1,0:T(8,128)S(1)}, u32[]{:S(2)}, u32[]{:S(2)}) %collective-permute-start.2) | collective-permute-done | bytes 524320 | tf_op jit(solution)/shard_map/ppermute | solution.py:553
  19.9 3.3 %collective-permute-start.4 = (f32[296,128]{1,0:T(8,128)S(1)}, f32[296,128]{1,0:T(8,128)S(1)}, u32[]{:S(2)}, u32[]{:S(2)}) collective-permute-start(f32[296,128]{1,0:T(8,128)S(1)} %get-tuple-element.73), channel_id=1, source_target_pairs={{0,8},{4,12},{8,0},{12,4},{1,9},{5,13},{9,1},{13,5},{2,10},{6,14},... | collective-permute-start | bytes 454664 | tf_op jit(solution)/shard_map/ppermute | solution.py:585
  23.1 1.3 %collective-permute-start.5 = (f32[296,128]{1,0:T(8,128)S(1)}, f32[296,128]{1,0:T(8,128)S(1)}, u32[]{:S(2)}, u32[]{:S(2)}) collective-permute-start(f32[296,128]{1,0:T(8,128)S(1)} %get-tuple-element.74), channel_id=1, source_target_pairs={{0,12},{4,0},{8,4},{12,8},{1,13},{5,1},{9,5},{13,9},{2,14},{6,2},{... | collective-permute-start | bytes 454664 | tf_op jit(solution)/shard_map/ppermute | solution.py:585
  24.5 0.7 collective-permute-start.6
  25.2 1.1 %slice.149 = f32[5,16,2048]{2,1,0:T(8,128)S(1)} slice(f32[18,16,2048]{2,1,0:T(8,128)} %bitcast.51), slice={[8:13], [0:16], [0:2048]} | slice | bytes 1310720 | tf_op jit(solution)/shard_map/slice | solution.py:556
  26.4 1.0 %slice.150 = f32[3,16,2048]{2,1,0:T(8,128)S(1)} slice(f32[18,16,2048]{2,1,0:T(8,128)} %bitcast.51), slice={[13:16], [0:16], [0:2048]} | slice | bytes 786432 | tf_op jit(solution)/shard_map/slice | solution.py:556
  27.4 1.7 %slice.151 = f32[2,16,2048]{2,1,0:T(8,128)} slice(f32[18,16,2048]{2,1,0:T(8,128)} %bitcast.51), slice={[16:18], [0:16], [0:2048]} | slice | bytes 524288 | tf_op jit(solution)/shard_map/slice | solution.py:556
  29.1 4.2 %collective-permute-done.6.beside_ref = f32[1,2048]{1,0:T(1,128)S(1)} collective-permute-done((f32[1,2048]{1,0:T(1,128)S(1)}, f32[1,2048]{1,0:T(1,128)S(1)}, u32[]{:S(2)}, u32[]{:S(2)}) %collective-permute-start.6) | collective-permute-done | bytes 8224 | tf_op jit(solution)/shard_map/ppermute | solution.py:553
  33.3 3.6 %collective-permute-start.13 = (f32[80,2048]{1,0:T(8,128)S(1)}, f32[80,2048]{1,0:T(8,128)S(1)}, u32[]{:S(2)}, u32[]{:S(2)}) collective-permute-start(f32[80,2048]{1,0:T(8,128)S(1)} %bitcast.132), channel_id=1, source_target_pairs={{0,4},{1,13},{4,8},{5,1},{8,12},{9,5},{12,0},{13,9},{2,6},{3,15},{... | collective-permute-start | bytes 1966088 | tf_op jit(solution)/shard_map/ppermute | solution.py:553
  36.9 0.2 collective-permute-start.14
  37.1 0.1 reduce_sum.85
  37.3 2.2 %shard_map.77 = f32[1,2048]{1,0:T(1,128)} custom-call(s32[5]{0:T(128)} %copy-done.9, s32[5,8,2048]{2,1,0:T(8,128)} %copy-done, f32[8,2048]{1,0:T(8,128)} %copy-done.8, f32[1,2048]{1,0:T(1,128)} %copy-done.18, f32[296,128]{1,0:T(8,128)} %copy-done.2, f32[296,128]{1,0:T(8,128)} %copy-done.4, f32[296,128]{1,0:T(8,128)} %copy-done.6), custom_call_target="tpu_custom_call" | custom-call | tf_op jit(solution)/shard_map/pallas_call | solution.py:602
  39.5 0.6 reduce_max.9
  40.1 1.5 %collective-permute-start.8 = (f32[1,2048]{1,0:T(1,128)}, f32[1,2048]{1,0:T(1,128)S(1)}, u32[]{:S(2)}, u32[]{:S(2)}) collective-permute-start(f32[1,2048]{1,0:T(1,128)} %shard_map.77), channel_id=1, source_target_pairs={{0,2},{1,3},{2,0},{3,1},{4,6},{5,7},{6,4},{7,5},{8,10},{9,11},{10,... | collective-permute-start | bytes 24584 | tf_op jit(solution)/shard_map/ppermute | solution.py:613
  41.6 1.5 %collective-permute-start.10 = (f32[1,1]{1,0:T(1,128)}, f32[1,1]{1,0:T(1,128)}, u32[]{:S(2)}, u32[]{:S(2)}) collective-permute-start(f32[1,1]{1,0:T(1,128)} %bitcast.57), channel_id=1, source_target_pairs={{0,16},{16,0},{1,17},{17,1},{2,18},{18,2},{3,19},{19,3},{4,20},{20... | collective-permute-start | bytes 20 | tf_op jit(solution)/shard_map/ppermute | solution.py:598
  43.1 2.1 %collective-permute-done.10 = f32[1,1]{1,0:T(1,128)} collective-permute-done((f32[1,1]{1,0:T(1,128)}, f32[1,1]{1,0:T(1,128)}, u32[]{:S(2)}, u32[]{:S(2)}) %collective-permute-start.10) | collective-permute-done | bytes 36 | tf_op jit(solution)/shard_map/ppermute | solution.py:598
  46.5 1.4 %collective-permute-start.12 = (f32[48,2048]{1,0:T(8,128)S(1)}, f32[48,2048]{1,0:T(8,128)S(1)}, u32[]{:S(2)}, u32[]{:S(2)}) collective-permute-start(f32[48,2048]{1,0:T(8,128)S(1)} %bitcast.137), channel_id=1, source_target_pairs={{0,4},{1,13},{4,8},{5,1},{8,12},{9,5},{12,0},{13,9},{2,6},{3,15},{... | collective-permute-start | bytes 1179656 | tf_op jit(solution)/shard_map/ppermute | solution.py:553
  47.9 0.5 collective-permute-start.11
  48.4 0.2 collective-permute-done.9
  48.5 0.7 add_add_fusion.slope_ref
  49.3 1.0 copy-done.1
  50.2 0.9 copy-done.3
  51.1 0.9 copy-done.5
  52.1 0.9 copy-done.7
  53.0 0.6 copy-done.10
  53.6 4.8 %shard_map.78 = (f32[288,2048]{1,0:T(8,128)}, f32[4,16,128]{2,1,0:T(8,128)S(1)}) custom-call(s32[5]{0:T(128)S(1)} %copy-done.10, s32[5,8,2048]{2,1,0:T(8,128)S(1)} %copy-done.1, f32[2,2048]{1,0:T(2,128)S(1)} %copy-done.14, f32[1,2048]{1,0:T(1,128)S(1)} %add_add_fusion.slope_ref, f32[288,16]{1,0:T(8,128)S(1)} %bitcast.119, f32[288,2048]{1,0:T(8,128)} %bitcast.52.g_ref, ...), custom_call_target="tpu_custom_call" | custom-call | flops 6553600 | bytes 1572864 | tf_op jit(solution)/shard_map/pallas_call | solution.py:635
  58.4 5.7 %collective-permute-done.14.beside_ref = f32[64,2048]{1,0:T(8,128)S(1)} collective-permute-done((f32[64,2048]{1,0:T(8,128)}, f32[64,2048]{1,0:T(8,128)S(1)}, u32[]{:S(2)}, u32[]{:S(2)}) %collective-permute-start.14) | collective-permute-done | bytes 524320 | tf_op jit(solution)/shard_map/ppermute | solution.py:553
  64.1 4.8 %shard_map.79 = (f32[288,2048]{1,0:T(8,128)}, f32[4,16,128]{2,1,0:T(8,128)S(1)}) custom-call(s32[5]{0:T(128)S(1)} %copy-done.10, s32[5,8,2048]{2,1,0:T(8,128)S(1)} %copy-done.1, f32[2,2048]{1,0:T(2,128)S(1)} %copy-done.14, f32[1,2048]{1,0:T(1,128)S(1)} %add_add_fusion.slope_ref, f32[288,16]{1,0:T(8,128)S(1)} %bitcast.120, ...), custom_call_target="tpu_custom_call", output_to_operand_aliasing={{0}: (10, {})} | custom-call | flops 6553600 | bytes 1572864 | tf_op jit(solution)/shard_map/pallas_call | solution.py:635
  69.0 5.5 %shard_map.80 = (f32[288,2048]{1,0:T(8,128)}, f32[4,16,128]{2,1,0:T(8,128)S(1)}) custom-call(s32[5]{0:T(128)S(1)} %copy-done.10, s32[5,8,2048]{2,1,0:T(8,128)S(1)} %copy-done.1, f32[2,2048]{1,0:T(2,128)S(1)} %copy-done.14, f32[1,2048]{1,0:T(1,128)S(1)} %add_add_fusion.slope_ref, f32[288,16]{1,0:T(8,128)S(1)} %bitcast.121, ...), custom_call_target="tpu_custom_call", output_to_operand_aliasing={{0}: (10, {})} | custom-call | flops 8192000 | bytes 1966080 | tf_op jit(solution)/shard_map/pallas_call | solution.py:635
  74.5 4.2 %shard_map.81 = (f32[288,2048]{1,0:T(8,128)}, f32[4,16,128]{2,1,0:T(8,128)S(1)}) custom-call(s32[5]{0:T(128)S(1)} %copy-done.10, s32[5,8,2048]{2,1,0:T(8,128)S(1)} %copy-done.1, f32[2,2048]{1,0:T(2,128)S(1)} %copy-done.14, f32[1,2048]{1,0:T(1,128)S(1)} %add_add_fusion.slope_ref, f32[288,16]{1,0:T(8,128)S(1)} %bitcast.122, ...), custom_call_target="tpu_custom_call", output_to_operand_aliasing={{0}: (10, {})} | custom-call | flops 4915200 | bytes 1179648 | tf_op jit(solution)/shard_map/pallas_call | solution.py:635
  78.7 3.6 %shard_map.82 = (f32[288,2048]{1,0:T(8,128)}, f32[2,16,128]{2,1,0:T(8,128)S(1)}, f32[2,16,128]{2,1,0:T(8,128)S(1)}) custom-call(s32[5]{0:T(128)S(1)} %copy-done.10, s32[5,8,2048]{2,1,0:T(8,128)S(1)} %copy-done.1, f32[2,2048]{1,0:T(2,128)S(1)} %copy-done.14, f32[1,2048]{1,0:T(1,128)S(1)} %add_add_fusion.slope_ref, ...), custom_call_target="tpu_custom_call", output_to_operand_aliasing={{0}: (10, {})} | custom-call | flops 3276800 | bytes 786432 | tf_op jit(solution)/shard_map/pallas_call | solution.py:635
  82.4 1.2 %collective-permute-done.15 = f32[2,16,128]{2,1,0:T(8,128)S(1)} collective-permute-done((f32[2,16,128]{2,1,0:T(8,128)S(1)}, f32[2,16,128]{2,1,0:T(8,128)S(1)}, u32[]{:S(2)}, u32[]{:S(2)}) %collective-permute-start.15) | collective-permute-done | bytes 16416 | tf_op jit(solution)/shard_map/ppermute | solution.py:654
  83.5 1.5 %collective-permute-start.16 = (f32[2,16,128]{2,1,0:T(8,128)S(1)}, f32[2,16,128]{2,1,0:T(8,128)S(1)}, u32[]{:S(2)}, u32[]{:S(2)}) collective-permute-start(f32[2,16,128]{2,1,0:T(8,128)S(1)} %add.597), channel_id=1, source_target_pairs={{0,2},{2,0},{1,3},{3,1},{4,6},{6,4},{5,7},{7,5},{8,10},{10,8},{9,1... | collective-permute-start | bytes 49160 | tf_op jit(solution)/shard_map/ppermute | solution.py:656
  85.0 2.2 %collective-permute-done.16 = f32[2,16,128]{2,1,0:T(8,128)S(1)} collective-permute-done((f32[2,16,128]{2,1,0:T(8,128)S(1)}, f32[2,16,128]{2,1,0:T(8,128)S(1)}, u32[]{:S(2)}, u32[]{:S(2)}) %collective-permute-start.16) | collective-permute-done | bytes 16416 | tf_op jit(solution)/shard_map/ppermute | solution.py:656
  87.3 1.7 %collective-permute-start.17 = (f32[2,16,128]{2,1,0:T(8,128)S(1)}, f32[2,16,128]{2,1,0:T(8,128)S(1)}, u32[]{:S(2)}, u32[]{:S(2)}) collective-permute-start(f32[2,16,128]{2,1,0:T(8,128)S(1)} %add.598.refs_0_), channel_id=1, source_target_pairs={{0,4},{4,0},{8,12},{12,8},{1,5},{5,1},{9,13},{13,9},{2,6},{6,2},{1... | collective-permute-start | bytes 49160 | tf_op jit(solution)/shard_map/ppermute | solution.py:661
  89.0 2.4 %collective-permute-start.18 = (f32[2,16,128]{2,1,0:T(8,128)S(1)}, f32[2,16,128]{2,1,0:T(8,128)S(1)}, u32[]{:S(2)}, u32[]{:S(2)}) collective-permute-start(f32[2,16,128]{2,1,0:T(8,128)S(1)} %add.598.refs_0_), channel_id=1, source_target_pairs={{0,8},{4,12},{8,0},{12,4},{1,9},{5,13},{9,1},{13,5},{2,10},{6,14},... | collective-permute-start | bytes 49160 | tf_op jit(solution)/shard_map/ppermute | solution.py:661
  91.4 0.3 collective-permute-start.19
  91.7 1.9 %collective-permute-done.18.refs_2_ = f32[2,16,128]{2,1,0:T(8,128)S(1)} collective-permute-done((f32[2,16,128]{2,1,0:T(8,128)S(1)}, f32[2,16,128]{2,1,0:T(8,128)S(1)}, u32[]{:S(2)}, u32[]{:S(2)}) %collective-permute-start.18) | collective-permute-done | bytes 16416 | tf_op jit(solution)/shard_map/ppermute | solution.py:661
  93.6 3.3 %collective-permute-done.19.refs_3_ = f32[2,16,128]{2,1,0:T(8,128)S(1)} collective-permute-done((f32[2,16,128]{2,1,0:T(8,128)S(1)}, f32[2,16,128]{2,1,0:T(8,128)S(1)}, u32[]{:S(2)}, u32[]{:S(2)}) %collective-permute-start.19) | collective-permute-done | bytes 16416 | tf_op jit(solution)/shard_map/ppermute | solution.py:661
  96.9 1.2 %shard_map.83 = (f32[1,1024]{1,0:T(1,128)}, f32[1,1024]{1,0:T(1,128)}) custom-call(s32[1,1024]{1,0:T(1,128)S(1)} %bitcast.125, s32[1,1024]{1,0:T(1,128)S(1)} %bitcast.124, f32[2,16,128]{2,1,0:T(8,128)S(1)} %add.598.refs_0_, f32[2,16,128]{2,1,0:T(8,128)S(1)} %collective-permute-done.17.refs_1_, f32[2,16,128]{2,1,0:T(8,128)S(1)} %collective-permute-done.18.refs_2_, ...), custom_call_target="tpu_custom_call" | custom-call | flops 100663296 | bytes 65536 | tf_op jit(solution)/shard_map/pallas_call | solution.py:670
  (80 shorter events, 1.3 us)
Async XLA Ops:
  0.6 48.6 %copy-start.14 = (f32[2,2048]{1,0:T(2,128)S(1)}, f32[2,2048]{1,0:T(2,128)}, u32[]{:S(2)}) copy-start(f32[2,2048]{1,0:T(2,128)} %wind_ref.9) | copy-start | bytes 49156
  2.7 17.1 %collective-permute-start.2 = (f32[64,2048]{1,0:T(8,128)S(1)}, f32[64,2048]{1,0:T(8,128)S(1)}, u32[]{:S(2)}, u32[]{:S(2)}) collective-permute-start(f32[64,2048]{1,0:T(8,128)S(1)} %bitcast.134), channel_id=1, source_target_pairs={{0,4},{1,13},{4,8},{5,1},{8,12},{9,5},{12,0},{13,9},{2,6},{3,15},{... | collective-permute-start | bytes 1572872 | tf_op jit(solution)/shard_map/ppermute | solution.py:553
  7.4 29.8 %copy-start.9 = (s32[5]{0:T(128)}, s32[5]{0:T(128)S(1)}, u32[]{:S(2)}) copy-start(s32[5]{0:T(128)S(1)} %stack.40.par_ref) | copy-start | bytes 64
  16.5 0.7 copy-start
  17.2 20.0 %copy-start.8 = (f32[8,2048]{1,0:T(8,128)}, f32[8,2048]{1,0:T(8,128)S(1)}, u32[]{:S(2)}) copy-start(f32[8,2048]{1,0:T(8,128)S(1)} %get-tuple-element.71.sum_ref) | copy-start | bytes 196612
  19.9 13.4 %collective-permute-start.3 = (f32[296,128]{1,0:T(8,128)S(1)}, f32[296,128]{1,0:T(8,128)S(1)}, u32[]{:S(2)}, u32[]{:S(2)}) collective-permute-start(f32[296,128]{1,0:T(8,128)S(1)} %get-tuple-element.72), channel_id=1, source_target_pairs={{0,4},{4,8},{8,12},{12,0},{1,5},{5,9},{9,13},{13,1},{2,6},{6,10},{... | collective-permute-start | bytes 454664 | tf_op jit(solution)/shard_map/ppermute | solution.py:585
  19.9 13.4 %collective-permute-start.4 = (f32[296,128]{1,0:T(8,128)S(1)}, f32[296,128]{1,0:T(8,128)S(1)}, u32[]{:S(2)}, u32[]{:S(2)}) collective-permute-start(f32[296,128]{1,0:T(8,128)S(1)} %get-tuple-element.73), channel_id=1, source_target_pairs={{0,8},{4,12},{8,0},{12,4},{1,9},{5,13},{9,1},{13,5},{2,10},{6,14},... | collective-permute-start | bytes 454664 | tf_op jit(solution)/shard_map/ppermute | solution.py:585
  23.1 10.1 %collective-permute-start.5 = (f32[296,128]{1,0:T(8,128)S(1)}, f32[296,128]{1,0:T(8,128)S(1)}, u32[]{:S(2)}, u32[]{:S(2)}) collective-permute-start(f32[296,128]{1,0:T(8,128)S(1)} %get-tuple-element.74), channel_id=1, source_target_pairs={{0,12},{4,0},{8,4},{12,8},{1,13},{5,1},{9,5},{13,9},{2,14},{6,2},{... | collective-permute-start | bytes 454664 | tf_op jit(solution)/shard_map/ppermute | solution.py:585
  24.5 8.8 %collective-permute-start.6 = (f32[1,2048]{1,0:T(1,128)S(1)}, f32[1,2048]{1,0:T(1,128)S(1)}, u32[]{:S(2)}, u32[]{:S(2)}) collective-permute-start(f32[1,2048]{1,0:T(1,128)S(1)} %slice.76), channel_id=1, source_target_pairs={{0,4},{1,13},{4,8},{5,1},{8,12},{9,5},{12,0},{13,9},{2,6},{3,15},{... | collective-permute-start | bytes 24584 | tf_op jit(solution)/shard_map/ppermute | solution.py:553
  33.3 4.0 %copy-start.18 = (f32[1,2048]{1,0:T(1,128)}, f32[1,2048]{1,0:T(1,128)S(1)}, u32[]{:S(2)}) copy-start(f32[1,2048]{1,0:T(1,128)S(1)} %collective-permute-done.6.beside_ref) | copy-start | bytes 24580
  33.3 4.0 %copy-start.2 = (f32[296,128]{1,0:T(8,128)}, f32[296,128]{1,0:T(8,128)S(1)}, u32[]{:S(2)}) copy-start(f32[296,128]{1,0:T(8,128)S(1)} %collective-permute-done.3.refs_0_) | copy-start | bytes 454660
  33.3 4.0 %copy-start.4 = (f32[296,128]{1,0:T(8,128)}, f32[296,128]{1,0:T(8,128)S(1)}, u32[]{:S(2)}) copy-start(f32[296,128]{1,0:T(8,128)S(1)} %collective-permute-done.4.refs_1_) | copy-start | bytes 454660
  33.3 4.0 %copy-start.6 = (f32[296,128]{1,0:T(8,128)}, f32[296,128]{1,0:T(8,128)S(1)}, u32[]{:S(2)}) copy-start(f32[296,128]{1,0:T(8,128)S(1)} %collective-permute-done.5.refs_2_) | copy-start | bytes 454660
  33.3 35.7 %collective-permute-start.13 = (f32[80,2048]{1,0:T(8,128)S(1)}, f32[80,2048]{1,0:T(8,128)S(1)}, u32[]{:S(2)}, u32[]{:S(2)}) collective-permute-start(f32[80,2048]{1,0:T(8,128)S(1)} %bitcast.132), channel_id=1, source_target_pairs={{0,4},{1,13},{4,8},{5,1},{8,12},{9,5},{12,0},{13,9},{2,6},{3,15},{... | collective-permute-start | bytes 1966088 | tf_op jit(solution)/shard_map/ppermute | solution.py:553
  36.9 27.2 %collective-permute-start.14 = (f32[64,2048]{1,0:T(8,128)}, f32[64,2048]{1,0:T(8,128)S(1)}, u32[]{:S(2)}, u32[]{:S(2)}) collective-permute-start(f32[64,2048]{1,0:T(8,128)} %bitcast.133), channel_id=1, source_target_pairs={{0,4},{1,13},{4,8},{5,1},{8,12},{9,5},{12,0},{13,9},{2,6},{3,15},{... | collective-permute-start | bytes 1572872 | tf_op jit(solution)/shard_map/ppermute | solution.py:553
  39.5 7.0 %collective-permute-start.7 = (f32[1,2048]{1,0:T(1,128)}, f32[1,2048]{1,0:T(1,128)S(1)}, u32[]{:S(2)}, u32[]{:S(2)}) collective-permute-start(f32[1,2048]{1,0:T(1,128)} %shard_map.77), channel_id=1, source_target_pairs={{0,1},{1,0},{2,3},{3,2},{4,5},{5,4},{6,7},{7,6},{8,9},{9,8},{10,11... | collective-permute-start | bytes 24584 | tf_op jit(solution)/shard_map/ppermute | solution.py:613
  40.1 7.8 %collective-permute-start.8 = (f32[1,2048]{1,0:T(1,128)}, f32[1,2048]{1,0:T(1,128)S(1)}, u32[]{:S(2)}, u32[]{:S(2)}) collective-permute-start(f32[1,2048]{1,0:T(1,128)} %shard_map.77), channel_id=1, source_target_pairs={{0,2},{1,3},{2,0},{3,1},{4,6},{5,7},{6,4},{7,5},{8,10},{9,11},{10,... | collective-permute-start | bytes 24584 | tf_op jit(solution)/shard_map/ppermute | solution.py:613
  41.6 3.6 %collective-permute-start.10 = (f32[1,1]{1,0:T(1,128)}, f32[1,1]{1,0:T(1,128)}, u32[]{:S(2)}, u32[]{:S(2)}) collective-permute-start(f32[1,1]{1,0:T(1,128)} %bitcast.57), channel_id=1, source_target_pairs={{0,16},{16,0},{1,17},{17,1},{2,18},{18,2},{3,19},{19,3},{4,20},{20... | collective-permute-start | bytes 20 | tf_op jit(solution)/shard_map/ppermute | solution.py:598
  45.2 3.3 %collective-permute-start.9 = (f32[1,2048]{1,0:T(1,128)}, f32[1,2048]{1,0:T(1,128)S(1)}, u32[]{:S(2)}, u32[]{:S(2)}) collective-permute-start(f32[1,2048]{1,0:T(1,128)} %shard_map.77), channel_id=1, source_target_pairs={{0,3},{1,2},{2,1},{3,0},{4,7},{5,6},{6,5},{7,4},{8,11},{9,10},{10,... | collective-permute-start | bytes 24584 | tf_op jit(solution)/shard_map/ppermute | solution.py:613
  46.5 28.0 %collective-permute-start.12 = (f32[48,2048]{1,0:T(8,128)S(1)}, f32[48,2048]{1,0:T(8,128)S(1)}, u32[]{:S(2)}, u32[]{:S(2)}) collective-permute-start(f32[48,2048]{1,0:T(8,128)S(1)} %bitcast.137), channel_id=1, source_target_pairs={{0,4},{1,13},{4,8},{5,1},{8,12},{9,5},{12,0},{13,9},{2,6},{3,15},{... | collective-permute-start | bytes 1179656 | tf_op jit(solution)/shard_map/ppermute | solution.py:553
  47.9 30.8 %collective-permute-start.11 = (f32[32,2048]{1,0:T(8,128)}, f32[32,2048]{1,0:T(8,128)S(1)}, u32[]{:S(2)}, u32[]{:S(2)}) collective-permute-start(f32[32,2048]{1,0:T(8,128)} %bitcast.138), channel_id=1, source_target_pairs={{0,4},{1,13},{4,8},{5,1},{8,12},{9,5},{12,0},{13,9},{2,6},{3,15},{... | collective-permute-start | bytes 786440 | tf_op jit(solution)/shard_map/ppermute | solution.py:553
  49.3 1.0 copy-start.1
  50.2 0.9 copy-start.3
  51.1 0.9 copy-start.5
  52.1 0.9 copy-start.7
  53.0 0.6 copy-start.10
  69.0 22.7 %copy-start.16 = (s32[1024]{0:T(1024)S(1)}, s32[1024]{0:T(1024)}, u32[]{:S(2)}) copy-start(s32[1024]{0:T(1024)} %param.13) | copy-start | bytes 12292
  69.0 22.7 %copy-start.17 = (s32[1024]{0:T(1024)S(1)}, s32[1024]{0:T(1024)}, u32[]{:S(2)}) copy-start(s32[1024]{0:T(1024)} %param.12) | copy-start | bytes 12292
  69.0 29.2 %copy-start.15 = (s32[128,128]{1,0:T(8,128)S(1)}, s32[128,128]{1,0:T(8,128)}, u32[]{:S(2)}) copy-start(s32[128,128]{1,0:T(8,128)} %cell_ref.1) | copy-start | bytes 196612
  82.4 1.2 %collective-permute-start.15 = (f32[2,16,128]{2,1,0:T(8,128)S(1)}, f32[2,16,128]{2,1,0:T(8,128)S(1)}, u32[]{:S(2)}, u32[]{:S(2)}) collective-permute-start(f32[2,16,128]{2,1,0:T(8,128)S(1)} %get-tuple-element.97), channel_id=1, source_target_pairs={{0,1},{1,0},{2,3},{3,2},{4,5},{5,4},{6,7},{7,6},{8,9},{9,8},{10,11... | collective-permute-start | bytes 49160 | tf_op jit(solution)/shard_map/ppermute | solution.py:654
  83.5 3.7 %collective-permute-start.16 = (f32[2,16,128]{2,1,0:T(8,128)S(1)}, f32[2,16,128]{2,1,0:T(8,128)S(1)}, u32[]{:S(2)}, u32[]{:S(2)}) collective-permute-start(f32[2,16,128]{2,1,0:T(8,128)S(1)} %add.597), channel_id=1, source_target_pairs={{0,2},{2,0},{1,3},{3,1},{4,6},{6,4},{5,7},{7,5},{8,10},{10,8},{9,1... | collective-permute-start | bytes 49160 | tf_op jit(solution)/shard_map/ppermute | solution.py:656
  87.3 4.4 %collective-permute-start.17 = (f32[2,16,128]{2,1,0:T(8,128)S(1)}, f32[2,16,128]{2,1,0:T(8,128)S(1)}, u32[]{:S(2)}, u32[]{:S(2)}) collective-permute-start(f32[2,16,128]{2,1,0:T(8,128)S(1)} %add.598.refs_0_), channel_id=1, source_target_pairs={{0,4},{4,0},{8,12},{12,8},{1,5},{5,1},{9,13},{13,9},{2,6},{6,2},{1... | collective-permute-start | bytes 49160 | tf_op jit(solution)/shard_map/ppermute | solution.py:661
  89.0 4.6 %collective-permute-start.18 = (f32[2,16,128]{2,1,0:T(8,128)S(1)}, f32[2,16,128]{2,1,0:T(8,128)S(1)}, u32[]{:S(2)}, u32[]{:S(2)}) collective-permute-start(f32[2,16,128]{2,1,0:T(8,128)S(1)} %add.598.refs_0_), channel_id=1, source_target_pairs={{0,8},{4,12},{8,0},{12,4},{1,9},{5,13},{9,1},{13,5},{2,10},{6,14},... | collective-permute-start | bytes 49160 | tf_op jit(solution)/shard_map/ppermute | solution.py:661
  91.4 5.5 %collective-permute-start.19 = (f32[2,16,128]{2,1,0:T(8,128)S(1)}, f32[2,16,128]{2,1,0:T(8,128)S(1)}, u32[]{:S(2)}, u32[]{:S(2)}) collective-permute-start(f32[2,16,128]{2,1,0:T(8,128)S(1)} %add.598.refs_0_), channel_id=1, source_target_pairs={{0,12},{4,8},{8,4},{12,0},{1,13},{5,9},{9,5},{13,1},{2,14},{6,10},... | collective-permute-start | bytes 49160 | tf_op jit(solution)/shard_map/ppermute | solution.py:661

commit v4 on v3

--- a/solution.py
+++ b/solution.py
@@ -20,6 +20,7 @@
 BF16 = jnp.bfloat16
 I32 = jnp.int32
 WHOLE = pl.BlockSpec(memory_space=pltpu.VMEM)
+SHORT = pl.CostEstimate(flops=1000, bytes_accessed=1000, transcendentals=0)
 SCALARS = pl.BlockSpec(memory_space=pltpu.SMEM)
 
 
@@ -167,27 +168,23 @@
 
 C_KEEP, C_ROW, C_COL, C_SLOPE, C_EAST, C_NORTH, C_ONE, C_DAMP = range(8)
 C_S_EAST, C_S_NORTH, C_T_EAST, C_T_NORTH = range(8, 12)
-CHUNK_ENDS = (4, 8, 13, 16)
-VMEM_BYTES = 40 * 1024 * 1024
-
-
-def split3(value):
-    high = value.astype(BF16)
-    rest = value - high.astype(F32)
-    middle = rest.astype(BF16)
-    low = (rest - middle.astype(F32)).astype(BF16)
-    return high, middle, low
-
-
-def times_exact(value, one_hot, dims):
-    parts = [
-        lax.dot_general(part, one_hot, (dims, ((), ())), preferred_element_type=F32)
-        for part in split3(value)
-    ]
-    return parts[0] + parts[1] + parts[2]
-
-
-def index_kernel(owners, par_ref, cell_ref, coef_ref, g_ref, idx_ref, count_ref, sum_ref, *list_refs):
+CHUNK_ENDS = (3, 6, 7, 12, 16)
+VMEM_BYTES = 24 * 1024 * 1024
+
+
+def times_hot(value, one_hot, dims, parts=3):
+    count = value.shape[0]
+    pieces = []
+    for _ in range(parts):
+        pieces.append(value.astype(BF16).astype(F32))
+        value = value - pieces[-1]
+    stacked = jnp.concatenate(pieces, axis=0).astype(BF16)
+    found = lax.dot_general(stacked, one_hot, (dims, ((), ())), preferred_element_type=F32)
+    return sum(found[part * count : (part + 1) * count] for part in range(parts))
+
+
+def index_kernel(owners, starts, par_ref, cell_ref, coef_ref, g_ref, idx_ref, count_ref, sum_ref, *refs):
+    list_refs, chunk_refs = refs[: owners - 2], refs[owners - 2 :]
     slots = g_ref.shape[1]
     blocks = slots // LANES
     half_rows = g_ref.shape[0] // 2
@@ -252,7 +249,7 @@
             step = jnp.where(minus, step_above, step_below)
             other = jnp.where(minus, point - step_above, point + step_below)
             owner = other & (owners - 1)
-            away = (pts - owner) if sends == 0 else (owner - pts)
+            away = ((pts - owner) if sends == 0 else (owner - pts)) * par_ref[5]
             away = jnp.where(step > 0, away & (owners - 1), -1)
             codes.append((away, other >> shift))
             masks.append(jnp.where(group == away, 1.0, 0.0))
@@ -279,9 +276,11 @@
             sum_ref[at : at + 1, :] += jnp.sum(
                 weighted * coef_ref[rows, column_of : column_of + 1], axis=0, keepdims=True
             )
-    entry = lax.broadcasted_iota(I32, ((owners - 1) * LANES, slots), 0)
+    lanes_all = (owners - 2) * 2 * LANES
+    entry = lax.broadcasted_iota(I32, (lanes_all, slots), 0)
+    packed, sums = [], []
     for half in range(2):
-        places = [
+        receive, send = [
             jnp.sum(
                 counts[(2 * half + sends) * groups : (2 * half + sends + 1) * groups],
                 axis=0,
@@ -290,26 +289,35 @@
             for sends in range(2)
         ]
         away, other_slot = codes[2 * half]
-        place = places[0]
-        same_block = (other_slot >> 7) == (slot >> 7)
-        code = jnp.where(away == 0, jnp.where(same_block, 1, 2), away + 2)
-        code = jnp.where(away < 0, 0, code)
-        lane = jnp.where(away == 0, other_slot & (LANES - 1), jnp.minimum(place, LANES - 1))
-        lane = jnp.where(away < 0, 0, lane)
-        idx_ref[2 * half] = jnp.broadcast_to(lane, (8, slots))
-        idx_ref[2 * half + 1] = jnp.broadcast_to(code, (8, slots))
+        spilled = receive >= LANES
+        place = jnp.where(spilled, jnp.maximum(2 * LANES - 1 - receive, 0), receive)
+        other_block = jnp.where((other_slot >> 7) == (slot >> 7), 0, 1)
+        code = jnp.where(away <= 1, 1 + 2 * away + other_block, 1 + 2 * away + jnp.where(spilled, 1, 0))
+        lane = jnp.where(away <= 1, other_slot & (LANES - 1), place)
+        idx_ref[2 * half] = jnp.broadcast_to(jnp.where(away < 0, 0, lane), (8, slots))
+        idx_ref[2 * half + 1] = jnp.broadcast_to(jnp.where(away < 0, 0, code), (8, slots))
         away, _ = codes[2 * half + 1]
-        place = places[1]
-        key = jnp.where((away > 0) & (place < LANES), (away - 1) * LANES + place, -1)
+        place = jnp.where(send >= LANES, 3 * LANES - 1 - send, send)
+        place = jnp.where(send >= 2 * LANES, -1, place)
+        key = jnp.where((away > 1) & (place >= 0), (away - 2) * 2 * LANES + place, -1)
         one_hot = jnp.where(entry == key, 1.0, 0.0).astype(BF16)
         rows = slice(half * half_rows, (half + 1) * half_rows)
-        packed = times_exact(g_ref[rows, :], one_hot, ((1,), (1,)))
-        sums = times_exact(sum_ref[...], one_hot, ((1,), (1,)))
-        for at, list_ref in enumerate(list_refs):
-            lanes = slice(at * LANES, (at + 1) * LANES)
-            list_ref[rows, :] = packed[:, lanes]
-            row = 2 * half_rows + half
-            list_ref[row : row + 1, :] = sums[1 + half : 2 + half, lanes]
+        packed.append(times_hot(g_ref[rows, :], one_hot, ((1,), (1,)), 2))
+        sums.append(times_hot(sum_ref[...], one_hot, ((1,), (1,))))
+    for at, list_ref in enumerate(list_refs):
+        inner = slice(2 * at * LANES, (2 * at + 1) * LANES)
+        outer = slice((2 * at + 1) * LANES, (2 * at + 2) * LANES)
+        for half in range(2):
+            rows = slice(half * half_rows, (half + 1) * half_rows)
+            list_ref[rows, :] = packed[half][:, inner] + packed[1 - half][:, outer]
+            row, other = 1 + half, 2 - half
+            list_ref[2 * half_rows + half : 2 * half_rows + half + 1, :] = (
+                sums[half][row : row + 1, inner] + sums[1 - half][other : other + 1, outer]
+            )
+    chunk_refs[0][-8:, :] = sum_ref[...]
+    for start, chunk_ref in zip(starts, chunk_refs):
+        count = chunk_ref.shape[0] - (8 if start == starts[0] else 0)
+        chunk_ref[:count, :] = g_ref[start : start + count, :]
     for list_ref in list_refs:
         list_ref[2 * half_rows + 2 :, :] = jnp.zeros((6, LANES), F32)
     idx_ref[4] = jnp.broadcast_to(has_beside, (8, slots))
@@ -319,11 +327,10 @@
     return jnp.take_along_axis(values, lanes, axis=1)
 
 
-def row_neighbour(shape, code, lanes, own, near, lists):
-    value = jnp.where(code == 1, lane_take(own, lanes), 0.0)
-    value = jnp.where(code == 2, lane_take(near, lanes), value)
-    for number, values in enumerate(lists):
-        value = jnp.where(code == 3 + number, lane_take(values, lanes), value)
+def row_neighbour(code, lanes, sources):
+    value = jnp.zeros(code.shape, F32)
+    for number, source in enumerate(sources):
+        value = jnp.where(code == 1 + number, lane_take(source, lanes), value)
     return value
 
 
@@ -343,32 +350,35 @@
     shape = (8, LANES)
     turn = par_ref[3]
     beside_lanes, beyond = turned_lanes(turn)
-    every = slice(0, 8)
+    every, last = slice(0, 8), slice(beside_ref.shape[0] - 8, beside_ref.shape[0])
     lists = [ref[-8:, :] for ref in list_refs]
     for block in range(sum_ref.shape[1] // LANES):
         at = slice(block * LANES, (block + 1) * LANES)
-        own = sum_ref[:, at]
+        own, beside = sum_ref[:, at], beside_ref[last, at]
         slope = own[0:1]
         for half in range(2):
             lanes, code = idx_ref[2 * half, :, at], idx_ref[2 * half + 1, :, at]
-            near = near_block(sum_ref, every, block, par_ref[1 + half])
-            here = jnp.where(code == 1, lane_take(own, lanes), 0.0)
-            here = jnp.where(code == 2, lane_take(near, lanes), here)
-            slope = slope + here[1 + half : 2 + half]
-            there = jnp.zeros(shape, F32)
-            for number, values in enumerate(lists):
-                there = jnp.where(code == 3 + number, lane_take(values, lanes), there)
-            slope = slope + there[half : half + 1]
+            way = par_ref[1 + half]
+            sources = [own, near_block(sum_ref, every, block, way)]
+            sources += [beside, near_block(beside_ref, last, block, way)]
+            value = row_neighbour(code, lanes, sources)
+            slope = slope + value[1 + half : 2 + half]
+            code = code - 4
+            for values in lists:
+                for row in (half, 1 - half):
+                    value = jnp.where(code == 1, lane_take(values, lanes), 0.0)
+                    slope = slope + value[row : row + 1]
+                    code = code - 1
         column = jnp.where(
             beyond,
-            lane_take(jnp.broadcast_to(near_block(beside_ref, slice(0, 1), block, turn), shape), beside_lanes),
-            lane_take(jnp.broadcast_to(beside_ref[:, at], shape), beside_lanes),
+            lane_take(near_block(beside_ref, last, block, turn), beside_lanes),
+            lane_take(beside, beside_lanes),
         )
-        slope_ref[:, at] = slope + jnp.where(idx_ref[4, 0:1, at] > 0, column[0:1], 0.0)
+        slope_ref[:, at] = slope + jnp.where(idx_ref[4, 0:1, at] > 0, column[3:4], 0.0)
 
 
 def step_kernel(owners, first_step, half_steps, chained, final, par_ref, idx_ref, wind_ref, slope_ref, coef_ref, g_ref, beside_ref, *refs):
-    list_refs, refs = refs[: owners - 1], refs[owners - 1 :]
+    list_refs, refs = refs[: owners - 2], refs[owners - 2 :]
     if chained:
         _, before_ref, refs = refs[0], refs[1], refs[2:]
     out_ref, sums_refs, total_ref, damp_ref = refs[0], refs[1:-2], refs[-2], refs[-1]
@@ -389,6 +399,10 @@
         first = pl.program_id(0) * out_ref.shape[0] + tile * 8
         near_rows = pl.ds(pl.multiple_of(first, 8), 8)
         rows = pl.ds(pl.multiple_of(first + first_step * out_ref.shape[0], 8), 8)
+        half_rows = half_steps * out_ref.shape[0]
+        other_rows = pl.ds(
+            pl.multiple_of(first + first_step * out_ref.shape[0] + (1 - 2 * half) * half_rows, 8), 8
+        )
         coef = coef_ref[rows, :]
 
         def factor(at):
@@ -398,18 +412,19 @@
         east, north, one, damp = factor(C_EAST), factor(C_NORTH), factor(C_ONE), factor(C_DAMP)
         s_east, s_north = factor(C_S_EAST), factor(C_S_NORTH)
         t_east, t_north = factor(C_T_EAST), factor(C_T_NORTH)
-        lists = [ref[rows, :] for ref in list_refs]
+        lists = [ref[which, :] for ref in list_refs for which in (rows, other_rows)]
         for block in range(blocks):
             at = slice(block * LANES, (block + 1) * LANES)
             lanes, code = idx_ref[2 * half, :, at], idx_ref[2 * half + 1, :, at]
             has_beside = idx_ref[4, :, at]
-            own = g_ref[rows, at]
-            near = near_block(g_ref, rows, block, way)
-            row_value = row_neighbour(shape, code, lanes, own, near, lists)
+            own, beside = g_ref[here, at], beside_ref[near_rows, at]
+            sources = [own, near_block(g_ref, here, block, way)]
+            sources += [beside, near_block(beside_ref, near_rows, block, way)]
+            row_value = row_neighbour(code, lanes, sources + lists)
             col_value = jnp.where(
                 beyond,
                 lane_take(near_block(beside_ref, near_rows, block, turn), beside_lanes),
-                lane_take(beside_ref[near_rows, at], beside_lanes),
+                lane_take(beside, beside_lanes),
             )
             col_value = jnp.where(has_beside > 0, col_value, 0.0)
             value = keep * own + by_row * row_value + by_col * col_value
@@ -459,7 +474,7 @@
         hot = jnp.where(lax.broadcasted_iota(I32, (rows, count), 0) == row, 1.0, 0.0).astype(BF16)
         table = jnp.concatenate([ref[item] for ref in table_refs], axis=0)
         table = jnp.transpose(table)
-        found = times_exact(table, hot, ((1,), (0,)))
+        found = times_hot(table, hot, ((1,), (0,)))
         pick = lax.broadcasted_iota(I32, (LANES, count), 0) == lane
         out_ref[...] = jnp.sum(jnp.where(pick, found, 0.0), axis=0, keepdims=True)
 
@@ -503,15 +518,14 @@
     return jax.ShapeDtypeStruct(dims, kind)
 
 
-def call(kernel, inputs, outputs, scratch=(), flops=0, moved=0):
+def call(kernel, inputs, outputs):
     return pl.pallas_call(
         kernel,
         in_specs=inputs,
         out_specs=[WHOLE] * len(outputs),
         out_shape=outputs,
-        scratch_shapes=list(scratch),
         compiler_params=pltpu.CompilerParams(vmem_limit_bytes=VMEM_BYTES),
-        cost_estimate=pl.CostEstimate(flops=flops, bytes_accessed=moved, transcendentals=0),
+        cost_estimate=SHORT,
     )
 
 
@@ -544,77 +558,66 @@
         field = jnp.pad(field, ((0, 0), (0, pad_half), (0, 0)))
     field = field.reshape(rows, slots)
 
-    ring = []
-    for owner in range(owners):
-        ring.append((owner * 2, (owner + 1) % owners * 2))
-        ring.append((owner * 2 + 1, (owner - 1) % owners * 2 + 1))
-
-    def around(values):
-        return lax.ppermute(values, ("pts", "cpl"), ring)
+    def around(values, distance=1):
+        pairs = []
+        for owner in range(owners):
+            pairs.append((owner * 2, (owner + distance) % owners * 2))
+            pairs.append((owner * 2 + 1, (owner - distance) % owners * 2 + 1))
+        return lax.ppermute(values, ("pts", "cpl"), pairs)
 
     def chunk(values, at):
         return values[at[0] * step_rows : at[1] * step_rows]
 
     chunks = chunks_of(steps)
-    beside = [around(chunk(field, chunks[0]))]
+    beside = [around(chunk(field, at)) for at in chunks[:2]]
 
     first_way = 2 * my_cpl - 1
     turn = jnp.where(
         (my_cpl == 0) & (my_pts == 0), -1, jnp.where((my_cpl == 1) & (my_pts == owners - 1), 1, 0)
     )
-    par = jnp.stack([my_pts, first_way, -first_way, turn, my_cpl]).astype(I32)
+    par = jnp.stack([my_pts, first_way, -first_way, turn, my_cpl, -first_way]).astype(I32)
     coef = coefficients(
         freq_local, dirs_local, pad_half, my_spec, my_cpl, freq_count, dir_count
     )
 
     found = call(
-        functools.partial(index_kernel, owners),
+        functools.partial(index_kernel, owners, [start * step_rows for start, _ in chunks[2:]]),
         [SCALARS, WHOLE, WHOLE, WHOLE],
         [
             shape_of(5, 8, slots, kind=I32),
             shape_of(owners * owners, cell_sea.shape[1]),
             shape_of(8, slots),
         ]
-        + [shape_of(rows + 8, LANES)] * (owners - 1),
-        flops=6 * rows * slots * LANES * owners,
-        moved=rows * slots * 4,
+        + [shape_of(rows + 8, LANES)] * (owners - 2)
+        + [
+            shape_of((stop - start) * step_rows + (8 if at == 0 else 0), slots)
+            for at, (start, stop) in enumerate(chunks[2:])
+        ],
     )(par, cell_sea, coef, field)
-    (idx, counts, row_sums), *lists = lax.optimization_barrier((found[:3], *found[3:], beside[0]))
-    beside = [lists.pop()]
-    arrived = [
-        lax.ppermute(values, "pts", [(i, (i + 1 + away) % owners) for i in range(owners)])
-        for away, values in enumerate(lists)
-    ]
-    beside_sums = around(row_sums[3:4])
-    second = chunk(field, chunks[1])
-    second, *_ = lax.optimization_barrier((second, *lists))
-    beside.append(around(second))
-    later = [chunk(field, at) for at in chunks[2:]]
-    later, arrived, beside_sums = lax.optimization_barrier((later, arrived, beside_sums))
+    found, beside[0] = lax.optimization_barrier((found, beside[0]))
+    (idx, counts, row_sums), lists = found[:3], found[3 : owners + 1]
+    leaving = found[owners + 1 :]
+    arrived = [around(values, 2 + at) for at, values in enumerate(lists)]
+    beside.append(around(leaving[0]))
+    later, arrived, beside = lax.optimization_barrier((leaving[1:], arrived, beside))
     beside += [around(values) for values in later]
 
-    longest = jnp.max(jnp.sum(counts, axis=1)).reshape(1, 1)
+    pairs = jnp.sum(counts, axis=1).reshape(owners, owners)
+    longest = jnp.max(pairs + pairs.T).reshape(1, 1)
     if groups == 2:
         longest = jnp.maximum(longest, lax.ppermute(longest, "grp", [(0, 1), (1, 0)]))
     else:
         longest = lax.pmax(longest, "grp")
 
-    slope_part = pl.pallas_call(
-        slope_kernel,
-        in_specs=[SCALARS, WHOLE, WHOLE, WHOLE] + [WHOLE] * (owners - 1),
-        out_specs=WHOLE,
-        out_shape=shape_of(1, slots),
-    )(par, idx, row_sums, beside_sums, *arrived)
-
-    peers = spec_groups * cpl_groups
-    slope = slope_part
+    (slope_part,) = call(
+        slope_kernel, [SCALARS] + [WHOLE] * (owners + 1), [shape_of(1, slots)]
+    )(par, idx, row_sums, beside[2], *arrived)
+
+    slope = slope_part + lax.ppermute(slope_part, "cpl", [(0, 1), (1, 0)])
     if spec_groups == 2:
-        for turned in range(1, peers):
-            slope = slope + lax.ppermute(
-                slope_part, ("spec", "cpl"), [(i, i ^ turned) for i in range(peers)]
-            )
+        slope = slope + lax.ppermute(slope, "spec", [(0, 1), (1, 0)])
     else:
-        slope = lax.psum(slope_part, ("spec", "cpl"))
+        slope = lax.psum(slope, "spec")
 
     slope, longest = lax.optimization_barrier((slope, longest))
     updated = sums = None
@@ -625,7 +628,7 @@
             (step_rows, width), functools.partial(lambda first, i: (first + i, 0), start)
         )
         inputs = [par, idx, wind_deck, slope, coef, field, near, *arrived]
-        specs = [SCALARS] + [WHOLE] * (owners + 5)
+        specs = [SCALARS] + [WHOLE] * 4 + [in_rows(slots)] + [WHOLE] * (owners - 1)
         aliases = {}
         if chained:
             aliases = {len(inputs): 0}
@@ -641,11 +644,7 @@
             scratch_shapes=[pltpu.VMEM((4, 8, slots), F32), pltpu.VMEM((8, slots), F32)],
             input_output_aliases=aliases,
             compiler_params=pltpu.CompilerParams(vmem_limit_bytes=VMEM_BYTES),
-            cost_estimate=pl.CostEstimate(
-                flops=(stop - start) * step_rows * slots * 50,
-                bytes_accessed=(stop - start) * step_rows * slots * 12,
-                transcendentals=(stop - start) * step_rows * slots,
-            ),
+            cost_estimate=SHORT,
         )(*inputs)
         if not final:
             sums = sums[0]
@@ -671,8 +670,6 @@
         functools.partial(pick_kernel, owners),
         [WHOLE] * (2 + owners),
         [shape_of(1, count)] * 2,
-        flops=owners * blocks * LANES * count * 12,
-        moved=owners * blocks * LANES * 8,
     )(looked(atm_order), looked(ocean_order), *tables)
 
     def by_direction(values):
@@ -686,7 +683,7 @@
         updated = updated.reshape(2, half_rows + pad_half, slots)[:, :half_rows]
         updated = updated.reshape(2 * half_rows, slots)
     updated, stress_atm, stokes_ocn = lax.cond(
-        longest[0, 0] > LANES, general_way, lambda: (updated, stress_atm, stokes_ocn)
+        longest[0, 0] > 2 * LANES, general_way, lambda: (updated, stress_atm, stokes_ocn)
     )
     updated = jnp.transpose(updated.reshape(dirs_local, freq_local, slots), (1, 0, 2))
     return updated, stress_atm, stokes_ocn

time: 98.8 us -> 92 us (0.931)
  local copies, waits for them, and re-layouts: 12.4 us -> 3.64 us
  starting transfers between devices: 23 us -> 26.8 us
  Pallas kernels: 35.5 us -> 33.9 us
    unnamed x38 -> x14, local copies, waits for them, and re-layouts: 5.25 us -> 0.17 us
    ppermute x12 -> x10, starting transfers between devices: 15.6 us -> 19.4 us  [the longest x8 17.8 us: around(): return lax.ppermute(values, ('pts', 'cpl'), pairs)]
    slice x4 -> x1, local copies, waits for them, and re-layouts: 5.91 us -> 2.07 us  [chunk(): return values[at[0] * step_rows:at[1] * step_rows]]
    pallas_call x2, Pallas kernels: 11.2 us -> 8.8 us  [the longest x1 7.79 us: local(): call(functools.partial(index_kernel, owners, [start * step_rows for start...]
    ppermute x12 -> x10, waiting for transfers between devices: 12.7 us -> 14.7 us  [the longest x8 13.8 us: around(): return lax.ppermute(values, ('pts', 'cpl'), pairs)]
    ppermute x3, waiting for transfers between devices: 5.19 us -> 3.65 us  [local(): lax.ppermute(mine, 'pts', [(i, i ^ turned) for i in range(owners)])]
    pallas_call x5 -> x6, Pallas kernels: 23 us -> 23.9 us  [local(): pl.pallas_call(functools.partial(step_kernel, owners, start, steps // 2,...]
  transfers between devices with their start and end apart: 18 -> 16, of which waited for: 9 -> 10; matrix products, arithmetic and copies ran while one was open for 7% -> 3% of each run, Pallas kernels for 31% -> 32%
where the time goes in v4:
time: 92 us; the launch traced here: 91.5 us
  Pallas kernels  33.9 us (37%)
  starting transfers between devices  26.8 us (29%)
  waiting for transfers between devices  24.1 us (26%)
  local copies, waits for them, and re-layouts  3.64 us (4%)
  between operations  2.12 us (2%)
  other arithmetic  0.95 us (1%)
    pallas_call x6, Pallas kernels, local(): pl.pallas_call(functools.partial(step_kernel, owners, start, steps // 2,...  23.9 us
    ppermute x8, starting transfers between devices, around(): return lax.ppermute(values, ('pts', 'cpl'), pairs)  17.8 us
    ppermute x8, waiting for transfers between devices, around(): return lax.ppermute(values, ('pts', 'cpl'), pairs)  13.8 us
    pallas_call x1, Pallas kernels, local(): call(functools.partial(index_kernel, owners, [start * step_rows for start...  7.79 us
    ppermute x3, starting transfers between devices, local(): lax.ppermute(mine, 'pts', [(i, i ^ turned) for i in range(owners)])  4.38 us
    ppermute x3, waiting for transfers between devices, local(): lax.ppermute(mine, 'pts', [(i, i ^ turned) for i in range(owners)])  3.65 us
    ppermute x1, waiting for transfers between devices, local(): lax.ppermute(longest, 'grp', [(0, 1), (1, 0)])  2.26 us
    ppermute x1, waiting for transfers between devices, local(): mine = mine + lax.ppermute(mine, 'spec', [(0, 1), (1, 0)])  2.25 us
  transfers between devices with their start and end apart: 16, of which 10 were waited for; matrix products, arithmetic and copies ran while one was open for 3% of the time, Pallas kernels for 32%

profile of v4, /device:TPU:0, one launch (start us, length us, event | category | flops | bytes accessed | tf_op | source)
XLA Modules:
  0.0 91.5 jit_solution(9986397619519236117)
XLA Ops:
  0.6 2.1 %fusion.61 = (f32[3,16,2048]{2,1,0:T(8,128)}, f32[3,16,2048]{2,1,0:T(8,128)}) fusion(f32[18,16,2048]{2,1,0:T(8,128)} %bitcast.51), kind=kLoop, calls=%fused_computation.224 | loop fusion | bytes 1572864 | tf_op jit(solution)/shard_map/slice | solution.py:569
  2.7 3.0 %collective-permute-start.2 = (f32[48,2048]{1,0:T(8,128)}, f32[48,2048]{1,0:T(8,128)S(1)}, u32[]{:S(2)}, u32[]{:S(2)}) collective-permute-start(f32[48,2048]{1,0:T(8,128)} %bitcast.53), channel_id=1, source_target_pairs={{0,4},{1,13},{4,8},{5,1},{8,12},{9,5},{12,0},{13,9},{2,6},{3,15},{... | collective-permute-start | bytes 1179656 | tf_op jit(solution)/shard_map/ppermute | solution.py:566
  5.7 1.6 %collective-permute-start.5 = (f32[48,2048]{1,0:T(8,128)}, f32[48,2048]{1,0:T(8,128)S(1)}, u32[]{:S(2)}, u32[]{:S(2)}) collective-permute-start(f32[48,2048]{1,0:T(8,128)} %bitcast.54), channel_id=1, source_target_pairs={{0,4},{1,13},{4,8},{5,1},{8,12},{9,5},{12,0},{13,9},{2,6},{3,15},{... | collective-permute-start | bytes 1179656 | tf_op jit(solution)/shard_map/ppermute | solution.py:566
  7.5 0.1 mul.605
  7.7 0.1 mul.608
  7.8 0.1 mul.602
  7.9 0.1 stack_broadcast_in_dim.42
  8.0 0.1 mul.615
  8.2 0.1 stack_broadcast_in_dim.48
  8.3 0.1 stack_broadcast_in_dim.51
  8.5 0.1 stack_broadcast_in_dim.53
  8.6 0.1 mul.623
  8.7 0.1 copy.46
  8.9 0.1 stack.41.par_ref
  9.0 7.8 %shard_map.76 = (s32[5,8,2048]{2,1,0:T(8,128)S(1)}, f32[16,128]{1,0:T(8,128)S(1)}, f32[8,2048]{1,0:T(8,128)S(1)}, f32[296,128]{1,0:T(8,128)S(1)}, f32[296,128]{1...) custom-call(s32[6]{0:T(128)S(1)} %stack.41.par_ref, ...), custom_call_target="tpu_custom_call" | custom-call | flops 1000 | bytes 1000 | tf_op jit(solution)/shard_map/pallas_call | solution.py:583
  16.8 1.1 %collective-permute-done.2.beside_ref = f32[48,2048]{1,0:T(8,128)S(1)} collective-permute-done((f32[48,2048]{1,0:T(8,128)}, f32[48,2048]{1,0:T(8,128)S(1)}, u32[]{:S(2)}, u32[]{:S(2)}) %collective-permute-start.2) | collective-permute-done | bytes 393248 | tf_op jit(solution)/shard_map/ppermute | solution.py:566
  17.9 0.5 collective-permute-start.6
  18.4 1.5 %collective-permute-start.3 = (f32[296,128]{1,0:T(8,128)S(1)}, f32[296,128]{1,0:T(8,128)S(1)}, u32[]{:S(2)}, u32[]{:S(2)}) collective-permute-start(f32[296,128]{1,0:T(8,128)S(1)} %get-tuple-element.86), channel_id=1, source_target_pairs={{0,8},{1,9},{4,12},{5,13},{8,0},{9,1},{12,4},{13,5},{2,10},{3,11},... | collective-permute-start | bytes 454664 | tf_op jit(solution)/shard_map/ppermute | solution.py:566
  19.9 1.9 %collective-permute-start.4 = (f32[296,128]{1,0:T(8,128)S(1)}, f32[296,128]{1,0:T(8,128)S(1)}, u32[]{:S(2)}, u32[]{:S(2)}) collective-permute-start(f32[296,128]{1,0:T(8,128)S(1)} %get-tuple-element.87), channel_id=1, source_target_pairs={{0,12},{1,5},{4,0},{5,9},{8,4},{9,13},{12,8},{13,1},{2,14},{3,7},{... | collective-permute-start | bytes 454664 | tf_op jit(solution)/shard_map/ppermute | solution.py:566
  21.7 4.6 %collective-permute-done.5.beside_ref = f32[48,2048]{1,0:T(8,128)S(1)} collective-permute-done((f32[48,2048]{1,0:T(8,128)}, f32[48,2048]{1,0:T(8,128)S(1)}, u32[]{:S(2)}, u32[]{:S(2)}) %collective-permute-start.5) | collective-permute-done | bytes 393248 | tf_op jit(solution)/shard_map/ppermute | solution.py:566
  26.3 7.7 %collective-permute-done.3.refs_0_ = f32[296,128]{1,0:T(8,128)S(1)} collective-permute-done((f32[296,128]{1,0:T(8,128)S(1)}, f32[296,128]{1,0:T(8,128)S(1)}, u32[]{:S(2)}, u32[]{:S(2)}) %collective-permute-start.3) | collective-permute-done | bytes 151584 | tf_op jit(solution)/shard_map/ppermute | solution.py:566
  34.0 5.4 %collective-permute-start.12 = (f32[80,2048]{1,0:T(8,128)}, f32[80,2048]{1,0:T(8,128)S(1)}, u32[]{:S(2)}, u32[]{:S(2)}) collective-permute-start(f32[80,2048]{1,0:T(8,128)} %get-tuple-element.98), channel_id=1, source_target_pairs={{0,4},{1,13},{4,8},{5,1},{8,12},{9,5},{12,0},{13,9},{2,6},{3,15},{... | collective-permute-start | bytes 1966088 | tf_op jit(solution)/shard_map/ppermute | solution.py:566
  39.4 0.8 collective-permute-start.11
  40.3 3.1 %collective-permute-start.10 = (f32[32,2048]{1,0:T(8,128)S(1)}, f32[32,2048]{1,0:T(8,128)S(1)}, u32[]{:S(2)}, u32[]{:S(2)}) collective-permute-start(f32[32,2048]{1,0:T(8,128)S(1)} %get-tuple-element.96), channel_id=1, source_target_pairs={{0,4},{1,13},{4,8},{5,1},{8,12},{9,5},{12,0},{13,9},{2,6},{3,15},{... | collective-permute-start | bytes 786440 | tf_op jit(solution)/shard_map/ppermute | solution.py:566
  43.4 1.0 %shard_map.77 = f32[1,2048]{1,0:T(1,128)S(1)} custom-call(s32[6]{0:T(128)S(1)} %stack.41.par_ref, s32[5,8,2048]{2,1,0:T(8,128)S(1)} %get-tuple-element.81.idx_ref, f32[8,2048]{1,0:T(8,128)S(1)} %get-tuple-element.82.sum_ref, f32[24,2048]{1,0:T(8,128)S(1)} %collective-permute-done.6.beside_ref, f32[296,128]{1,0:T(8,128)S(1)} %collective-permute-done.3.refs_0_, ...), custom_call_target="tpu_custom_call" | custom-call | flops 1000 | bytes 1000 | tf_op jit(solution)/shard_map/pallas_call | solution.py:612
  44.5 0.1 reduce_sum.85
  44.6 0.1 reshape.1209
  44.7 0.1 copy.42
  44.8 0.9 collective-permute-done.7
  45.6 1.6 %collective-permute-start.8 = (f32[1,2048]{1,0:T(1,128)S(1)}, f32[1,2048]{1,0:T(1,128)S(1)}, u32[]{:S(2)}, u32[]{:S(2)}) collective-permute-start(f32[1,2048]{1,0:T(1,128)S(1)} %add.594), channel_id=1, source_target_pairs={{0,2},{2,0},{1,3},{3,1},{4,6},{6,4},{5,7},{7,5},{8,10},{10,8},{9,1... | collective-permute-start | bytes 24584 | tf_op jit(solution)/shard_map/ppermute | solution.py:618
  47.2 0.6 fusion.52
  47.8 1.5 %collective-permute-start.9 = (f32[1,1]{1,0:T(1,128)}, f32[1,1]{1,0:T(1,128)}, u32[]{:S(2)}, u32[]{:S(2)}) collective-permute-start(f32[1,1]{1,0:T(1,128)} %bitcast.56), channel_id=1, source_target_pairs={{0,16},{16,0},{1,17},{17,1},{2,18},{18,2},{3,19},{19,3},{4,20},{20... | collective-permute-start | bytes 20 | tf_op jit(solution)/shard_map/ppermute | solution.py:608
  49.3 2.3 %collective-permute-done.9 = f32[1,1]{1,0:T(1,128)} collective-permute-done((f32[1,1]{1,0:T(1,128)}, f32[1,1]{1,0:T(1,128)}, u32[]{:S(2)}, u32[]{:S(2)}) %collective-permute-start.9) | collective-permute-done | bytes 36 | tf_op jit(solution)/shard_map/ppermute | solution.py:608
  52.9 4.0 %shard_map.78 = (f32[288,2048]{1,0:T(8,128)}, f32[4,16,128]{2,1,0:T(8,128)S(1)}) custom-call(s32[6]{0:T(128)S(1)} %stack.41.par_ref, s32[5,8,2048]{2,1,0:T(8,128)S(1)} %get-tuple-element.81.idx_ref, f32[2,2048]{1,0:T(2,128)S(1)} %copy-done.4, f32[1,2048]{1,0:T(1,128)S(1)} %add.595.slope_ref, f32[288,16]{1,0:T(8,128)S(1)} %bitcast.120, ...), custom_call_target="tpu_custom_call" | custom-call | flops 1000 | bytes 1000 | tf_op jit(solution)/shard_map/pallas_call | solution.py:638
  56.9 4.0 %shard_map.79 = (f32[288,2048]{1,0:T(8,128)}, f32[4,16,128]{2,1,0:T(8,128)S(1)}) custom-call(s32[6]{0:T(128)S(1)} %stack.41.par_ref, s32[5,8,2048]{2,1,0:T(8,128)S(1)} %get-tuple-element.81.idx_ref, f32[2,2048]{1,0:T(2,128)S(1)} %copy-done.4, f32[1,2048]{1,0:T(1,128)S(1)} %add.595.slope_ref, ...), custom_call_target="tpu_custom_call", output_to_operand_aliasing={{0}: (9, {})} | custom-call | flops 1000 | bytes 1000 | tf_op jit(solution)/shard_map/pallas_call | solution.py:638
  60.9 2.3 %shard_map.80 = (f32[288,2048]{1,0:T(8,128)}, f32[4,16,128]{2,1,0:T(8,128)S(1)}) custom-call(s32[6]{0:T(128)S(1)} %stack.41.par_ref, s32[5,8,2048]{2,1,0:T(8,128)S(1)} %get-tuple-element.81.idx_ref, f32[2,2048]{1,0:T(2,128)S(1)} %copy-done.4, f32[1,2048]{1,0:T(1,128)S(1)} %add.595.slope_ref, ...), custom_call_target="tpu_custom_call", output_to_operand_aliasing={{0}: (9, {})} | custom-call | flops 1000 | bytes 1000 | tf_op jit(solution)/shard_map/pallas_call | solution.py:638
  63.2 5.7 %shard_map.81 = (f32[288,2048]{1,0:T(8,128)}, f32[4,16,128]{2,1,0:T(8,128)S(1)}) custom-call(s32[6]{0:T(128)S(1)} %stack.41.par_ref, s32[5,8,2048]{2,1,0:T(8,128)S(1)} %get-tuple-element.81.idx_ref, f32[2,2048]{1,0:T(2,128)S(1)} %copy-done.4, f32[1,2048]{1,0:T(1,128)S(1)} %add.595.slope_ref, ...), custom_call_target="tpu_custom_call", output_to_operand_aliasing={{0}: (9, {})} | custom-call | flops 1000 | bytes 1000 | tf_op jit(solution)/shard_map/pallas_call | solution.py:638
  68.9 0.5 collective-permute-done.11.beside_ref
  69.3 4.8 %shard_map.82 = (f32[288,2048]{1,0:T(8,128)}, f32[4,16,128]{2,1,0:T(8,128)S(1)}) custom-call(s32[6]{0:T(128)S(1)} %stack.41.par_ref, s32[5,8,2048]{2,1,0:T(8,128)S(1)} %get-tuple-element.81.idx_ref, f32[2,2048]{1,0:T(2,128)S(1)} %copy-done.4, f32[1,2048]{1,0:T(1,128)S(1)} %add.595.slope_ref, ...), custom_call_target="tpu_custom_call", output_to_operand_aliasing={{0}: (9, {})} | custom-call | flops 1000 | bytes 1000 | tf_op jit(solution)/shard_map/pallas_call | solution.py:638
  74.1 3.1 %shard_map.83 = (f32[288,2048]{1,0:T(8,128)}, f32[2,16,128]{2,1,0:T(8,128)S(1)}, f32[2,16,128]{2,1,0:T(8,128)S(1)}) custom-call(s32[6]{0:T(128)S(1)} %stack.41.par_ref, s32[5,8,2048]{2,1,0:T(8,128)S(1)} %get-tuple-element.81.idx_ref, f32[2,2048]{1,0:T(2,128)S(1)} %copy-done.4, f32[1,2048]{1,0:T(1,128)S(1)} %add.595.slope_ref, ...), custom_call_target="tpu_custom_call", output_to_operand_aliasing={{0}: (9, {})} | custom-call | flops 1000 | bytes 1000 | tf_op jit(solution)/shard_map/pallas_call | solution.py:638
  77.3 1.2 %collective-permute-done.13 = f32[2,16,128]{2,1,0:T(8,128)S(1)} collective-permute-done((f32[2,16,128]{2,1,0:T(8,128)S(1)}, f32[2,16,128]{2,1,0:T(8,128)S(1)}, u32[]{:S(2)}, u32[]{:S(2)}) %collective-permute-start.13) | collective-permute-done | bytes 16416 | tf_op jit(solution)/shard_map/ppermute | solution.py:653
  78.5 1.5 %collective-permute-start.14 = (f32[2,16,128]{2,1,0:T(8,128)S(1)}, f32[2,16,128]{2,1,0:T(8,128)S(1)}, u32[]{:S(2)}, u32[]{:S(2)}) collective-permute-start(f32[2,16,128]{2,1,0:T(8,128)S(1)} %add.597), channel_id=1, source_target_pairs={{0,2},{2,0},{1,3},{3,1},{4,6},{6,4},{5,7},{7,5},{8,10},{10,8},{9,1... | collective-permute-start | bytes 49160 | tf_op jit(solution)/shard_map/ppermute | solution.py:655
  79.9 2.2 %collective-permute-done.14 = f32[2,16,128]{2,1,0:T(8,128)S(1)} collective-permute-done((f32[2,16,128]{2,1,0:T(8,128)S(1)}, f32[2,16,128]{2,1,0:T(8,128)S(1)}, u32[]{:S(2)}, u32[]{:S(2)}) %collective-permute-start.14) | collective-permute-done | bytes 16416 | tf_op jit(solution)/shard_map/ppermute | solution.py:655
  82.2 2.5 %collective-permute-start.16 = (f32[2,16,128]{2,1,0:T(8,128)S(1)}, f32[2,16,128]{2,1,0:T(8,128)S(1)}, u32[]{:S(2)}, u32[]{:S(2)}) collective-permute-start(f32[2,16,128]{2,1,0:T(8,128)S(1)} %add.598.refs_0_), channel_id=1, source_target_pairs={{0,8},{4,12},{8,0},{12,4},{1,9},{5,13},{9,1},{13,5},{2,10},{6,14},... | collective-permute-start | bytes 49160 | tf_op jit(solution)/shard_map/ppermute | solution.py:660
  84.7 1.9 %collective-permute-start.17 = (f32[2,16,128]{2,1,0:T(8,128)S(1)}, f32[2,16,128]{2,1,0:T(8,128)S(1)}, u32[]{:S(2)}, u32[]{:S(2)}) collective-permute-start(f32[2,16,128]{2,1,0:T(8,128)S(1)} %add.598.refs_0_), channel_id=1, source_target_pairs={{0,12},{4,8},{8,4},{12,0},{1,13},{5,9},{9,5},{13,1},{2,14},{6,10},... | collective-permute-start | bytes 49160 | tf_op jit(solution)/shard_map/ppermute | solution.py:660
  86.6 0.3 collective-permute-done.16.refs_2_
  86.9 3.4 %collective-permute-done.17.refs_3_ = f32[2,16,128]{2,1,0:T(8,128)S(1)} collective-permute-done((f32[2,16,128]{2,1,0:T(8,128)S(1)}, f32[2,16,128]{2,1,0:T(8,128)S(1)}, u32[]{:S(2)}, u32[]{:S(2)}) %collective-permute-start.17) | collective-permute-done | bytes 16416 | tf_op jit(solution)/shard_map/ppermute | solution.py:660
  90.3 1.2 %shard_map.84 = (f32[1,1024]{1,0:T(1,128)}, f32[1,1024]{1,0:T(1,128)}) custom-call(s32[1,1024]{1,0:T(1,128)S(1)} %bitcast.127, s32[1,1024]{1,0:T(1,128)S(1)} %bitcast.126, f32[2,16,128]{2,1,0:T(8,128)S(1)} %add.598.refs_0_, f32[2,16,128]{2,1,0:T(8,128)S(1)} %collective-permute-done.15.refs_1_, f32[2,16,128]{2,1,0:T(8,128)S(1)} %collective-permute-done.16.refs_2_, ...), custom_call_target="tpu_custom_call" | custom-call | flops 1000 | bytes 1000 | tf_op jit(solution)/shard_map/pallas_call | solution.py:669
  (52 shorter events, 0.8 us)
Async XLA Ops:
  0.6 52.2 %copy-start.4 = (f32[2,2048]{1,0:T(2,128)S(1)}, f32[2,2048]{1,0:T(2,128)}, u32[]{:S(2)}) copy-start(f32[2,2048]{1,0:T(2,128)} %wind_ref.11) | copy-start | bytes 49156
  2.7 15.2 %collective-permute-start.2 = (f32[48,2048]{1,0:T(8,128)}, f32[48,2048]{1,0:T(8,128)S(1)}, u32[]{:S(2)}, u32[]{:S(2)}) collective-permute-start(f32[48,2048]{1,0:T(8,128)} %bitcast.53), channel_id=1, source_target_pairs={{0,4},{1,13},{4,8},{5,1},{8,12},{9,5},{12,0},{13,9},{2,6},{3,15},{... | collective-permute-start | bytes 1179656 | tf_op jit(solution)/shard_map/ppermute | solution.py:566
  5.7 20.6 %collective-permute-start.5 = (f32[48,2048]{1,0:T(8,128)}, f32[48,2048]{1,0:T(8,128)S(1)}, u32[]{:S(2)}, u32[]{:S(2)}) collective-permute-start(f32[48,2048]{1,0:T(8,128)} %bitcast.54), channel_id=1, source_target_pairs={{0,4},{1,13},{4,8},{5,1},{8,12},{9,5},{12,0},{13,9},{2,6},{3,15},{... | collective-permute-start | bytes 1179656 | tf_op jit(solution)/shard_map/ppermute | solution.py:566
  17.9 16.1 %collective-permute-start.6 = (f32[24,2048]{1,0:T(8,128)S(1)}, f32[24,2048]{1,0:T(8,128)S(1)}, u32[]{:S(2)}, u32[]{:S(2)}) collective-permute-start(f32[24,2048]{1,0:T(8,128)S(1)} %get-tuple-element.89), channel_id=1, source_target_pairs={{0,4},{1,13},{4,8},{5,1},{8,12},{9,5},{12,0},{13,9},{2,6},{3,15},{... | collective-permute-start | bytes 589832 | tf_op jit(solution)/shard_map/ppermute | solution.py:566
  18.4 15.6 %collective-permute-start.3 = (f32[296,128]{1,0:T(8,128)S(1)}, f32[296,128]{1,0:T(8,128)S(1)}, u32[]{:S(2)}, u32[]{:S(2)}) collective-permute-start(f32[296,128]{1,0:T(8,128)S(1)} %get-tuple-element.86), channel_id=1, source_target_pairs={{0,8},{1,9},{4,12},{5,13},{8,0},{9,1},{12,4},{13,5},{2,10},{3,11},... | collective-permute-start | bytes 454664 | tf_op jit(solution)/shard_map/ppermute | solution.py:566
  19.9 14.1 %collective-permute-start.4 = (f32[296,128]{1,0:T(8,128)S(1)}, f32[296,128]{1,0:T(8,128)S(1)}, u32[]{:S(2)}, u32[]{:S(2)}) collective-permute-start(f32[296,128]{1,0:T(8,128)S(1)} %get-tuple-element.87), channel_id=1, source_target_pairs={{0,12},{1,5},{4,0},{5,9},{8,4},{9,13},{12,8},{13,1},{2,14},{3,7},{... | collective-permute-start | bytes 454664 | tf_op jit(solution)/shard_map/ppermute | solution.py:566
  34.0 29.2 %collective-permute-start.12 = (f32[80,2048]{1,0:T(8,128)}, f32[80,2048]{1,0:T(8,128)S(1)}, u32[]{:S(2)}, u32[]{:S(2)}) collective-permute-start(f32[80,2048]{1,0:T(8,128)} %get-tuple-element.98), channel_id=1, source_target_pairs={{0,4},{1,13},{4,8},{5,1},{8,12},{9,5},{12,0},{13,9},{2,6},{3,15},{... | collective-permute-start | bytes 1966088 | tf_op jit(solution)/shard_map/ppermute | solution.py:566
  39.4 29.9 %collective-permute-start.11 = (f32[64,2048]{1,0:T(8,128)}, f32[64,2048]{1,0:T(8,128)S(1)}, u32[]{:S(2)}, u32[]{:S(2)}) collective-permute-start(f32[64,2048]{1,0:T(8,128)} %get-tuple-element.97), channel_id=1, source_target_pairs={{0,4},{1,13},{4,8},{5,1},{8,12},{9,5},{12,0},{13,9},{2,6},{3,15},{... | collective-permute-start | bytes 1572872 | tf_op jit(solution)/shard_map/ppermute | solution.py:566
  40.3 33.8 %collective-permute-start.10 = (f32[32,2048]{1,0:T(8,128)S(1)}, f32[32,2048]{1,0:T(8,128)S(1)}, u32[]{:S(2)}, u32[]{:S(2)}) collective-permute-start(f32[32,2048]{1,0:T(8,128)S(1)} %get-tuple-element.96), channel_id=1, source_target_pairs={{0,4},{1,13},{4,8},{5,1},{8,12},{9,5},{12,0},{13,9},{2,6},{3,15},{... | collective-permute-start | bytes 786440 | tf_op jit(solution)/shard_map/ppermute | solution.py:566
  44.4 1.2 %collective-permute-start.7 = (f32[1,2048]{1,0:T(1,128)S(1)}, f32[1,2048]{1,0:T(1,128)S(1)}, u32[]{:S(2)}, u32[]{:S(2)}) collective-permute-start(f32[1,2048]{1,0:T(1,128)S(1)} %shard_map.77), channel_id=1, source_target_pairs={{0,1},{1,0},{2,3},{3,2},{4,5},{5,4},{6,7},{7,6},{8,9},{9,8},{10,11... | collective-permute-start | bytes 24584 | tf_op jit(solution)/shard_map/ppermute | solution.py:616
  45.6 7.2 %collective-permute-start.8 = (f32[1,2048]{1,0:T(1,128)S(1)}, f32[1,2048]{1,0:T(1,128)S(1)}, u32[]{:S(2)}, u32[]{:S(2)}) collective-permute-start(f32[1,2048]{1,0:T(1,128)S(1)} %add.594), channel_id=1, source_target_pairs={{0,2},{2,0},{1,3},{3,1},{4,6},{6,4},{5,7},{7,5},{8,10},{10,8},{9,1... | collective-permute-start | bytes 24584 | tf_op jit(solution)/shard_map/ppermute | solution.py:618
  47.8 3.8 %collective-permute-start.9 = (f32[1,1]{1,0:T(1,128)}, f32[1,1]{1,0:T(1,128)}, u32[]{:S(2)}, u32[]{:S(2)}) collective-permute-start(f32[1,1]{1,0:T(1,128)} %bitcast.56), channel_id=1, source_target_pairs={{0,16},{16,0},{1,17},{17,1},{2,18},{18,2},{3,19},{19,3},{4,20},{20... | collective-permute-start | bytes 20 | tf_op jit(solution)/shard_map/ppermute | solution.py:608
  74.1 12.5 %copy-start.5 = (s32[1024]{0:T(1024)S(1)}, s32[1024]{0:T(1024)}, u32[]{:S(2)}) copy-start(s32[1024]{0:T(1024)} %param.13) | copy-start | bytes 12292
  74.1 12.5 %copy-start.6 = (s32[1024]{0:T(1024)S(1)}, s32[1024]{0:T(1024)}, u32[]{:S(2)}) copy-start(s32[1024]{0:T(1024)} %param.12) | copy-start | bytes 12292
  74.1 17.4 %copy-start.3 = (s32[128,128]{1,0:T(8,128)S(1)}, s32[128,128]{1,0:T(8,128)}, u32[]{:S(2)}) copy-start(s32[128,128]{1,0:T(8,128)} %cell_ref.1) | copy-start | bytes 196612
  77.3 1.2 %collective-permute-start.13 = (f32[2,16,128]{2,1,0:T(8,128)S(1)}, f32[2,16,128]{2,1,0:T(8,128)S(1)}, u32[]{:S(2)}, u32[]{:S(2)}) collective-permute-start(f32[2,16,128]{2,1,0:T(8,128)S(1)} %get-tuple-element.113), channel_id=1, source_target_pairs={{0,1},{1,0},{2,3},{3,2},{4,5},{5,4},{6,7},{7,6},{8,9},{9,8},{10,11... | collective-permute-start | bytes 49160 | tf_op jit(solution)/shard_map/ppermute | solution.py:653
  78.5 3.7 %collective-permute-start.14 = (f32[2,16,128]{2,1,0:T(8,128)S(1)}, f32[2,16,128]{2,1,0:T(8,128)S(1)}, u32[]{:S(2)}, u32[]{:S(2)}) collective-permute-start(f32[2,16,128]{2,1,0:T(8,128)S(1)} %add.597), channel_id=1, source_target_pairs={{0,2},{2,0},{1,3},{3,1},{4,6},{6,4},{5,7},{7,5},{8,10},{10,8},{9,1... | collective-permute-start | bytes 49160 | tf_op jit(solution)/shard_map/ppermute | solution.py:655
  82.2 4.4 %collective-permute-start.15 = (f32[2,16,128]{2,1,0:T(8,128)S(1)}, f32[2,16,128]{2,1,0:T(8,128)S(1)}, u32[]{:S(2)}, u32[]{:S(2)}) collective-permute-start(f32[2,16,128]{2,1,0:T(8,128)S(1)} %add.598.refs_0_), channel_id=1, source_target_pairs={{0,4},{4,0},{8,12},{12,8},{1,5},{5,1},{9,13},{13,9},{2,6},{6,2},{1... | collective-permute-start | bytes 49160 | tf_op jit(solution)/shard_map/ppermute | solution.py:660
  82.2 4.7 %collective-permute-start.16 = (f32[2,16,128]{2,1,0:T(8,128)S(1)}, f32[2,16,128]{2,1,0:T(8,128)S(1)}, u32[]{:S(2)}, u32[]{:S(2)}) collective-permute-start(f32[2,16,128]{2,1,0:T(8,128)S(1)} %add.598.refs_0_), channel_id=1, source_target_pairs={{0,8},{4,12},{8,0},{12,4},{1,9},{5,13},{9,1},{13,5},{2,10},{6,14},... | collective-permute-start | bytes 49160 | tf_op jit(solution)/shard_map/ppermute | solution.py:660
  84.7 5.5 %collective-permute-start.17 = (f32[2,16,128]{2,1,0:T(8,128)S(1)}, f32[2,16,128]{2,1,0:T(8,128)S(1)}, u32[]{:S(2)}, u32[]{:S(2)}) collective-permute-start(f32[2,16,128]{2,1,0:T(8,128)S(1)} %add.598.refs_0_), channel_id=1, source_target_pairs={{0,12},{4,8},{8,4},{12,0},{1,13},{5,9},{9,5},{13,1},{2,14},{6,10},... | collective-permute-start | bytes 49160 | tf_op jit(solution)/shard_map/ppermute | solution.py:660

commit v5 on v4

--- a/solution.py
+++ b/solution.py
@@ -169,6 +169,7 @@
 C_KEEP, C_ROW, C_COL, C_SLOPE, C_EAST, C_NORTH, C_ONE, C_DAMP = range(8)
 C_S_EAST, C_S_NORTH, C_T_EAST, C_T_NORTH = range(8, 12)
 CHUNK_ENDS = (3, 6, 7, 12, 16)
+FOURTH_EARLY = True
 VMEM_BYTES = 24 * 1024 * 1024
 
 
@@ -276,9 +277,8 @@
             sum_ref[at : at + 1, :] += jnp.sum(
                 weighted * coef_ref[rows, column_of : column_of + 1], axis=0, keepdims=True
             )
-    lanes_all = (owners - 2) * 2 * LANES
-    entry = lax.broadcasted_iota(I32, (lanes_all, slots), 0)
-    packed, sums = [], []
+    entry = lax.broadcasted_iota(I32, (2 * LANES, slots), 0)
+    keys = []
     for half in range(2):
         receive, send = [
             jnp.sum(
@@ -300,20 +300,26 @@
         place = jnp.where(send >= LANES, 3 * LANES - 1 - send, send)
         place = jnp.where(send >= 2 * LANES, -1, place)
         key = jnp.where((away > 1) & (place >= 0), (away - 2) * 2 * LANES + place, -1)
-        one_hot = jnp.where(entry == key, 1.0, 0.0).astype(BF16)
-        rows = slice(half * half_rows, (half + 1) * half_rows)
-        packed.append(times_hot(g_ref[rows, :], one_hot, ((1,), (1,)), 2))
-        sums.append(times_hot(sum_ref[...], one_hot, ((1,), (1,))))
+        keys.append(key)
     for at, list_ref in enumerate(list_refs):
-        inner = slice(2 * at * LANES, (2 * at + 1) * LANES)
-        outer = slice((2 * at + 1) * LANES, (2 * at + 2) * LANES)
         for half in range(2):
+            one_hot = jnp.where(entry == keys[half] - at * 2 * LANES, 1.0, 0.0).astype(BF16)
             rows = slice(half * half_rows, (half + 1) * half_rows)
-            list_ref[rows, :] = packed[half][:, inner] + packed[1 - half][:, outer]
-            row, other = 1 + half, 2 - half
-            list_ref[2 * half_rows + half : 2 * half_rows + half + 1, :] = (
-                sums[half][row : row + 1, inner] + sums[1 - half][other : other + 1, outer]
-            )
+            packed = times_hot(g_ref[rows, :], one_hot, ((1,), (1,)), 2)
+            sums = times_hot(sum_ref[...], one_hot, ((1,), (1,)))[1 + half : 2 + half]
+            other = slice((1 - half) * half_rows, (2 - half) * half_rows)
+            own_row = slice(2 * half_rows + half, 2 * half_rows + half + 1)
+            other_row = slice(2 * half_rows + 1 - half, 2 * half_rows + 2 - half)
+            if half == 0:
+                list_ref[rows, :] = packed[:, :LANES]
+                list_ref[other, :] = packed[:, LANES:]
+                list_ref[own_row, :] = sums[:, :LANES]
+                list_ref[other_row, :] = sums[:, LANES:]
+            else:
+                list_ref[rows, :] += packed[:, :LANES]
+                list_ref[other, :] += packed[:, LANES:]
+                list_ref[own_row, :] += sums[:, :LANES]
+                list_ref[other_row, :] += sums[:, LANES:]
     chunk_refs[0][-8:, :] = sum_ref[...]
     for start, chunk_ref in zip(starts, chunk_refs):
         count = chunk_ref.shape[0] - (8 if start == starts[0] else 0)
@@ -327,10 +333,10 @@
     return jnp.take_along_axis(values, lanes, axis=1)
 
 
-def row_neighbour(code, lanes, sources):
+def row_neighbour(code, lanes, sources, places=range(4)):
     value = jnp.zeros(code.shape, F32)
-    for number, source in enumerate(sources):
-        value = jnp.where(code == 1 + number, lane_take(source, lanes), value)
+    for place, source in zip(places, sources):
+        value = jnp.where(code == 1 + place, lane_take(source, lanes), value)
     return value
 
 
@@ -377,69 +383,84 @@
         slope_ref[:, at] = slope + jnp.where(idx_ref[4, 0:1, at] > 0, column[3:4], 0.0)
 
 
-def step_kernel(owners, first_step, half_steps, chained, final, par_ref, idx_ref, wind_ref, slope_ref, coef_ref, g_ref, beside_ref, *refs):
+def step_kernel(owners, parts, half_steps, chained, final, par_ref, spill_ref, idx_ref, wind_ref, slope_ref, coef_ref, g_ref, *refs):
+    beside_refs, refs = refs[: len(parts)], refs[len(parts) :]
     list_refs, refs = refs[: owners - 2], refs[owners - 2 :]
     if chained:
         _, before_ref, refs = refs[0], refs[1], refs[2:]
     out_ref, sums_refs, total_ref, damp_ref = refs[0], refs[1:-2], refs[-2], refs[-1]
     blocks = g_ref.shape[1] // LANES
     shape = (8, LANES)
-    half = jnp.where(pl.program_id(0) + first_step >= half_steps, 1, 0)
+    step = pl.program_id(0)
+    step_rows = out_ref.shape[0]
+    first_step = parts[0][0]
+    half = jnp.where(step + first_step >= half_steps, 1, 0)
     way, turn = par_ref[1 + half], par_ref[3]
-    beside_lanes, beyond = turned_lanes(turn)
-
-    @pl.when(pl.program_id(0) == 0)
+    lane = lax.broadcasted_iota(I32, shape, 1)
+    turned = (lane + turn) & (LANES - 1)
+    edge = lane == jnp.where(turn < 0, LANES - 1, jnp.where(turn > 0, 0, -1))
+
+    @pl.when(step == 0)
     def _():
         total_ref[...] = jnp.zeros_like(total_ref)
         slope = slope_ref[...]
         damp_ref[...] = jnp.broadcast_to(slope * slope, damp_ref.shape)
 
-    for tile in range(out_ref.shape[0] // 8):
-        here = slice(tile * 8, tile * 8 + 8)
-        first = pl.program_id(0) * out_ref.shape[0] + tile * 8
-        near_rows = pl.ds(pl.multiple_of(first, 8), 8)
-        rows = pl.ds(pl.multiple_of(first + first_step * out_ref.shape[0], 8), 8)
-        half_rows = half_steps * out_ref.shape[0]
-        other_rows = pl.ds(
-            pl.multiple_of(first + first_step * out_ref.shape[0] + (1 - 2 * half) * half_rows, 8), 8
-        )
-        coef = coef_ref[rows, :]
-
-        def factor(at):
-            return jnp.broadcast_to(coef[:, at : at + 1], shape)
-
-        keep, by_row, by_col = factor(C_KEEP), factor(C_ROW), factor(C_COL)
-        east, north, one, damp = factor(C_EAST), factor(C_NORTH), factor(C_ONE), factor(C_DAMP)
-        s_east, s_north = factor(C_S_EAST), factor(C_S_NORTH)
-        t_east, t_north = factor(C_T_EAST), factor(C_T_NORTH)
-        lists = [ref[which, :] for ref in list_refs for which in (rows, other_rows)]
-        for block in range(blocks):
-            at = slice(block * LANES, (block + 1) * LANES)
-            lanes, code = idx_ref[2 * half, :, at], idx_ref[2 * half + 1, :, at]
-            has_beside = idx_ref[4, :, at]
-            own, beside = g_ref[here, at], beside_ref[near_rows, at]
-            sources = [own, near_block(g_ref, here, block, way)]
-            sources += [beside, near_block(beside_ref, near_rows, block, way)]
-            row_value = row_neighbour(code, lanes, sources + lists)
-            col_value = jnp.where(
-                beyond,
-                lane_take(near_block(beside_ref, near_rows, block, turn), beside_lanes),
-                lane_take(beside, beside_lanes),
-            )
-            col_value = jnp.where(has_beside > 0, col_value, 0.0)
-            value = keep * own + by_row * row_value + by_col * col_value
-            wind_east = jnp.broadcast_to(wind_ref[0:1, at], shape)
-            wind_north = jnp.broadcast_to(wind_ref[1:2, at], shape)
-            growth = jnp.maximum(east * wind_east + north * wind_north - one, 0.0)
-            updated = value * jnp.exp(growth - damp * damp_ref[:, at])
-            out_ref[here, at] = updated
-            lifted = growth * value
-            total_ref[0, :, at] += s_east * lifted
-            total_ref[1, :, at] += s_north * lifted
-            total_ref[2, :, at] += t_east * updated
-            total_ref[3, :, at] += t_north * updated
-
-    @pl.when(pl.program_id(0) == pl.num_programs(0) - 1)
+    def tiles(beside_ref, spills):
+        for tile in range(step_rows // 8):
+            here = slice(tile * 8, tile * 8 + 8)
+
+            def at_row(first):
+                return pl.ds(pl.multiple_of(first, 8), 8)
+
+            first = (step + first_step) * step_rows + tile * 8
+            rows = at_row(first)
+            other_rows = at_row(first + (1 - 2 * half) * half_steps * step_rows)
+            coef = coef_ref[rows, :]
+
+            def factor(at):
+                return jnp.broadcast_to(coef[:, at : at + 1], shape)
+
+            keep, by_row, by_col = factor(C_KEEP), factor(C_ROW), factor(C_COL)
+            east, north, one, damp = factor(C_EAST), factor(C_NORTH), factor(C_ONE), factor(C_DAMP)
+            s_east, s_north = factor(C_S_EAST), factor(C_S_NORTH)
+            t_east, t_north = factor(C_T_EAST), factor(C_T_NORTH)
+            sides = (rows, other_rows) if spills else (rows,)
+            lists = [ref[which, :] for ref in list_refs for which in sides]
+            places = list(range(4))
+            places += [4 + 2 * at + side for at in range(owners - 2) for side in range(len(sides))]
+            for block in range(blocks):
+                at = slice(block * LANES, (block + 1) * LANES)
+                lanes, code = idx_ref[2 * half, :, at], idx_ref[2 * half + 1, :, at]
+                has_beside = idx_ref[4, :, at]
+                own, beside = g_ref[here, at], beside_ref[here, at]
+                sources = [own, near_block(g_ref, here, block, way)]
+                sources += [beside, near_block(beside_ref, here, block, way)]
+                row_value = row_neighbour(code, lanes, sources + lists, places)
+                turning = near_block(beside_ref, here, block, turn)
+                col_value = lane_take(jnp.where(edge, turning, beside), turned)
+                col_value = jnp.where(has_beside > 0, col_value, 0.0)
+                value = keep * own + by_row * row_value + by_col * col_value
+                wind_east = jnp.broadcast_to(wind_ref[0:1, at], shape)
+                wind_north = jnp.broadcast_to(wind_ref[1:2, at], shape)
+                growth = jnp.maximum(east * wind_east + north * wind_north - one, 0.0)
+                updated = value * jnp.exp(growth - damp * damp_ref[:, at])
+                out_ref[here, at] = updated
+                lifted = growth * value
+                total_ref[0, :, at] += s_east * lifted
+                total_ref[1, :, at] += s_north * lifted
+                total_ref[2, :, at] += t_east * updated
+                total_ref[3, :, at] += t_north * updated
+
+    for (start, stop), beside_ref in zip(parts, beside_refs):
+        for spills in (False, True):
+            inside = (step >= start - first_step) & (step < stop - first_step)
+
+            @pl.when(inside & ((spill_ref[0] > 0) == spills))
+            def _():
+                tiles(beside_ref, spills)
+
+    @pl.when(step == pl.num_programs(0) - 1)
     def _():
         cpl = par_ref[4]
         for item in range(2):
@@ -569,7 +590,9 @@
         return values[at[0] * step_rows : at[1] * step_rows]
 
     chunks = chunks_of(steps)
-    beside = [around(chunk(field, at)) for at in chunks[:2]]
+    first = chunk(field, chunks[0])
+    rest, first = lax.optimization_barrier((field, first))
+    beside = [around(first), around(chunk(rest, chunks[1]))]
 
     first_way = 2 * my_cpl - 1
     turn = jnp.where(
@@ -598,16 +621,22 @@
     (idx, counts, row_sums), lists = found[:3], found[3 : owners + 1]
     leaving = found[owners + 1 :]
     arrived = [around(values, 2 + at) for at, values in enumerate(lists)]
-    beside.append(around(leaving[0]))
-    later, arrived, beside = lax.optimization_barrier((leaving[1:], arrived, beside))
-    beside += [around(values) for values in later]
-
     pairs = jnp.sum(counts, axis=1).reshape(owners, owners)
+    spills = jnp.where(jnp.max(pairs) > LANES, 1, 0).astype(I32).reshape(1)
     longest = jnp.max(pairs + pairs.T).reshape(1, 1)
     if groups == 2:
         longest = jnp.maximum(longest, lax.ppermute(longest, "grp", [(0, 1), (1, 0)]))
     else:
         longest = lax.pmax(longest, "grp")
+    beside.append(around(leaving[0]))
+    later = list(leaving[1:])
+    if FOURTH_EARLY:
+        later[0], beside[1] = lax.optimization_barrier((later[0], beside[1]))
+        beside.append(around(later.pop(0)))
+    later, arrived, beside[2], longest, spills = lax.optimization_barrier(
+        (later, arrived, beside[2], longest, spills)
+    )
+    beside += [around(values) for values in later]
 
     (slope_part,) = call(
         slope_kernel, [SCALARS] + [WHOLE] * (owners + 1), [shape_of(1, slots)]
@@ -619,16 +648,21 @@
     else:
         slope = lax.psum(slope, "spec")
 
-    slope, longest = lax.optimization_barrier((slope, longest))
     updated = sums = None
-    for at, near in zip(chunks, beside):
-        start, stop = at
+    for parts in [chunks[:3]] + [[at] for at in chunks[3:]]:
+        start, stop = parts[0][0], parts[-1][1]
         chained, final = start > 0, stop == steps
-        in_rows = lambda width: pl.BlockSpec(
-            (step_rows, width), functools.partial(lambda first, i: (first + i, 0), start)
+        in_rows = pl.BlockSpec(
+            (step_rows, slots), functools.partial(lambda first, i: (first + i, 0), start)
         )
-        inputs = [par, idx, wind_deck, slope, coef, field, near, *arrived]
-        specs = [SCALARS] + [WHOLE] * 4 + [in_rows(slots)] + [WHOLE] * (owners - 1)
+        near, beside = beside[: len(parts)], beside[len(parts) :]
+        inputs = [par, spills, idx, wind_deck, slope, coef, field, *near, *arrived]
+        specs = [SCALARS] * 2 + [WHOLE] * 4 + [in_rows]
+        for first, end in parts:
+            within = lambda skipped, most, i: (jnp.clip(i - skipped, 0, most), 0)
+            within = functools.partial(within, first - start, end - first - 1)
+            specs.append(pl.BlockSpec((step_rows, slots), within))
+        specs += [WHOLE] * len(arrived)
         aliases = {}
         if chained:
             aliases = {len(inputs): 0}
@@ -636,10 +670,10 @@
             specs += [pl.BlockSpec(memory_space=pl.ANY), WHOLE]
         sum_shapes = [(2, blocks, LANES)] * 2 if final else [(4, blocks, LANES)]
         updated, *sums = pl.pallas_call(
-            functools.partial(step_kernel, owners, start, steps // 2, chained, final),
+            functools.partial(step_kernel, owners, parts, steps // 2, chained, final),
             grid=(stop - start,),
             in_specs=specs,
-            out_specs=[in_rows(slots)] + [WHOLE] * len(sum_shapes),
+            out_specs=[in_rows] + [WHOLE] * len(sum_shapes),
             out_shape=[pltpu.HBM((rows, slots), F32)] + [shape_of(*dims) for dims in sum_shapes],
             scratch_shapes=[pltpu.VMEM((4, 8, slots), F32), pltpu.VMEM((8, slots), F32)],
             input_output_aliases=aliases,

time: 92 us -> 88.8 us (0.965)
  Pallas kernels: 33.9 us -> 29.4 us
  waiting for transfers between devices: 24.1 us -> 20.3 us
  local copies, waits for them, and re-layouts: 3.64 us -> 5.91 us
  starting transfers between devices: 26.8 us -> 28.4 us
    ppermute x8, waiting for transfers between devices: 13.8 us -> 8.39 us  [around(): return lax.ppermute(values, ('pts', 'cpl'), pairs)]
    pallas_call x6 -> x4, Pallas kernels: 23.9 us -> 19.8 us  [local(): pl.pallas_call(functools.partial(step_kernel, owners, parts, steps // 2,...]
    ppermute x3, starting transfers between devices: 4.38 us -> 8 us  [local(): lax.ppermute(mine, 'pts', [(i, i ^ turned) for i in range(owners)])]
    ppermute x1, waiting for transfers between devices: 0.01 us -> 2.15 us  [local(): slope = slope + lax.ppermute(slope, 'spec', [(0, 1), (1, 0)])]
    ppermute x8, starting transfers between devices: 17.8 us -> 15.8 us  [around(): return lax.ppermute(values, ('pts', 'cpl'), pairs)]
    slice x1 -> x2, local copies, waits for them, and re-layouts: 2.07 us -> 3.55 us  [chunk(): return values[at[0] * step_rows:at[1] * step_rows]]
    ppermute x1, waiting for transfers between devices: 2.26 us -> 1 us  [local(): lax.ppermute(longest, 'grp', [(0, 1), (1, 0)])]
  transfers between devices with their start and end apart: 16 -> 16, of which waited for: 10 -> 11; matrix products, arithmetic and copies ran while one was open for 3% -> 6% of each run, Pallas kernels for 32% -> 29%
where the time goes in v5:
time: 88.8 us; the launch traced here: 88.3 us
  Pallas kernels  29.4 us (33%)
  starting transfers between devices  28.4 us (32%)
  waiting for transfers between devices  20.3 us (23%)
  local copies, waits for them, and re-layouts  5.91 us (7%)
  between operations  2.71 us (3%)
  other arithmetic  1.56 us (2%)
    pallas_call x4, Pallas kernels, local(): pl.pallas_call(functools.partial(step_kernel, owners, parts, steps // 2,...  19.8 us
    ppermute x8, starting transfers between devices, around(): return lax.ppermute(values, ('pts', 'cpl'), pairs)  15.8 us
    ppermute x8, waiting for transfers between devices, around(): return lax.ppermute(values, ('pts', 'cpl'), pairs)  8.39 us
    ppermute x3, starting transfers between devices, local(): lax.ppermute(mine, 'pts', [(i, i ^ turned) for i in range(owners)])  8 us
    pallas_call x1, Pallas kernels, local(): call(functools.partial(index_kernel, owners, [start * step_rows for start...  7.36 us
    ppermute x3, waiting for transfers between devices, local(): lax.ppermute(mine, 'pts', [(i, i ^ turned) for i in range(owners)])  4.12 us
    slice x2, local copies, waits for them, and re-layouts, chunk(): return values[at[0] * step_rows:at[1] * step_rows]  3.55 us
    ppermute x1, waiting for transfers between devices, local(): mine = mine + lax.ppermute(mine, 'spec', [(0, 1), (1, 0)])  2.25 us
  transfers between devices with their start and end apart: 16, of which 11 were waited for; matrix products, arithmetic and copies ran while one was open for 6% of the time, Pallas kernels for 29%

profile of v5, /device:TPU:0, one launch (start us, length us, event | category | flops | bytes accessed | tf_op | source)
XLA Modules:
  0.0 88.3 jit_solution(3781896131439904391)
XLA Ops:
  0.6 1.8 %slice.116 = f32[3,16,2048]{2,1,0:T(8,128)} slice(f32[18,16,2048]{2,1,0:T(8,128)} %bitcast.51), slice={[0:3], [0:16], [0:2048]} | slice | bytes 786432 | tf_op jit(solution)/shard_map/slice | solution.py:590
  2.4 3.0 %collective-permute-start.2 = (f32[48,2048]{1,0:T(8,128)}, f32[48,2048]{1,0:T(8,128)S(1)}, u32[]{:S(2)}, u32[]{:S(2)}) collective-permute-start(f32[48,2048]{1,0:T(8,128)} %bitcast.54), channel_id=1, source_target_pairs={{0,4},{1,13},{4,8},{5,1},{8,12},{9,5},{12,0},{13,9},{2,6},{3,15},{... | collective-permute-start | bytes 1179656 | tf_op jit(solution)/shard_map/ppermute | solution.py:587
  5.4 1.8 %slice.46 = f32[48,2048]{1,0:T(8,128)} slice(f32[288,2048]{1,0:T(8,128)} %bitcast.52.g_ref), slice={[48:96], [0:2048]} | slice | bytes 786432 | tf_op jit(solution)/shard_map/slice | solution.py:590
  7.2 1.6 %collective-permute-start.11 = (f32[48,2048]{1,0:T(8,128)}, f32[48,2048]{1,0:T(8,128)S(1)}, u32[]{:S(2)}, u32[]{:S(2)}) collective-permute-start(f32[48,2048]{1,0:T(8,128)} %slice.46), channel_id=1, source_target_pairs={{0,4},{1,13},{4,8},{5,1},{8,12},{9,5},{12,0},{13,9},{2,6},{3,15},{... | collective-permute-start | bytes 1179656 | tf_op jit(solution)/shard_map/ppermute | solution.py:587
  9.0 0.1 mul.605
  9.2 0.1 mul.608
  9.3 0.1 mul.602
  9.5 0.1 mul.615
  9.8 0.1 stack_broadcast_in_dim.51
  10.0 0.1 stack_broadcast_in_dim.53
  10.2 0.1 copy.44
  10.4 0.1 stack.41.par_ref
  10.5 7.4 %shard_map.76 = (s32[5,8,2048]{2,1,0:T(8,128)S(1)}, f32[16,128]{1,0:T(8,128)S(1)}, f32[8,2048]{1,0:T(8,128)S(1)}, f32[296,128]{1,0:T(8,128)}, f32[296,128]{1,0:T...) custom-call(s32[6]{0:T(128)S(1)} %stack.41.par_ref, ...), custom_call_target="tpu_custom_call" | custom-call | flops 1000 | bytes 1000 | tf_op jit(solution)/shard_map/pallas_call | solution.py:606
  17.9 0.8 copy-done
  18.6 1.6 %collective-permute-start.5 = (f32[24,2048]{1,0:T(8,128)}, f32[24,2048]{1,0:T(8,128)S(1)}, u32[]{:S(2)}, u32[]{:S(2)}) collective-permute-start(f32[24,2048]{1,0:T(8,128)} %get-tuple-element.83), channel_id=1, source_target_pairs={{0,4},{1,13},{4,8},{5,1},{8,12},{9,5},{12,0},{13,9},{2,6},{3,15},{... | collective-permute-start | bytes 589832 | tf_op jit(solution)/shard_map/ppermute | solution.py:587
  20.2 1.2 %collective-permute-start.3 = (f32[296,128]{1,0:T(8,128)}, f32[296,128]{1,0:T(8,128)S(1)}, u32[]{:S(2)}, u32[]{:S(2)}) collective-permute-start(f32[296,128]{1,0:T(8,128)} %get-tuple-element.81), channel_id=1, source_target_pairs={{0,8},{1,9},{4,12},{5,13},{8,0},{9,1},{12,4},{13,5},{2,10},{3,11},... | collective-permute-start | bytes 454664 | tf_op jit(solution)/shard_map/ppermute | solution.py:587
  21.5 1.1 %collective-permute-start.4 = (f32[296,128]{1,0:T(8,128)}, f32[296,128]{1,0:T(8,128)S(1)}, u32[]{:S(2)}, u32[]{:S(2)}) collective-permute-start(f32[296,128]{1,0:T(8,128)} %get-tuple-element.82), channel_id=1, source_target_pairs={{0,12},{1,5},{4,0},{5,9},{8,4},{9,13},{12,8},{13,1},{2,14},{3,7},{... | collective-permute-start | bytes 454664 | tf_op jit(solution)/shard_map/ppermute | solution.py:587
  22.6 3.4 %collective-permute-done.11.refs_1_ = f32[48,2048]{1,0:T(8,128)S(1)} collective-permute-done((f32[48,2048]{1,0:T(8,128)}, f32[48,2048]{1,0:T(8,128)S(1)}, u32[]{:S(2)}, u32[]{:S(2)}) %collective-permute-start.11) | collective-permute-done | bytes 393248 | tf_op jit(solution)/shard_map/ppermute | solution.py:587
  26.0 1.1 %collective-permute-start.12 = (f32[80,2048]{1,0:T(8,128)S(1)}, f32[80,2048]{1,0:T(8,128)S(1)}, u32[]{:S(2)}, u32[]{:S(2)}) collective-permute-start(f32[80,2048]{1,0:T(8,128)S(1)} %get-tuple-element.96), channel_id=1, source_target_pairs={{0,4},{1,13},{4,8},{5,1},{8,12},{9,5},{12,0},{13,9},{2,6},{3,15},{... | collective-permute-start | bytes 1966088 | tf_op jit(solution)/shard_map/ppermute | solution.py:587
  27.1 0.1 reduce_sum.85
  27.2 0.1 reshape.1211
  27.3 0.1 copy.40
  27.4 0.6 fusion.52
  28.0 1.5 %collective-permute-start.6 = (f32[1,1]{1,0:T(1,128)}, f32[1,1]{1,0:T(1,128)}, u32[]{:S(2)}, u32[]{:S(2)}) collective-permute-start(f32[1,1]{1,0:T(1,128)} %bitcast.56), channel_id=1, source_target_pairs={{0,16},{16,0},{1,17},{17,1},{2,18},{18,2},{3,19},{19,3},{4,20},{20... | collective-permute-start | bytes 20 | tf_op jit(solution)/shard_map/ppermute | solution.py:628
  29.5 0.6 reduce_max.19
  30.8 1.0 %collective-permute-done.6 = f32[1,1]{1,0:T(1,128)} collective-permute-done((f32[1,1]{1,0:T(1,128)}, f32[1,1]{1,0:T(1,128)}, u32[]{:S(2)}, u32[]{:S(2)}) %collective-permute-start.6) | collective-permute-done | bytes 36 | tf_op jit(solution)/shard_map/ppermute | solution.py:628
  33.0 2.8 %collective-permute-done.3.refs_0_.refs_3_.refs_1_ = f32[296,128]{1,0:T(8,128)S(1)} collective-permute-done((f32[296,128]{1,0:T(8,128)}, f32[296,128]{1,0:T(8,128)S(1)}, u32[]{:S(2)}, u32[]{:S(2)}) %collective-permute-start.3) | collective-permute-done | bytes 151584 | tf_op jit(solution)/shard_map/ppermute | solution.py:587
  35.9 6.1 %collective-permute-start.10 = (f32[64,2048]{1,0:T(8,128)}, f32[64,2048]{1,0:T(8,128)S(1)}, u32[]{:S(2)}, u32[]{:S(2)}) collective-permute-start(f32[64,2048]{1,0:T(8,128)} %copy-done), channel_id=1, source_target_pairs={{0,4},{1,13},{4,8},{5,1},{8,12},{9,5},{12,0},{13,9},{2,6},{3,15},{... | collective-permute-start | bytes 1572872 | tf_op jit(solution)/shard_map/ppermute | solution.py:587
  41.9 0.1 collective-permute-start.9
  42.0 1.0 %shard_map.77 = f32[1,2048]{1,0:T(1,128)S(1)} custom-call(s32[6]{0:T(128)S(1)} %stack.41.par_ref, s32[5,8,2048]{2,1,0:T(8,128)S(1)} %get-tuple-element.87.idx_ref, f32[8,2048]{1,0:T(8,128)S(1)} %get-tuple-element.88.sum_ref, f32[24,2048]{1,0:T(8,128)S(1)} %collective-permute-done.5.beside_ref.refs_2_, ...), custom_call_target="tpu_custom_call" | custom-call | flops 1000 | bytes 1000 | tf_op jit(solution)/shard_map/pallas_call | solution.py:641
  43.1 1.2 %collective-permute-done.7 = f32[1,2048]{1,0:T(1,128)S(1)} collective-permute-done((f32[1,2048]{1,0:T(1,128)S(1)}, f32[1,2048]{1,0:T(1,128)S(1)}, u32[]{:S(2)}, u32[]{:S(2)}) %collective-permute-start.7) | collective-permute-done | bytes 8224 | tf_op jit(solution)/shard_map/ppermute | solution.py:645
  44.3 1.6 %collective-permute-start.8 = (f32[1,2048]{1,0:T(1,128)S(1)}, f32[1,2048]{1,0:T(1,128)S(1)}, u32[]{:S(2)}, u32[]{:S(2)}) collective-permute-start(f32[1,2048]{1,0:T(1,128)S(1)} %add.595), channel_id=1, source_target_pairs={{0,2},{2,0},{1,3},{3,1},{4,6},{6,4},{5,7},{7,5},{8,10},{10,8},{9,1... | collective-permute-start | bytes 24584 | tf_op jit(solution)/shard_map/ppermute | solution.py:647
  45.8 2.2 %collective-permute-done.8 = f32[1,2048]{1,0:T(1,128)S(1)} collective-permute-done((f32[1,2048]{1,0:T(1,128)S(1)}, f32[1,2048]{1,0:T(1,128)S(1)}, u32[]{:S(2)}, u32[]{:S(2)}) %collective-permute-start.8) | collective-permute-done | bytes 8224 | tf_op jit(solution)/shard_map/ppermute | solution.py:647
  48.0 7.1 %shard_map.78 = (f32[288,2048]{1,0:T(8,128)}, f32[4,16,128]{2,1,0:T(8,128)S(1)}) custom-call(s32[6]{0:T(128)S(1)} %stack.41.par_ref, s32[1]{0:T(128)} %bitcast.57.spill_ref, s32[5,8,2048]{2,1,0:T(8,128)S(1)} %get-tuple-element.87.idx_ref, f32[2,2048]{1,0:T(2,128)} %wind_ref.7, f32[1,2048]{1,0:T(1,128)S(1)} %add.596.slope_ref, f32[288,16]{1,0:T(8,128)S(1)} %bitcast.120, ...), custom_call_target="tpu_custom_call" | custom-call | flops 1000 | bytes 1000 | tf_op jit(solution)/shard_map/pallas_call | solution.py:672
  55.1 5.4 %shard_map.79 = (f32[288,2048]{1,0:T(8,128)}, f32[4,16,128]{2,1,0:T(8,128)S(1)}) custom-call(s32[6]{0:T(128)S(1)} %stack.41.par_ref, s32[1]{0:T(128)} %bitcast.57.spill_ref, s32[5,8,2048]{2,1,0:T(8,128)S(1)} %get-tuple-element.87.idx_ref, f32[2,2048]{1,0:T(2,128)S(1)} %copy-done.5, f32[1,2048]{1,0:T(1,128)S(1)} %add.596.slope_ref, ...), custom_call_target="tpu_custom_call", output_to_operand_aliasing={{0}: (10, {})} | custom-call | flops 1000 | bytes 1000 | tf_op jit(solution)/shard_map/pallas_call | solution.py:672
  60.6 1.5 %collective-permute-done.10.refs_0_ = f32[64,2048]{1,0:T(8,128)S(1)} collective-permute-done((f32[64,2048]{1,0:T(8,128)}, f32[64,2048]{1,0:T(8,128)S(1)}, u32[]{:S(2)}, u32[]{:S(2)}) %collective-permute-start.10) | collective-permute-done | bytes 524320 | tf_op jit(solution)/shard_map/ppermute | solution.py:587
  62.0 4.4 %shard_map.80 = (f32[288,2048]{1,0:T(8,128)}, f32[4,16,128]{2,1,0:T(8,128)S(1)}) custom-call(s32[6]{0:T(128)S(1)} %stack.41.par_ref, s32[1]{0:T(128)} %bitcast.57.spill_ref, s32[5,8,2048]{2,1,0:T(8,128)S(1)} %get-tuple-element.87.idx_ref, f32[2,2048]{1,0:T(2,128)S(1)} %copy-done.5, f32[1,2048]{1,0:T(1,128)S(1)} %add.596.slope_ref, ...), custom_call_target="tpu_custom_call", output_to_operand_aliasing={{0}: (10, {})} | custom-call | flops 1000 | bytes 1000 | tf_op jit(solution)/shard_map/pallas_call | solution.py:672
  66.5 0.6 collective-permute-done.9.refs_0_
  67.1 2.9 %shard_map.81 = (f32[288,2048]{1,0:T(8,128)}, f32[2,16,128]{2,1,0:T(8,128)S(1)}, f32[2,16,128]{2,1,0:T(8,128)S(1)}) custom-call(s32[6]{0:T(128)S(1)} %stack.41.par_ref, s32[1]{0:T(128)} %bitcast.57.spill_ref, s32[5,8,2048]{2,1,0:T(8,128)S(1)} %get-tuple-element.87.idx_ref, f32[2,2048]{1,0:T(2,128)S(1)} %copy-done.5, ...), custom_call_target="tpu_custom_call", output_to_operand_aliasing={{0}: (10, {})} | custom-call | flops 1000 | bytes 1000 | tf_op jit(solution)/shard_map/pallas_call | solution.py:672
  70.0 1.2 %collective-permute-done.13 = f32[2,16,128]{2,1,0:T(8,128)S(1)} collective-permute-done((f32[2,16,128]{2,1,0:T(8,128)S(1)}, f32[2,16,128]{2,1,0:T(8,128)S(1)}, u32[]{:S(2)}, u32[]{:S(2)}) %collective-permute-start.13) | collective-permute-done | bytes 16416 | tf_op jit(solution)/shard_map/ppermute | solution.py:687
  71.1 1.5 %collective-permute-start.14 = (f32[2,16,128]{2,1,0:T(8,128)S(1)}, f32[2,16,128]{2,1,0:T(8,128)S(1)}, u32[]{:S(2)}, u32[]{:S(2)}) collective-permute-start(f32[2,16,128]{2,1,0:T(8,128)S(1)} %add.597), channel_id=1, source_target_pairs={{0,2},{2,0},{1,3},{3,1},{4,6},{6,4},{5,7},{7,5},{8,10},{10,8},{9,1... | collective-permute-start | bytes 49160 | tf_op jit(solution)/shard_map/ppermute | solution.py:689
  72.6 2.2 %collective-permute-done.14 = f32[2,16,128]{2,1,0:T(8,128)S(1)} collective-permute-done((f32[2,16,128]{2,1,0:T(8,128)S(1)}, f32[2,16,128]{2,1,0:T(8,128)S(1)}, u32[]{:S(2)}, u32[]{:S(2)}) %collective-permute-start.14) | collective-permute-done | bytes 16416 | tf_op jit(solution)/shard_map/ppermute | solution.py:689
  74.9 4.8 %collective-permute-start.15 = (f32[2,16,128]{2,1,0:T(8,128)S(1)}, f32[2,16,128]{2,1,0:T(8,128)S(1)}, u32[]{:S(2)}, u32[]{:S(2)}) collective-permute-start(f32[2,16,128]{2,1,0:T(8,128)S(1)} %add.598.refs_0_), channel_id=1, source_target_pairs={{0,4},{4,0},{8,12},{12,8},{1,5},{5,1},{9,13},{13,9},{2,6},{6,2},{1... | collective-permute-start | bytes 49160 | tf_op jit(solution)/shard_map/ppermute | solution.py:694
  79.6 1.9 %collective-permute-start.16 = (f32[2,16,128]{2,1,0:T(8,128)S(1)}, f32[2,16,128]{2,1,0:T(8,128)S(1)}, u32[]{:S(2)}, u32[]{:S(2)}) collective-permute-start(f32[2,16,128]{2,1,0:T(8,128)S(1)} %add.598.refs_0_), channel_id=1, source_target_pairs={{0,8},{4,12},{8,0},{12,4},{1,9},{5,13},{9,1},{13,5},{2,10},{6,14},... | collective-permute-start | bytes 49160 | tf_op jit(solution)/shard_map/ppermute | solution.py:694
  81.5 1.4 %collective-permute-start.17 = (f32[2,16,128]{2,1,0:T(8,128)S(1)}, f32[2,16,128]{2,1,0:T(8,128)S(1)}, u32[]{:S(2)}, u32[]{:S(2)}) collective-permute-start(f32[2,16,128]{2,1,0:T(8,128)S(1)} %add.598.refs_0_), channel_id=1, source_target_pairs={{0,12},{4,8},{8,4},{12,0},{1,13},{5,9},{9,5},{13,1},{2,14},{6,10},... | collective-permute-start | bytes 49160 | tf_op jit(solution)/shard_map/ppermute | solution.py:694
  82.9 1.4 %collective-permute-done.16.refs_2_ = f32[2,16,128]{2,1,0:T(8,128)S(1)} collective-permute-done((f32[2,16,128]{2,1,0:T(8,128)S(1)}, f32[2,16,128]{2,1,0:T(8,128)S(1)}, u32[]{:S(2)}, u32[]{:S(2)}) %collective-permute-start.16) | collective-permute-done | bytes 16416 | tf_op jit(solution)/shard_map/ppermute | solution.py:694
  84.3 2.7 %collective-permute-done.17.refs_3_ = f32[2,16,128]{2,1,0:T(8,128)S(1)} collective-permute-done((f32[2,16,128]{2,1,0:T(8,128)S(1)}, f32[2,16,128]{2,1,0:T(8,128)S(1)}, u32[]{:S(2)}, u32[]{:S(2)}) %collective-permute-start.17) | collective-permute-done | bytes 16416 | tf_op jit(solution)/shard_map/ppermute | solution.py:694
  87.0 1.2 %shard_map.82 = (f32[1,1024]{1,0:T(1,128)}, f32[1,1024]{1,0:T(1,128)}) custom-call(s32[1,1024]{1,0:T(1,128)S(1)} %bitcast.125, s32[1,1024]{1,0:T(1,128)S(1)} %bitcast.124, f32[2,16,128]{2,1,0:T(8,128)S(1)} %add.598.refs_0_, f32[2,16,128]{2,1,0:T(8,128)S(1)} %collective-permute-done.15.refs_1_, f32[2,16,128]{2,1,0:T(8,128)S(1)} %collective-permute-done.16.refs_2_, ...), custom_call_target="tpu_custom_call" | custom-call | flops 1000 | bytes 1000 | tf_op jit(solution)/shard_map/pallas_call | solution.py:703
  (54 shorter events, 1.0 us)
Async XLA Ops:
  0.6 54.5 %copy-start.5 = (f32[2,2048]{1,0:T(2,128)S(1)}, f32[2,2048]{1,0:T(2,128)}, u32[]{:S(2)}) copy-start(f32[2,2048]{1,0:T(2,128)} %wind_ref.7) | copy-start | bytes 49156
  2.4 16.2 %collective-permute-start.2 = (f32[48,2048]{1,0:T(8,128)}, f32[48,2048]{1,0:T(8,128)S(1)}, u32[]{:S(2)}, u32[]{:S(2)}) collective-permute-start(f32[48,2048]{1,0:T(8,128)} %bitcast.54), channel_id=1, source_target_pairs={{0,4},{1,13},{4,8},{5,1},{8,12},{9,5},{12,0},{13,9},{2,6},{3,15},{... | collective-permute-start | bytes 1179656 | tf_op jit(solution)/shard_map/ppermute | solution.py:587
  7.2 18.8 %collective-permute-start.11 = (f32[48,2048]{1,0:T(8,128)}, f32[48,2048]{1,0:T(8,128)S(1)}, u32[]{:S(2)}, u32[]{:S(2)}) collective-permute-start(f32[48,2048]{1,0:T(8,128)} %slice.46), channel_id=1, source_target_pairs={{0,4},{1,13},{4,8},{5,1},{8,12},{9,5},{12,0},{13,9},{2,6},{3,15},{... | collective-permute-start | bytes 1179656 | tf_op jit(solution)/shard_map/ppermute | solution.py:587
  17.9 0.8 copy-start
  18.6 17.2 %collective-permute-start.5 = (f32[24,2048]{1,0:T(8,128)}, f32[24,2048]{1,0:T(8,128)S(1)}, u32[]{:S(2)}, u32[]{:S(2)}) collective-permute-start(f32[24,2048]{1,0:T(8,128)} %get-tuple-element.83), channel_id=1, source_target_pairs={{0,4},{1,13},{4,8},{5,1},{8,12},{9,5},{12,0},{13,9},{2,6},{3,15},{... | collective-permute-start | bytes 589832 | tf_op jit(solution)/shard_map/ppermute | solution.py:587
  20.2 15.6 %collective-permute-start.3 = (f32[296,128]{1,0:T(8,128)}, f32[296,128]{1,0:T(8,128)S(1)}, u32[]{:S(2)}, u32[]{:S(2)}) collective-permute-start(f32[296,128]{1,0:T(8,128)} %get-tuple-element.81), channel_id=1, source_target_pairs={{0,8},{1,9},{4,12},{5,13},{8,0},{9,1},{12,4},{13,5},{2,10},{3,11},... | collective-permute-start | bytes 454664 | tf_op jit(solution)/shard_map/ppermute | solution.py:587
  21.5 14.4 %collective-permute-start.4 = (f32[296,128]{1,0:T(8,128)}, f32[296,128]{1,0:T(8,128)S(1)}, u32[]{:S(2)}, u32[]{:S(2)}) collective-permute-start(f32[296,128]{1,0:T(8,128)} %get-tuple-element.82), channel_id=1, source_target_pairs={{0,12},{1,5},{4,0},{5,9},{8,4},{9,13},{12,8},{13,1},{2,14},{3,7},{... | collective-permute-start | bytes 454664 | tf_op jit(solution)/shard_map/ppermute | solution.py:587
  26.0 29.1 %collective-permute-start.12 = (f32[80,2048]{1,0:T(8,128)S(1)}, f32[80,2048]{1,0:T(8,128)S(1)}, u32[]{:S(2)}, u32[]{:S(2)}) collective-permute-start(f32[80,2048]{1,0:T(8,128)S(1)} %get-tuple-element.96), channel_id=1, source_target_pairs={{0,4},{1,13},{4,8},{5,1},{8,12},{9,5},{12,0},{13,9},{2,6},{3,15},{... | collective-permute-start | bytes 1966088 | tf_op jit(solution)/shard_map/ppermute | solution.py:587
  28.0 3.8 %collective-permute-start.6 = (f32[1,1]{1,0:T(1,128)}, f32[1,1]{1,0:T(1,128)}, u32[]{:S(2)}, u32[]{:S(2)}) collective-permute-start(f32[1,1]{1,0:T(1,128)} %bitcast.56), channel_id=1, source_target_pairs={{0,16},{16,0},{1,17},{17,1},{2,18},{18,2},{3,19},{19,3},{4,20},{20... | collective-permute-start | bytes 20 | tf_op jit(solution)/shard_map/ppermute | solution.py:628
  35.9 26.2 %collective-permute-start.10 = (f32[64,2048]{1,0:T(8,128)}, f32[64,2048]{1,0:T(8,128)S(1)}, u32[]{:S(2)}, u32[]{:S(2)}) collective-permute-start(f32[64,2048]{1,0:T(8,128)} %copy-done), channel_id=1, source_target_pairs={{0,4},{1,13},{4,8},{5,1},{8,12},{9,5},{12,0},{13,9},{2,6},{3,15},{... | collective-permute-start | bytes 1572872 | tf_op jit(solution)/shard_map/ppermute | solution.py:587
  41.9 25.2 %collective-permute-start.9 = (f32[32,2048]{1,0:T(8,128)S(1)}, f32[32,2048]{1,0:T(8,128)S(1)}, u32[]{:S(2)}, u32[]{:S(2)}) collective-permute-start(f32[32,2048]{1,0:T(8,128)S(1)} %get-tuple-element.92), channel_id=1, source_target_pairs={{0,4},{1,13},{4,8},{5,1},{8,12},{9,5},{12,0},{13,9},{2,6},{3,15},{... | collective-permute-start | bytes 786440 | tf_op jit(solution)/shard_map/ppermute | solution.py:587
  43.0 1.2 %collective-permute-start.7 = (f32[1,2048]{1,0:T(1,128)S(1)}, f32[1,2048]{1,0:T(1,128)S(1)}, u32[]{:S(2)}, u32[]{:S(2)}) collective-permute-start(f32[1,2048]{1,0:T(1,128)S(1)} %shard_map.77), channel_id=1, source_target_pairs={{0,1},{1,0},{2,3},{3,2},{4,5},{5,4},{6,7},{7,6},{8,9},{9,8},{10,11... | collective-permute-start | bytes 24584 | tf_op jit(solution)/shard_map/ppermute | solution.py:645
  44.3 3.7 %collective-permute-start.8 = (f32[1,2048]{1,0:T(1,128)S(1)}, f32[1,2048]{1,0:T(1,128)S(1)}, u32[]{:S(2)}, u32[]{:S(2)}) collective-permute-start(f32[1,2048]{1,0:T(1,128)S(1)} %add.595), channel_id=1, source_target_pairs={{0,2},{2,0},{1,3},{3,1},{4,6},{6,4},{5,7},{7,5},{8,10},{10,8},{9,1... | collective-permute-start | bytes 24584 | tf_op jit(solution)/shard_map/ppermute | solution.py:647
  55.1 27.8 %copy-start.6 = (s32[1024]{0:T(1024)S(1)}, s32[1024]{0:T(1024)}, u32[]{:S(2)}) copy-start(s32[1024]{0:T(1024)} %param.13) | copy-start | bytes 12292
  55.1 27.8 %copy-start.7 = (s32[1024]{0:T(1024)S(1)}, s32[1024]{0:T(1024)}, u32[]{:S(2)}) copy-start(s32[1024]{0:T(1024)} %param.12) | copy-start | bytes 12292
  55.1 33.2 %copy-start.4 = (s32[128,128]{1,0:T(8,128)S(1)}, s32[128,128]{1,0:T(8,128)}, u32[]{:S(2)}) copy-start(s32[128,128]{1,0:T(8,128)} %cell_ref.1) | copy-start | bytes 196612
  70.0 1.2 %collective-permute-start.13 = (f32[2,16,128]{2,1,0:T(8,128)S(1)}, f32[2,16,128]{2,1,0:T(8,128)S(1)}, u32[]{:S(2)}, u32[]{:S(2)}) collective-permute-start(f32[2,16,128]{2,1,0:T(8,128)S(1)} %get-tuple-element.107), channel_id=1, source_target_pairs={{0,1},{1,0},{2,3},{3,2},{4,5},{5,4},{6,7},{7,6},{8,9},{9,8},{10,11... | collective-permute-start | bytes 49160 | tf_op jit(solution)/shard_map/ppermute | solution.py:687
  71.1 3.7 %collective-permute-start.14 = (f32[2,16,128]{2,1,0:T(8,128)S(1)}, f32[2,16,128]{2,1,0:T(8,128)S(1)}, u32[]{:S(2)}, u32[]{:S(2)}) collective-permute-start(f32[2,16,128]{2,1,0:T(8,128)S(1)} %add.597), channel_id=1, source_target_pairs={{0,2},{2,0},{1,3},{3,1},{4,6},{6,4},{5,7},{7,5},{8,10},{10,8},{9,1... | collective-permute-start | bytes 49160 | tf_op jit(solution)/shard_map/ppermute | solution.py:689
  74.9 8.0 %collective-permute-start.15 = (f32[2,16,128]{2,1,0:T(8,128)S(1)}, f32[2,16,128]{2,1,0:T(8,128)S(1)}, u32[]{:S(2)}, u32[]{:S(2)}) collective-permute-start(f32[2,16,128]{2,1,0:T(8,128)S(1)} %add.598.refs_0_), channel_id=1, source_target_pairs={{0,4},{4,0},{8,12},{12,8},{1,5},{5,1},{9,13},{13,9},{2,6},{6,2},{1... | collective-permute-start | bytes 49160 | tf_op jit(solution)/shard_map/ppermute | solution.py:694
  79.6 4.6 %collective-permute-start.16 = (f32[2,16,128]{2,1,0:T(8,128)S(1)}, f32[2,16,128]{2,1,0:T(8,128)S(1)}, u32[]{:S(2)}, u32[]{:S(2)}) collective-permute-start(f32[2,16,128]{2,1,0:T(8,128)S(1)} %add.598.refs_0_), channel_id=1, source_target_pairs={{0,8},{4,12},{8,0},{12,4},{1,9},{5,13},{9,1},{13,5},{2,10},{6,14},... | collective-permute-start | bytes 49160 | tf_op jit(solution)/shard_map/ppermute | solution.py:694
  81.5 5.5 %collective-permute-start.17 = (f32[2,16,128]{2,1,0:T(8,128)S(1)}, f32[2,16,128]{2,1,0:T(8,128)S(1)}, u32[]{:S(2)}, u32[]{:S(2)}) collective-permute-start(f32[2,16,128]{2,1,0:T(8,128)S(1)} %add.598.refs_0_), channel_id=1, source_target_pairs={{0,12},{4,8},{8,4},{12,0},{1,13},{5,9},{9,5},{13,1},{2,14},{6,10},... | collective-permute-start | bytes 49160 | tf_op jit(solution)/shard_map/ppermute | solution.py:694

commit v6 on v5

--- a/solution.py
+++ b/solution.py
@@ -169,7 +169,6 @@
 C_KEEP, C_ROW, C_COL, C_SLOPE, C_EAST, C_NORTH, C_ONE, C_DAMP = range(8)
 C_S_EAST, C_S_NORTH, C_T_EAST, C_T_NORTH = range(8, 12)
 CHUNK_ENDS = (3, 6, 7, 12, 16)
-FOURTH_EARLY = True
 VMEM_BYTES = 24 * 1024 * 1024
 
 
@@ -329,6 +328,10 @@
     idx_ref[4] = jnp.broadcast_to(has_beside, (8, slots))
 
 
+def copy_kernel(in_ref, out_ref):
+    out_ref[...] = in_ref[...]
+
+
 def lane_take(values, lanes):
     return jnp.take_along_axis(values, lanes, axis=1)
 
@@ -383,7 +386,7 @@
         slope_ref[:, at] = slope + jnp.where(idx_ref[4, 0:1, at] > 0, column[3:4], 0.0)
 
 
-def step_kernel(owners, parts, half_steps, chained, final, par_ref, spill_ref, idx_ref, wind_ref, slope_ref, coef_ref, g_ref, *refs):
+def step_kernel(owners, parts, half_rows, chained, final, par_ref, spill_ref, idx_ref, wind_ref, slope_ref, coef_ref, g_ref, *refs):
     beside_refs, refs = refs[: len(parts)], refs[len(parts) :]
     list_refs, refs = refs[: owners - 2], refs[owners - 2 :]
     if chained:
@@ -394,8 +397,7 @@
     step = pl.program_id(0)
     step_rows = out_ref.shape[0]
     first_step = parts[0][0]
-    half = jnp.where(step + first_step >= half_steps, 1, 0)
-    way, turn = par_ref[1 + half], par_ref[3]
+    turn = par_ref[3]
     lane = lax.broadcasted_iota(I32, shape, 1)
     turned = (lane + turn) & (LANES - 1)
     edge = lane == jnp.where(turn < 0, LANES - 1, jnp.where(turn > 0, 0, -1))
@@ -414,8 +416,10 @@
                 return pl.ds(pl.multiple_of(first, 8), 8)
 
             first = (step + first_step) * step_rows + tile * 8
+            half = jnp.where(first >= half_rows, 1, 0)
+            way = par_ref[1 + half]
             rows = at_row(first)
-            other_rows = at_row(first + (1 - 2 * half) * half_steps * step_rows)
+            other_rows = at_row(first + (1 - 2 * half) * half_rows)
             coef = coef_ref[rows, :]
 
             def factor(at):
@@ -590,9 +594,23 @@
         return values[at[0] * step_rows : at[1] * step_rows]
 
     chunks = chunks_of(steps)
-    first = chunk(field, chunks[0])
+    def cut(values, at):
+        size = (at[1] - at[0]) * step_rows
+        if at[0] * step_rows % size:
+            return chunk(values, at)
+        return pl.pallas_call(
+            copy_kernel,
+            grid=(1,),
+            in_specs=[pl.BlockSpec((size, slots), lambda i: (at[0] * step_rows // size, 0))],
+            out_specs=WHOLE,
+            out_shape=shape_of(size, slots),
+            compiler_params=pltpu.CompilerParams(vmem_limit_bytes=VMEM_BYTES),
+            cost_estimate=SHORT,
+        )(values)
+
+    first = cut(field, chunks[0])
     rest, first = lax.optimization_barrier((field, first))
-    beside = [around(first), around(chunk(rest, chunks[1]))]
+    beside = [around(first), around(cut(rest, chunks[1]))]
 
     first_way = 2 * my_cpl - 1
     turn = jnp.where(
@@ -630,9 +648,8 @@
         longest = lax.pmax(longest, "grp")
     beside.append(around(leaving[0]))
     later = list(leaving[1:])
-    if FOURTH_EARLY:
-        later[0], beside[1] = lax.optimization_barrier((later[0], beside[1]))
-        beside.append(around(later.pop(0)))
+    later[0], beside[1] = lax.optimization_barrier((later[0], beside[1]))
+    beside.append(around(later.pop(0)))
     later, arrived, beside[2], longest, spills = lax.optimization_barrier(
         (later, arrived, beside[2], longest, spills)
     )
@@ -650,10 +667,16 @@
 
     updated = sums = None
     for parts in [chunks[:3]] + [[at] for at in chunks[3:]]:
+        ends = [(first * step_rows, end * step_rows) for first, end in parts]
+        final = ends[-1][1] == rows
+        block_rows = step_rows
+        while all(end % (2 * block_rows) == 0 for part in ends for end in part) and block_rows < 32:
+            block_rows *= 2
+        parts = [(first // block_rows, end // block_rows) for first, end in ends]
         start, stop = parts[0][0], parts[-1][1]
-        chained, final = start > 0, stop == steps
+        chained = start > 0
         in_rows = pl.BlockSpec(
-            (step_rows, slots), functools.partial(lambda first, i: (first + i, 0), start)
+            (block_rows, slots), functools.partial(lambda first, i: (first + i, 0), start)
         )
         near, beside = beside[: len(parts)], beside[len(parts) :]
         inputs = [par, spills, idx, wind_deck, slope, coef, field, *near, *arrived]
@@ -661,7 +684,7 @@
         for first, end in parts:
             within = lambda skipped, most, i: (jnp.clip(i - skipped, 0, most), 0)
             within = functools.partial(within, first - start, end - first - 1)
-            specs.append(pl.BlockSpec((step_rows, slots), within))
+            specs.append(pl.BlockSpec((block_rows, slots), within))
         specs += [WHOLE] * len(arrived)
         aliases = {}
         if chained:
@@ -670,7 +693,7 @@
             specs += [pl.BlockSpec(memory_space=pl.ANY), WHOLE]
         sum_shapes = [(2, blocks, LANES)] * 2 if final else [(4, blocks, LANES)]
         updated, *sums = pl.pallas_call(
-            functools.partial(step_kernel, owners, parts, steps // 2, chained, final),
+            functools.partial(step_kernel, owners, parts, rows // 2, chained, final),
             grid=(stop - start,),
             in_specs=specs,
             out_specs=[in_rows] + [WHOLE] * len(sum_shapes),
@@ -684,11 +707,14 @@
             sums = sums[0]
 
     mine, others = sums
-    mine = mine + lax.ppermute(others, "cpl", [(0, 1), (1, 0)])
     if spec_groups == 2:
-        mine = mine + lax.ppermute(mine, "spec", [(0, 1), (1, 0)])
+        peers = spec_groups * cpl_groups
+        mine = sum(
+            lax.ppermute(values, ("spec", "cpl"), [(i, i ^ turned) for i in range(peers)])
+            for values, turned in ((mine, 2), (others, 3), (others, 1))
+        ) + mine
     else:
-        mine = lax.psum(mine, "spec")
+        mine = lax.psum(mine + lax.ppermute(others, "cpl", [(0, 1), (1, 0)]), "spec")
     if owners == 4:
         tables = [mine] + [
             lax.ppermute(mine, "pts", [(i, i ^ turned) for i in range(owners)])

time: 88.8 us -> 87.1 us (0.981)
  local copies, waits for them, and re-layouts: 5.91 us -> 1.58 us
  Pallas kernels: 29.4 us -> 30.7 us
  starting transfers between devices: 28.4 us -> 29.6 us
    slice x2 -> x0, local copies, waits for them, and re-layouts: 3.55 us -> none  [chunk(): return values[at[0] * step_rows:at[1] * step_rows]]
    pallas_call x4 -> x6, Pallas kernels: 19.8 us -> 21.1 us  [the longest x4 19 us: local(): pl.pallas_call(functools.partial(step_kernel, owners, parts, rows // 2, c...]
    ppermute x8, starting transfers between devices: 15.8 us -> 16.8 us  [around(): return lax.ppermute(values, ('pts', 'cpl'), pairs)]
    ppermute x8, waiting for transfers between devices: 8.39 us -> 9.44 us  [around(): return lax.ppermute(values, ('pts', 'cpl'), pairs)]
    ppermute x2 -> x3, waiting for transfers between devices: 3.43 us -> 2.52 us  [local(): lax.ppermute(values, ('spec', 'cpl'), [(i, i ^ turned) for i in range(pee...]
    ppermute x2 -> x3, starting transfers between devices: 1.49 us -> 2.14 us  [local(): lax.ppermute(values, ('spec', 'cpl'), [(i, i ^ turned) for i in range(pee...]
  transfers between devices with their start and end apart: 16 -> 17, of which waited for: 11 -> 12; matrix products, arithmetic and copies ran while one was open for 6% -> 4% of each run, Pallas kernels for 29% -> 30%
where the time goes in v6:
time: 87.1 us; the launch traced here: 86.4 us
  Pallas kernels  30.7 us (35%)
  starting transfers between devices  29.6 us (34%)
  waiting for transfers between devices  20.2 us (23%)
  between operations  2.76 us (3%)
  local copies, waits for them, and re-layouts  1.58 us (2%)
  other arithmetic  1.58 us (2%)
    pallas_call x4, Pallas kernels, local(): pl.pallas_call(functools.partial(step_kernel, owners, parts, rows // 2, c...  19 us
    ppermute x8, starting transfers between devices, around(): return lax.ppermute(values, ('pts', 'cpl'), pairs)  16.8 us
    ppermute x8, waiting for transfers between devices, around(): return lax.ppermute(values, ('pts', 'cpl'), pairs)  9.44 us
    ppermute x3, starting transfers between devices, local(): lax.ppermute(mine, 'pts', [(i, i ^ turned) for i in range(owners)])  7.48 us
    pallas_call x1, Pallas kernels, local(): call(functools.partial(index_kernel, owners, [start * step_rows for start...  7.36 us
    ppermute x3, waiting for transfers between devices, local(): lax.ppermute(mine, 'pts', [(i, i ^ turned) for i in range(owners)])  4.12 us
    ppermute x3, waiting for transfers between devices, local(): lax.ppermute(values, ('spec', 'cpl'), [(i, i ^ turned) for i in range(pee...  2.52 us
    ppermute x1, waiting for transfers between devices, local(): slope = slope + lax.ppermute(slope, 'spec', [(0, 1), (1, 0)])  2.16 us
  transfers between devices with their start and end apart: 17, of which 12 were waited for; matrix products, arithmetic and copies ran while one was open for 4% of the time, Pallas kernels for 30%

profile of v6, /device:TPU:0, one launch (start us, length us, event | category | flops | bytes accessed | tf_op | source)
XLA Modules:
  0.0 86.4 jit_solution(4203152735746066378)
XLA Ops:
  0.6 1.0 %shard_map.77 = f32[48,2048]{1,0:T(8,128)S(1)} custom-call(f32[288,2048]{1,0:T(8,128)} %bitcast.52.g_ref.in_ref), custom_call_target="tpu_custom_call" | custom-call | flops 1000 | bytes 1000 | tf_op jit(solution)/shard_map/pallas_call | solution.py:601
  1.7 3.1 %collective-permute-start.2 = (f32[48,2048]{1,0:T(8,128)S(1)}, f32[48,2048]{1,0:T(8,128)S(1)}, u32[]{:S(2)}, u32[]{:S(2)}) collective-permute-start(f32[48,2048]{1,0:T(8,128)S(1)} %shard_map.77), channel_id=1, source_target_pairs={{0,4},{1,13},{4,8},{5,1},{8,12},{9,5},{12,0},{13,9},{2,6},{3,15},{... | collective-permute-start | bytes 1179656 | tf_op jit(solution)/shard_map/ppermute | solution.py:591
  4.7 1.0 %shard_map.79 = f32[48,2048]{1,0:T(8,128)S(1)} custom-call(f32[288,2048]{1,0:T(8,128)} %bitcast.52.g_ref.in_ref), custom_call_target="tpu_custom_call" | custom-call | flops 1000 | bytes 1000 | tf_op jit(solution)/shard_map/pallas_call | solution.py:601
  5.8 1.6 %collective-permute-start.11 = (f32[48,2048]{1,0:T(8,128)S(1)}, f32[48,2048]{1,0:T(8,128)S(1)}, u32[]{:S(2)}, u32[]{:S(2)}) collective-permute-start(f32[48,2048]{1,0:T(8,128)S(1)} %shard_map.79), channel_id=1, source_target_pairs={{0,4},{1,13},{4,8},{5,1},{8,12},{9,5},{12,0},{13,9},{2,6},{3,15},{... | collective-permute-start | bytes 1179656 | tf_op jit(solution)/shard_map/ppermute | solution.py:591
  7.6 0.1 mul.605
  7.8 0.1 mul.608
  8.1 0.1 mul.615
  8.4 0.1 stack_broadcast_in_dim.51
  8.6 0.1 stack_broadcast_in_dim.53
  8.8 0.1 copy.44
  9.0 0.1 stack.41.par_ref
  9.1 7.4 %shard_map.76 = (s32[5,8,2048]{2,1,0:T(8,128)S(1)}, f32[16,128]{1,0:T(8,128)S(1)}, f32[8,2048]{1,0:T(8,128)S(1)}, f32[296,128]{1,0:T(8,128)}, f32[296,128]{1,0:T...) custom-call(s32[6]{0:T(128)S(1)} %stack.41.par_ref, ...), custom_call_target="tpu_custom_call" | custom-call | flops 1000 | bytes 1000 | tf_op jit(solution)/shard_map/pallas_call | solution.py:624
  16.5 0.2 collective-permute-done.2.refs_0_
  16.7 1.3 %collective-permute-start.5 = (f32[24,2048]{1,0:T(8,128)}, f32[24,2048]{1,0:T(8,128)S(1)}, u32[]{:S(2)}, u32[]{:S(2)}) collective-permute-start(f32[24,2048]{1,0:T(8,128)} %get-tuple-element.83), channel_id=1, source_target_pairs={{0,4},{1,13},{4,8},{5,1},{8,12},{9,5},{12,0},{13,9},{2,6},{3,15},{... | collective-permute-start | bytes 589832 | tf_op jit(solution)/shard_map/ppermute | solution.py:591
  18.0 1.2 %collective-permute-start.3 = (f32[296,128]{1,0:T(8,128)}, f32[296,128]{1,0:T(8,128)S(1)}, u32[]{:S(2)}, u32[]{:S(2)}) collective-permute-start(f32[296,128]{1,0:T(8,128)} %get-tuple-element.81), channel_id=1, source_target_pairs={{0,8},{1,9},{4,12},{5,13},{8,0},{9,1},{12,4},{13,5},{2,10},{3,11},... | collective-permute-start | bytes 454664 | tf_op jit(solution)/shard_map/ppermute | solution.py:591
  19.3 1.3 %collective-permute-start.4 = (f32[296,128]{1,0:T(8,128)}, f32[296,128]{1,0:T(8,128)S(1)}, u32[]{:S(2)}, u32[]{:S(2)}) collective-permute-start(f32[296,128]{1,0:T(8,128)} %get-tuple-element.82), channel_id=1, source_target_pairs={{0,12},{1,5},{4,0},{5,9},{8,4},{9,13},{12,8},{13,1},{2,14},{3,7},{... | collective-permute-start | bytes 454664 | tf_op jit(solution)/shard_map/ppermute | solution.py:591
  20.5 4.6 %collective-permute-done.11.refs_1_ = f32[48,2048]{1,0:T(8,128)S(1)} collective-permute-done((f32[48,2048]{1,0:T(8,128)S(1)}, f32[48,2048]{1,0:T(8,128)S(1)}, u32[]{:S(2)}, u32[]{:S(2)}) %collective-permute-start.11) | collective-permute-done | bytes 393248 | tf_op jit(solution)/shard_map/ppermute | solution.py:591
  25.1 1.1 %collective-permute-start.12 = (f32[80,2048]{1,0:T(8,128)S(1)}, f32[80,2048]{1,0:T(8,128)S(1)}, u32[]{:S(2)}, u32[]{:S(2)}) collective-permute-start(f32[80,2048]{1,0:T(8,128)S(1)} %get-tuple-element.96), channel_id=1, source_target_pairs={{0,4},{1,13},{4,8},{5,1},{8,12},{9,5},{12,0},{13,9},{2,6},{3,15},{... | collective-permute-start | bytes 1966088 | tf_op jit(solution)/shard_map/ppermute | solution.py:591
  26.2 0.1 reduce_sum.85
  26.4 0.1 reshape.1210
  26.4 0.1 copy.40
  26.5 0.6 fusion.52
  27.1 1.5 %collective-permute-start.6 = (f32[1,1]{1,0:T(1,128)}, f32[1,1]{1,0:T(1,128)}, u32[]{:S(2)}, u32[]{:S(2)}) collective-permute-start(f32[1,1]{1,0:T(1,128)} %bitcast.55), channel_id=1, source_target_pairs={{0,16},{16,0},{1,17},{17,1},{2,18},{18,2},{3,19},{19,3},{4,20},{20... | collective-permute-start | bytes 20 | tf_op jit(solution)/shard_map/ppermute | solution.py:646
  28.7 0.6 reduce_max.19
  29.9 0.8 collective-permute-done.6
  32.0 1.8 %collective-permute-done.3.refs_0_.refs_3_.refs_1_ = f32[296,128]{1,0:T(8,128)S(1)} collective-permute-done((f32[296,128]{1,0:T(8,128)}, f32[296,128]{1,0:T(8,128)S(1)}, u32[]{:S(2)}, u32[]{:S(2)}) %collective-permute-start.3) | collective-permute-done | bytes 151584 | tf_op jit(solution)/shard_map/ppermute | solution.py:591
  33.9 6.9 %collective-permute-start.10 = (f32[64,2048]{1,0:T(8,128)}, f32[64,2048]{1,0:T(8,128)S(1)}, u32[]{:S(2)}, u32[]{:S(2)}) collective-permute-start(f32[64,2048]{1,0:T(8,128)} %copy-done), channel_id=1, source_target_pairs={{0,4},{1,13},{4,8},{5,1},{8,12},{9,5},{12,0},{13,9},{2,6},{3,15},{... | collective-permute-start | bytes 1572872 | tf_op jit(solution)/shard_map/ppermute | solution.py:591
  40.8 0.3 collective-permute-start.9
  41.1 1.0 %shard_map.78 = f32[1,2048]{1,0:T(1,128)S(1)} custom-call(s32[6]{0:T(128)S(1)} %stack.41.par_ref, s32[5,8,2048]{2,1,0:T(8,128)S(1)} %get-tuple-element.87.idx_ref, f32[8,2048]{1,0:T(8,128)S(1)} %get-tuple-element.88.sum_ref, f32[24,2048]{1,0:T(8,128)S(1)} %collective-permute-done.5.beside_ref.refs_2_, ...), custom_call_target="tpu_custom_call" | custom-call | flops 1000 | bytes 1000 | tf_op jit(solution)/shard_map/pallas_call | solution.py:658
  42.2 1.2 %collective-permute-done.7 = f32[1,2048]{1,0:T(1,128)S(1)} collective-permute-done((f32[1,2048]{1,0:T(1,128)S(1)}, f32[1,2048]{1,0:T(1,128)S(1)}, u32[]{:S(2)}, u32[]{:S(2)}) %collective-permute-start.7) | collective-permute-done | bytes 8224 | tf_op jit(solution)/shard_map/ppermute | solution.py:662
  43.4 1.6 %collective-permute-start.8 = (f32[1,2048]{1,0:T(1,128)S(1)}, f32[1,2048]{1,0:T(1,128)S(1)}, u32[]{:S(2)}, u32[]{:S(2)}) collective-permute-start(f32[1,2048]{1,0:T(1,128)S(1)} %add.598), channel_id=1, source_target_pairs={{0,2},{2,0},{1,3},{3,1},{4,6},{6,4},{5,7},{7,5},{8,10},{10,8},{9,1... | collective-permute-start | bytes 24584 | tf_op jit(solution)/shard_map/ppermute | solution.py:664
  44.9 2.2 %collective-permute-done.8 = f32[1,2048]{1,0:T(1,128)S(1)} collective-permute-done((f32[1,2048]{1,0:T(1,128)S(1)}, f32[1,2048]{1,0:T(1,128)S(1)}, u32[]{:S(2)}, u32[]{:S(2)}) %collective-permute-start.8) | collective-permute-done | bytes 8224 | tf_op jit(solution)/shard_map/ppermute | solution.py:664
  47.1 7.0 %shard_map.80 = (f32[288,2048]{1,0:T(8,128)}, f32[4,16,128]{2,1,0:T(8,128)S(1)}) custom-call(s32[6]{0:T(128)S(1)} %stack.41.par_ref, s32[1]{0:T(128)} %bitcast.56.spill_ref, s32[5,8,2048]{2,1,0:T(8,128)S(1)} %get-tuple-element.87.idx_ref, f32[2,2048]{1,0:T(2,128)S(1)} %copy-done.5, f32[1,2048]{1,0:T(1,128)S(1)} %add.599.slope_ref, f32[288,16]{1,0:T(8,128)S(1)} %bitcast.119, ...), custom_call_target="tpu_custom_call" | custom-call | flops 1000 | bytes 1000 | tf_op jit(solution)/shard_map/pallas_call | solution.py:695
  54.2 5.4 %shard_map.81 = (f32[288,2048]{1,0:T(8,128)}, f32[4,16,128]{2,1,0:T(8,128)S(1)}) custom-call(s32[6]{0:T(128)S(1)} %stack.41.par_ref, s32[1]{0:T(128)} %bitcast.56.spill_ref, s32[5,8,2048]{2,1,0:T(8,128)S(1)} %get-tuple-element.87.idx_ref, f32[2,2048]{1,0:T(2,128)S(1)} %copy-done.5, f32[1,2048]{1,0:T(1,128)S(1)} %add.599.slope_ref, ...), custom_call_target="tpu_custom_call", output_to_operand_aliasing={{0}: (10, {})} | custom-call | flops 1000 | bytes 1000 | tf_op jit(solution)/shard_map/pallas_call | solution.py:695
  59.6 1.6 %collective-permute-done.10.refs_0_ = f32[64,2048]{1,0:T(8,128)S(1)} collective-permute-done((f32[64,2048]{1,0:T(8,128)}, f32[64,2048]{1,0:T(8,128)S(1)}, u32[]{:S(2)}, u32[]{:S(2)}) %collective-permute-start.10) | collective-permute-done | bytes 524320 | tf_op jit(solution)/shard_map/ppermute | solution.py:591
  61.1 3.9 %shard_map.82 = (f32[288,2048]{1,0:T(8,128)}, f32[4,16,128]{2,1,0:T(8,128)S(1)}) custom-call(s32[6]{0:T(128)S(1)} %stack.41.par_ref, s32[1]{0:T(128)} %bitcast.56.spill_ref, s32[5,8,2048]{2,1,0:T(8,128)S(1)} %get-tuple-element.87.idx_ref, f32[2,2048]{1,0:T(2,128)S(1)} %copy-done.5, f32[1,2048]{1,0:T(1,128)S(1)} %add.599.slope_ref, ...), custom_call_target="tpu_custom_call", output_to_operand_aliasing={{0}: (10, {})} | custom-call | flops 1000 | bytes 1000 | tf_op jit(solution)/shard_map/pallas_call | solution.py:695
  65.0 1.2 %collective-permute-done.9.refs_0_ = f32[32,2048]{1,0:T(8,128)S(1)} collective-permute-done((f32[32,2048]{1,0:T(8,128)S(1)}, f32[32,2048]{1,0:T(8,128)S(1)}, u32[]{:S(2)}, u32[]{:S(2)}) %collective-permute-start.9) | collective-permute-done | bytes 262176 | tf_op jit(solution)/shard_map/ppermute | solution.py:591
  66.2 2.7 %shard_map.83 = (f32[288,2048]{1,0:T(8,128)}, f32[2,16,128]{2,1,0:T(8,128)S(1)}, f32[2,16,128]{2,1,0:T(8,128)S(1)}) custom-call(s32[6]{0:T(128)S(1)} %stack.41.par_ref, s32[1]{0:T(128)} %bitcast.56.spill_ref, s32[5,8,2048]{2,1,0:T(8,128)S(1)} %get-tuple-element.87.idx_ref, f32[2,2048]{1,0:T(2,128)S(1)} %copy-done.5, ...), custom_call_target="tpu_custom_call", output_to_operand_aliasing={{0}: (10, {})} | custom-call | flops 1000 | bytes 1000 | tf_op jit(solution)/shard_map/pallas_call | solution.py:695
  68.9 1.5 %collective-permute-start.13 = (f32[2,16,128]{2,1,0:T(8,128)S(1)}, f32[2,16,128]{2,1,0:T(8,128)S(1)}, u32[]{:S(2)}, u32[]{:S(2)}) collective-permute-start(f32[2,16,128]{2,1,0:T(8,128)S(1)} %get-tuple-element.106), channel_id=1, source_target_pairs={{0,2},{1,3},{2,0},{3,1},{4,6},{5,7},{6,4},{7,5},{8,10},{9,11},{10,... | collective-permute-start | bytes 49160 | tf_op jit(solution)/shard_map/ppermute | solution.py:713
  70.4 0.6 collective-permute-start.15
  71.0 1.6 %collective-permute-done.13 = f32[2,16,128]{2,1,0:T(8,128)S(1)} collective-permute-done((f32[2,16,128]{2,1,0:T(8,128)S(1)}, f32[2,16,128]{2,1,0:T(8,128)S(1)}, u32[]{:S(2)}, u32[]{:S(2)}) %collective-permute-start.13) | collective-permute-done | bytes 16416 | tf_op jit(solution)/shard_map/ppermute | solution.py:713
  72.6 0.9 %collective-permute-done.14 = f32[2,16,128]{2,1,0:T(8,128)S(1)} collective-permute-done((f32[2,16,128]{2,1,0:T(8,128)S(1)}, f32[2,16,128]{2,1,0:T(8,128)S(1)}, u32[]{:S(2)}, u32[]{:S(2)}) %collective-permute-start.14) | collective-permute-done | bytes 16416 | tf_op jit(solution)/shard_map/ppermute | solution.py:713
  73.6 4.2 %collective-permute-start.16 = (f32[2,16,128]{2,1,0:T(8,128)S(1)}, f32[2,16,128]{2,1,0:T(8,128)S(1)}, u32[]{:S(2)}, u32[]{:S(2)}) collective-permute-start(f32[2,16,128]{2,1,0:T(8,128)S(1)} %add_add_fusion.refs_0_), channel_id=1, source_target_pairs={{0,4},{4,0},{8,12},{12,8},{1,5},{5,1},{9,13},{13,9},{2,6},{6,2},{1... | collective-permute-start | bytes 49160 | tf_op jit(solution)/shard_map/ppermute | solution.py:720
  77.8 1.9 %collective-permute-start.17 = (f32[2,16,128]{2,1,0:T(8,128)S(1)}, f32[2,16,128]{2,1,0:T(8,128)S(1)}, u32[]{:S(2)}, u32[]{:S(2)}) collective-permute-start(f32[2,16,128]{2,1,0:T(8,128)S(1)} %add_add_fusion.refs_0_), channel_id=1, source_target_pairs={{0,8},{4,12},{8,0},{12,4},{1,9},{5,13},{9,1},{13,5},{2,10},{6,14},... | collective-permute-start | bytes 49160 | tf_op jit(solution)/shard_map/ppermute | solution.py:720
  79.7 1.4 %collective-permute-start.18 = (f32[2,16,128]{2,1,0:T(8,128)S(1)}, f32[2,16,128]{2,1,0:T(8,128)S(1)}, u32[]{:S(2)}, u32[]{:S(2)}) collective-permute-start(f32[2,16,128]{2,1,0:T(8,128)S(1)} %add_add_fusion.refs_0_), channel_id=1, source_target_pairs={{0,12},{4,8},{8,4},{12,0},{1,13},{5,9},{9,5},{13,1},{2,14},{6,10},... | collective-permute-start | bytes 49160 | tf_op jit(solution)/shard_map/ppermute | solution.py:720
  81.1 1.5 %collective-permute-done.17.refs_2_ = f32[2,16,128]{2,1,0:T(8,128)S(1)} collective-permute-done((f32[2,16,128]{2,1,0:T(8,128)S(1)}, f32[2,16,128]{2,1,0:T(8,128)S(1)}, u32[]{:S(2)}, u32[]{:S(2)}) %collective-permute-start.17) | collective-permute-done | bytes 16416 | tf_op jit(solution)/shard_map/ppermute | solution.py:720
  82.6 2.6 %collective-permute-done.18.refs_3_ = f32[2,16,128]{2,1,0:T(8,128)S(1)} collective-permute-done((f32[2,16,128]{2,1,0:T(8,128)S(1)}, f32[2,16,128]{2,1,0:T(8,128)S(1)}, u32[]{:S(2)}, u32[]{:S(2)}) %collective-permute-start.18) | collective-permute-done | bytes 16416 | tf_op jit(solution)/shard_map/ppermute | solution.py:720
  85.2 1.2 %shard_map.84 = (f32[1,1024]{1,0:T(1,128)}, f32[1,1024]{1,0:T(1,128)}) custom-call(s32[1,1024]{1,0:T(1,128)S(1)} %bitcast.124, s32[1,1024]{1,0:T(1,128)S(1)} %bitcast.123, f32[2,16,128]{2,1,0:T(8,128)S(1)} %add_add_fusion.refs_0_, f32[2,16,128]{2,1,0:T(8,128)S(1)} %collective-permute-done.16.refs_1_, f32[2,16,128]{2,1,0:T(8,128)S(1)} %collective-permute-done.17.refs_2_, ...), custom_call_target="tpu_custom_call" | custom-call | flops 1000 | bytes 1000 | tf_op jit(solution)/shard_map/pallas_call | solution.py:729
  (55 shorter events, 1.1 us)
Async XLA Ops:
  0.6 46.5 %copy-start.5 = (f32[2,2048]{1,0:T(2,128)S(1)}, f32[2,2048]{1,0:T(2,128)}, u32[]{:S(2)}) copy-start(f32[2,2048]{1,0:T(2,128)} %wind_ref.7) | copy-start | bytes 49156
  1.7 15.0 %collective-permute-start.2 = (f32[48,2048]{1,0:T(8,128)S(1)}, f32[48,2048]{1,0:T(8,128)S(1)}, u32[]{:S(2)}, u32[]{:S(2)}) collective-permute-start(f32[48,2048]{1,0:T(8,128)S(1)} %shard_map.77), channel_id=1, source_target_pairs={{0,4},{1,13},{4,8},{5,1},{8,12},{9,5},{12,0},{13,9},{2,6},{3,15},{... | collective-permute-start | bytes 1179656 | tf_op jit(solution)/shard_map/ppermute | solution.py:591
  5.8 19.4 %collective-permute-start.11 = (f32[48,2048]{1,0:T(8,128)S(1)}, f32[48,2048]{1,0:T(8,128)S(1)}, u32[]{:S(2)}, u32[]{:S(2)}) collective-permute-start(f32[48,2048]{1,0:T(8,128)S(1)} %shard_map.79), channel_id=1, source_target_pairs={{0,4},{1,13},{4,8},{5,1},{8,12},{9,5},{12,0},{13,9},{2,6},{3,15},{... | collective-permute-start | bytes 1179656 | tf_op jit(solution)/shard_map/ppermute | solution.py:591
  16.5 8.7 %copy-start = (f32[64,2048]{1,0:T(8,128)}, f32[64,2048]{1,0:T(8,128)S(1)}, u32[]{:S(2)}) copy-start(f32[64,2048]{1,0:T(8,128)S(1)} %get-tuple-element.93) | copy-start | bytes 1572868
  16.7 17.2 %collective-permute-start.5 = (f32[24,2048]{1,0:T(8,128)}, f32[24,2048]{1,0:T(8,128)S(1)}, u32[]{:S(2)}, u32[]{:S(2)}) collective-permute-start(f32[24,2048]{1,0:T(8,128)} %get-tuple-element.83), channel_id=1, source_target_pairs={{0,4},{1,13},{4,8},{5,1},{8,12},{9,5},{12,0},{13,9},{2,6},{3,15},{... | collective-permute-start | bytes 589832 | tf_op jit(solution)/shard_map/ppermute | solution.py:591
  18.0 15.9 %collective-permute-start.3 = (f32[296,128]{1,0:T(8,128)}, f32[296,128]{1,0:T(8,128)S(1)}, u32[]{:S(2)}, u32[]{:S(2)}) collective-permute-start(f32[296,128]{1,0:T(8,128)} %get-tuple-element.81), channel_id=1, source_target_pairs={{0,8},{1,9},{4,12},{5,13},{8,0},{9,1},{12,4},{13,5},{2,10},{3,11},... | collective-permute-start | bytes 454664 | tf_op jit(solution)/shard_map/ppermute | solution.py:591
  19.3 14.6 %collective-permute-start.4 = (f32[296,128]{1,0:T(8,128)}, f32[296,128]{1,0:T(8,128)S(1)}, u32[]{:S(2)}, u32[]{:S(2)}) collective-permute-start(f32[296,128]{1,0:T(8,128)} %get-tuple-element.82), channel_id=1, source_target_pairs={{0,12},{1,5},{4,0},{5,9},{8,4},{9,13},{12,8},{13,1},{2,14},{3,7},{... | collective-permute-start | bytes 454664 | tf_op jit(solution)/shard_map/ppermute | solution.py:591
  25.1 29.0 %collective-permute-start.12 = (f32[80,2048]{1,0:T(8,128)S(1)}, f32[80,2048]{1,0:T(8,128)S(1)}, u32[]{:S(2)}, u32[]{:S(2)}) collective-permute-start(f32[80,2048]{1,0:T(8,128)S(1)} %get-tuple-element.96), channel_id=1, source_target_pairs={{0,4},{1,13},{4,8},{5,1},{8,12},{9,5},{12,0},{13,9},{2,6},{3,15},{... | collective-permute-start | bytes 1966088 | tf_op jit(solution)/shard_map/ppermute | solution.py:591
  27.1 3.6 %collective-permute-start.6 = (f32[1,1]{1,0:T(1,128)}, f32[1,1]{1,0:T(1,128)}, u32[]{:S(2)}, u32[]{:S(2)}) collective-permute-start(f32[1,1]{1,0:T(1,128)} %bitcast.55), channel_id=1, source_target_pairs={{0,16},{16,0},{1,17},{17,1},{2,18},{18,2},{3,19},{19,3},{4,20},{20... | collective-permute-start | bytes 20 | tf_op jit(solution)/shard_map/ppermute | solution.py:646
  33.9 27.2 %collective-permute-start.10 = (f32[64,2048]{1,0:T(8,128)}, f32[64,2048]{1,0:T(8,128)S(1)}, u32[]{:S(2)}, u32[]{:S(2)}) collective-permute-start(f32[64,2048]{1,0:T(8,128)} %copy-done), channel_id=1, source_target_pairs={{0,4},{1,13},{4,8},{5,1},{8,12},{9,5},{12,0},{13,9},{2,6},{3,15},{... | collective-permute-start | bytes 1572872 | tf_op jit(solution)/shard_map/ppermute | solution.py:591
  40.8 25.4 %collective-permute-start.9 = (f32[32,2048]{1,0:T(8,128)S(1)}, f32[32,2048]{1,0:T(8,128)S(1)}, u32[]{:S(2)}, u32[]{:S(2)}) collective-permute-start(f32[32,2048]{1,0:T(8,128)S(1)} %get-tuple-element.92), channel_id=1, source_target_pairs={{0,4},{1,13},{4,8},{5,1},{8,12},{9,5},{12,0},{13,9},{2,6},{3,15},{... | collective-permute-start | bytes 786440 | tf_op jit(solution)/shard_map/ppermute | solution.py:591
  42.1 1.2 %collective-permute-start.7 = (f32[1,2048]{1,0:T(1,128)S(1)}, f32[1,2048]{1,0:T(1,128)S(1)}, u32[]{:S(2)}, u32[]{:S(2)}) collective-permute-start(f32[1,2048]{1,0:T(1,128)S(1)} %shard_map.78), channel_id=1, source_target_pairs={{0,1},{1,0},{2,3},{3,2},{4,5},{5,4},{6,7},{7,6},{8,9},{9,8},{10,11... | collective-permute-start | bytes 24584 | tf_op jit(solution)/shard_map/ppermute | solution.py:662
  43.4 3.7 %collective-permute-start.8 = (f32[1,2048]{1,0:T(1,128)S(1)}, f32[1,2048]{1,0:T(1,128)S(1)}, u32[]{:S(2)}, u32[]{:S(2)}) collective-permute-start(f32[1,2048]{1,0:T(1,128)S(1)} %add.598), channel_id=1, source_target_pairs={{0,2},{2,0},{1,3},{3,1},{4,6},{6,4},{5,7},{7,5},{8,10},{10,8},{9,1... | collective-permute-start | bytes 24584 | tf_op jit(solution)/shard_map/ppermute | solution.py:664
  54.2 26.9 %copy-start.6 = (s32[1024]{0:T(1024)S(1)}, s32[1024]{0:T(1024)}, u32[]{:S(2)}) copy-start(s32[1024]{0:T(1024)} %param.13) | copy-start | bytes 12292
  54.2 26.9 %copy-start.7 = (s32[1024]{0:T(1024)S(1)}, s32[1024]{0:T(1024)}, u32[]{:S(2)}) copy-start(s32[1024]{0:T(1024)} %param.12) | copy-start | bytes 12292
  54.2 32.3 %copy-start.4 = (s32[128,128]{1,0:T(8,128)S(1)}, s32[128,128]{1,0:T(8,128)}, u32[]{:S(2)}) copy-start(s32[128,128]{1,0:T(8,128)} %cell_ref.1) | copy-start | bytes 196612
  68.9 3.7 %collective-permute-start.13 = (f32[2,16,128]{2,1,0:T(8,128)S(1)}, f32[2,16,128]{2,1,0:T(8,128)S(1)}, u32[]{:S(2)}, u32[]{:S(2)}) collective-permute-start(f32[2,16,128]{2,1,0:T(8,128)S(1)} %get-tuple-element.106), channel_id=1, source_target_pairs={{0,2},{1,3},{2,0},{3,1},{4,6},{5,7},{6,4},{7,5},{8,10},{9,11},{10,... | collective-permute-start | bytes 49160 | tf_op jit(solution)/shard_map/ppermute | solution.py:713
  70.4 3.2 %collective-permute-start.14 = (f32[2,16,128]{2,1,0:T(8,128)S(1)}, f32[2,16,128]{2,1,0:T(8,128)S(1)}, u32[]{:S(2)}, u32[]{:S(2)}) collective-permute-start(f32[2,16,128]{2,1,0:T(8,128)S(1)} %get-tuple-element.107), channel_id=1, source_target_pairs={{0,3},{1,2},{2,1},{3,0},{4,7},{5,6},{6,5},{7,4},{8,11},{9,10},{10,... | collective-permute-start | bytes 49160 | tf_op jit(solution)/shard_map/ppermute | solution.py:713
  70.4 3.2 %collective-permute-start.15 = (f32[2,16,128]{2,1,0:T(8,128)S(1)}, f32[2,16,128]{2,1,0:T(8,128)S(1)}, u32[]{:S(2)}, u32[]{:S(2)}) collective-permute-start(f32[2,16,128]{2,1,0:T(8,128)S(1)} %get-tuple-element.107), channel_id=1, source_target_pairs={{0,1},{1,0},{2,3},{3,2},{4,5},{5,4},{6,7},{7,6},{8,9},{9,8},{10,11... | collective-permute-start | bytes 49160 | tf_op jit(solution)/shard_map/ppermute | solution.py:713
  73.6 7.5 %collective-permute-start.16 = (f32[2,16,128]{2,1,0:T(8,128)S(1)}, f32[2,16,128]{2,1,0:T(8,128)S(1)}, u32[]{:S(2)}, u32[]{:S(2)}) collective-permute-start(f32[2,16,128]{2,1,0:T(8,128)S(1)} %add_add_fusion.refs_0_), channel_id=1, source_target_pairs={{0,4},{4,0},{8,12},{12,8},{1,5},{5,1},{9,13},{13,9},{2,6},{6,2},{1... | collective-permute-start | bytes 49160 | tf_op jit(solution)/shard_map/ppermute | solution.py:720
  77.8 4.8 %collective-permute-start.17 = (f32[2,16,128]{2,1,0:T(8,128)S(1)}, f32[2,16,128]{2,1,0:T(8,128)S(1)}, u32[]{:S(2)}, u32[]{:S(2)}) collective-permute-start(f32[2,16,128]{2,1,0:T(8,128)S(1)} %add_add_fusion.refs_0_), channel_id=1, source_target_pairs={{0,8},{4,12},{8,0},{12,4},{1,9},{5,13},{9,1},{13,5},{2,10},{6,14},... | collective-permute-start | bytes 49160 | tf_op jit(solution)/shard_map/ppermute | solution.py:720
  79.7 5.5 %collective-permute-start.18 = (f32[2,16,128]{2,1,0:T(8,128)S(1)}, f32[2,16,128]{2,1,0:T(8,128)S(1)}, u32[]{:S(2)}, u32[]{:S(2)}) collective-permute-start(f32[2,16,128]{2,1,0:T(8,128)S(1)} %add_add_fusion.refs_0_), channel_id=1, source_target_pairs={{0,12},{4,8},{8,4},{12,0},{1,13},{5,9},{9,5},{13,1},{2,14},{6,10},... | collective-permute-start | bytes 49160 | tf_op jit(solution)/shard_map/ppermute | solution.py:720
